TPU v7x, 32 devices: a whole 2x2x4 slice. The times are simulated.
32 devices in a mesh: stream: 8 (over z, y), cross: 4 (over x, core).
Axes of the slice: x: 2, y: 2, z: 4, core: 2. Of those that a mesh axis runs over, the one named last changes fastest.
Arguments:
- forcing: bfloat16 [24, 8, 144, 384], P('stream', 'cross'), may hold values from -1.1953125 to 1.1953125
- deformation_velocity: bfloat16 [24, 8, 144, 384], P('stream', 'cross'), may hold values from -6 to 6
- face_mask: int32 [4, 24, 8, 144], P(None, 'stream', 'cross'), may hold values 0 or 1
- lifting: bfloat16 [4, 384, 384], replicated, may hold values from -0.0625 to 0.0625
- inverse: bfloat16 [24, 8, 384, 384], P('stream', 'cross'), may hold values from -1 to 1
- retention: float32 [24, 384], P('stream'), may hold values from 0 to 1
Outputs:
- stress: float32 [24, 8, 144, 384], P('stream', 'cross')
All inputs are finite; a program needn't handle non-finite values. No bound on the sum of `face_mask` on one device may be relied on, other than what follows from the above.
Results may differ from a plain program's by a relative error of at most 0.0039.
Values may be sent and summed in bfloat16 or wider, within the bound.
No kernel may reach another device: no remote copies, remote signals or barrier semaphores. Data moves between devices by JAX's collectives and lax.ppermute only.
A program may use at most 128 MiB of HBM per device.

v0:
```python
import jax
import jax.numpy as jnp
from jax import lax
from jax.sharding import PartitionSpec as P


def extended(cells, sides, width):
    for axis, dim in sides:
        count = lax.axis_size(axis)
        ends = count - 1
        head = lax.slice_in_dim(cells, 0, width, axis=dim)
        tail = lax.slice_in_dim(cells, cells.shape[dim] - width, cells.shape[dim], axis=dim)
        cells = jnp.concatenate(
            [
                lax.ppermute(tail, axis, [(i, (i + 1) % count) for i in range(ends)]),
                cells,
                lax.ppermute(head, axis, [((i + 1) % count, i) for i in range(ends)]),
            ],
            axis=dim,
        )
    return cells


def prefix(array, axis, combine, identity):
    devices, position = (lax.axis_size(axis), lax.axis_index(axis))
    everything = jax.tree.map(lambda part: lax.all_gather(part, axis), array)
    start = jax.tree.map(
        lambda part, zero: jnp.broadcast_to(jnp.asarray(zero, part.dtype), part.shape),
        array,
        identity,
    )

    def lap(k, before):
        reached = k < position
        new = combine(before, jax.tree.map(lambda part: part[k], everything))
        return jax.tree.map(lambda a, b: jnp.where(reached, a, b), new, before)

    return lax.fori_loop(0, devices, lap, start)


def chain_link(earlier, later):
    return (earlier[0] * later[0], later[0] * earlier[1] + later[1])


def sweep_terms(padded, forcing_part, mask_part, lifting, inverse, retention):
    layers_here = forcing_part.shape[0]
    center = padded[:, 1:-1, 1:-1].astype(jnp.float32)
    neighbours = (
        padded[:, :-2, 1:-1],
        padded[:, 2:, 1:-1],
        padded[:, 1:-1, :-2],
        padded[:, 1:-1, 2:],
    )
    source = forcing_part.astype(jnp.float32)
    for face_index in range(4):
        jump_term = (
            mask_part[face_index][..., None].astype(jnp.float32)
            * (neighbours[face_index].astype(jnp.float32) - center)
        ).astype(jnp.bfloat16)
        source = source + jnp.einsum(
            "labd,de->labe", jump_term, lifting[face_index], preferred_element_type=jnp.float32
        )
    solved = jnp.einsum(
        "labd,lade->labe", source.astype(jnp.bfloat16), inverse, preferred_element_type=jnp.float32
    )
    partial_sum = jnp.zeros(solved.shape[1:], jnp.float32)
    multiplier = jnp.ones((solved.shape[-1],), jnp.float32)
    partials = []
    factors = []
    for layer_index in range(layers_here):
        partial_sum = retention[layer_index] * partial_sum + solved[layer_index]
        multiplier = multiplier * retention[layer_index]
        partials.append(partial_sum)
        factors.append(multiplier)
    return (jnp.stack(partials), jnp.stack(factors))


def body(forcing, deformation_velocity, face_mask, lifting, inverse, retention):
    widened = jnp.pad(deformation_velocity, ((0, 0), (0, 0), (1, 1), (0, 0)))
    edged = extended(widened, (("cross", 1),), 1)
    partials, factors = sweep_terms(edged, forcing, face_mask, lifting, inverse, retention)
    identity = (jnp.ones_like(factors[-1]), jnp.zeros_like(partials[-1]))
    incoming = prefix((factors[-1], partials[-1]), "stream", chain_link, identity)[1]
    return partials + factors[:, None, None, :] * incoming[None]


def solution(mesh):
    return jax.shard_map(
        body,
        mesh=mesh,
        in_specs=(
            P("stream", "cross", None, None),
            P("stream", "cross", None, None),
            P(None, "stream", "cross", None),
            P(),
            P("stream", "cross", None, None),
            P("stream", None),
        ),
        out_specs=P("stream", "cross", None, None),
        check_vma=False,
    )
```

profile of v0, /device:TPU:0, one launch (start us, length us, event | category | flops | bytes accessed | tf_op | source)
XLA Modules:
  0.0 115.5 jit_solution(7275684202366346327)
XLA Ops:
  6.5 0.0 copy-start
  6.5 0.0 copy-start.1
  6.5 0.0 copy-start.5
  6.5 0.0 copy-start.6
  6.5 0.0 copy-start.4
  6.5 0.0 all-gather.3.cloned.1.call-start
  6.6 0.0 copy-start.3
  6.6 1.4 %pad_slice_fusion = (bf16[3,1,146,384]{3,2,1,0:T(8,128)(2,1)S(1)}, bf16[3,1,146,384]{3,2,1,0:T(8,128)(2,1)S(1)}) fusion(bf16[3,2,144,384]{3,2,1,0:T(8,128)(2,1)} %param.9), kind=kLoop, calls=%fused_computation.58 | loop fusion | bytes 1336320 | tf_op jit(solution)/shard_map/slice | solution.py:11
  8.0 2.5 %collective-permute-start = (bf16[3,1,146,384]{3,2,1,0:T(8,128)(2,1)S(1)}, bf16[3,1,146,384]{3,2,1,0:T(8,128)(2,1)S(1)}, u32[]{:S(2)}, u32[]{:S(2)}) collective-permute-start(bf16[3,1,146,384]{3,2,1,0:T(8,128)(2,1)S(1)} %get-tuple-element.137), channel_id=1, source_target_pairs={{0,1},{1,2},{2,3},{4,5},{5,6},{6,7},{8,9},{9,10},{10,11},{12,13},{... | collective-permute-start | bytes 1009160 | tf_op jit(solution)/shard_map/ppermute | solution.py:15
  10.5 1.3 %collective-permute-start.1 = (bf16[3,1,146,384]{3,2,1,0:T(8,128)(2,1)S(1)}, bf16[3,1,146,384]{3,2,1,0:T(8,128)(2,1)S(1)}, u32[]{:S(2)}, u32[]{:S(2)}) collective-permute-start(bf16[3,1,146,384]{3,2,1,0:T(8,128)(2,1)S(1)} %get-tuple-element.136), channel_id=1, source_target_pairs={{1,0},{2,1},{3,2},{5,4},{6,5},{7,6},{9,8},{10,9},{11,10},{13,12},{... | collective-permute-start | bytes 1009160 | tf_op jit(solution)/shard_map/ppermute | solution.py:17
  11.8 0.0 copy-done.5
  11.9 0.0 copy-done.6
  11.9 0.0 copy-done.1
  11.9 0.2 pad.4
  12.1 0.0 collective-permute-done
  12.1 0.0 copy-done.4
  12.1 0.0 copy-done.3
  12.1 0.7 convolution_add_fusion.3
  12.8 3.3 %collective-permute-done.1 = bf16[3,1,146,384]{3,2,1,0:T(8,128)(2,1)S(1)} collective-permute-done((bf16[3,1,146,384]{3,2,1,0:T(8,128)(2,1)S(1)}, bf16[3,1,146,384]{3,2,1,0:T(8,128)(2,1)S(1)}, u32[]{:S(2)}, u32[]{:S(2)}) %collective-permute-start.1) | collective-permute-done | bytes 336416 | tf_op jit(solution)/shard_map/ppermute | solution.py:17
  16.2 0.7 convolution_add_fusion.2
  16.9 1.8 %convolution_add_fusion.1 = f32[3,2,144,384]{3,2,1,0:T(8,128)} fusion(f32[3,2,144,384]{3,2,1,0:T(8,128)S(1)} %convolution_add_fusion.2, bf16[3,2,144,384]{3,2,1,0:T(8,128)(2,1)S(1)} %copy-done.1, f32[3,2,144]{2,1,0:T(2,128)S(1)} %get-tuple-element.141, bf16[4,384,384]{2,1,0:T(8,128)(2,1)S(1)} %copy-done.3), kind=kOutput, calls=%fused_computation.8 | convolution fusion | flops 256794624 | bytes 3618816 | tf_op jit(solution)/shard_map/labd,de->labe/dot_general | solution.py:60
  18.6 0.0 copy-done
  18.6 3.6 %fusion.10 = f32[3,2,144,384]{3,2,1,0:T(8,128)} fusion(bf16[3,2,384,384]{3,2,1,0:T(8,128)(2,1)S(1)} %copy-done, f32[3,2,144,384]{3,2,1,0:T(8,128)} %convolution_add_fusion.1, bf16[3,2,144,384]{3,2,1,0:T(8,128)(2,1)S(1)} %copy-done.1, f32[3,2,144]{2,1,0:T(2,128)S(1)} %get-tuple-element.138, bf16[4,384,384]{2,1,0:T(8,128)(2,1)} %param.11), kind=kOutput, calls=%fused_computation.21 | convolution fusion | flops 511930368 | bytes 5385600 | tf_op jit(solution)/shard_map/labd,lade->labe/dot_general | solution.py:63
  22.2 2.1 %slice_add_fusion = (f32[1,2,144,384]{3,2,1,0:T(8,128)}, f32[1,2,144,384]{3,2,1,0:T(8,128)S(1)}, f32[1,2,144,384]{3,2,1,0:T(8,128)S(1)}) fusion(f32[3,2,144,384]{3,2,1,0:T(8,128)} %fusion.10, f32[384]{0:T(512)S(1)} %get-tuple-element.146, f32[384]{0:T(512)S(1)} %get-tuple-element.144, f32[384]{0:T(512)S(1)} %get-tuple-element.145), kind=kLoop, calls=%fused_computation.32 | loop fusion | flops 552960 | bytes 2658816 | tf_op jit(solution)/shard_map/add | solution.py:71
  24.4 0.0 all-gather.3.cloned.1.call-update
  24.4 26.4 %all-gather = f32[8,1,384]{2,1,0:T(1,128)S(1)} all-gather(f32[1,1,384]{2,1,0:T(1,128)S(1)} %bitcast.49), channel_id=1, replica_groups=mesh['stream'=8,'cross'=4] {'stream'}, dimensions={0}, use_global_device_ids=true | all-gather | bytes 13824 | tf_op jit(solution)/shard_map/all_gather | solution.py:26
  50.8 0.6 pad_maximum_fusion.4
  51.4 44.0 %all-gather.3.cloned.1.call-done = f32[8,2,144,384]{3,2,1,0:T(8,128)} async-done(((f32[1,2,144,384]{3,2,1,0:T(8,128)}), f32[8,2,144,384]{3,2,1,0:T(8,128)}) %all-gather.3.cloned.1.call-update) | async-done | bytes 3538960 | tf_op jit(solution)/shard_map/all_gather | solution.py:26
  95.4 0.0 copy-start.2
  95.4 11.4 %while.14 = (s32[]{:T(128)}, f32[2,144,384]{2,1,0:T(8,128)S(1)}, s32[]{:T(128)}, f32[8,384]{1,0:T(8,128)S(1)}, f32[8,2,144,384]{3,2,1,0:T(8,128)}, /*index=5*/s32[]{:T(128)}, s32[]{:T(128)}) while((s32[]{:T(128)}, f32[2,144,384]{2,1,0:T(8,128)S(1)}, s32[]{:T(128)}, f32[8,384]{1,0:T(8,128)S(1)}, f32[8,2,144,384]{3,2,1,0:T(8,128)}, ...), condition=%wide.region_1.2_spmd.clone, body=%wide.region_0.1_spmd.clone.sunk | while | flops 442372 | bytes 1331817 | solution.py:38
  95.4 1.4 %fusion.46 = f32[2,144,384]{2,1,0:T(8,128)S(1)} fusion(f32[8,2,144,384]{3,2,1,0:T(8,128)} %get-tuple-element.196, s32[]{:T(128)} %get-tuple-element.185, f32[2,144,384]{2,1,0:T(8,128)S(1)} %get-tuple-element.186, f32[384]{0:T(512)S(1)} %dynamic-slice_reduce_fusion.2, pred[]{:T(512)S(6)} %compare.4, pred[]{:T(512)S(6)} %lt.22), kind=kLoop, calls=%fused_computation.1.clone.1 | loop fusion | flops 442368 | bytes 1328646 | tf_op jit(solution)/shard_map/while/body/eval_jaxpr/jit(_where)/select_n | solution.py:36
  96.9 1.4 %fusion.46 = f32[2,144,384]{2,1,0:T(8,128)S(1)} fusion(f32[8,2,144,384]{3,2,1,0:T(8,128)} %get-tuple-element.196, s32[]{:T(128)} %get-tuple-element.185, f32[2,144,384]{2,1,0:T(8,128)S(1)} %get-tuple-element.186, f32[384]{0:T(512)S(1)} %dynamic-slice_reduce_fusion.2, pred[]{:T(512)S(6)} %compare.4, pred[]{:T(512)S(6)} %lt.22), kind=kLoop, calls=%fused_computation.1.clone.1 | loop fusion | flops 442368 | bytes 1328646 | tf_op jit(solution)/shard_map/while/body/eval_jaxpr/jit(_where)/select_n | solution.py:36
  98.3 1.4 %fusion.46 = f32[2,144,384]{2,1,0:T(8,128)S(1)} fusion(f32[8,2,144,384]{3,2,1,0:T(8,128)} %get-tuple-element.196, s32[]{:T(128)} %get-tuple-element.185, f32[2,144,384]{2,1,0:T(8,128)S(1)} %get-tuple-element.186, f32[384]{0:T(512)S(1)} %dynamic-slice_reduce_fusion.2, pred[]{:T(512)S(6)} %compare.4, pred[]{:T(512)S(6)} %lt.22), kind=kLoop, calls=%fused_computation.1.clone.1 | loop fusion | flops 442368 | bytes 1328646 | tf_op jit(solution)/shard_map/while/body/eval_jaxpr/jit(_where)/select_n | solution.py:36
  99.7 1.4 %fusion.46 = f32[2,144,384]{2,1,0:T(8,128)S(1)} fusion(f32[8,2,144,384]{3,2,1,0:T(8,128)} %get-tuple-element.196, s32[]{:T(128)} %get-tuple-element.185, f32[2,144,384]{2,1,0:T(8,128)S(1)} %get-tuple-element.186, f32[384]{0:T(512)S(1)} %dynamic-slice_reduce_fusion.2, pred[]{:T(512)S(6)} %compare.4, pred[]{:T(512)S(6)} %lt.22), kind=kLoop, calls=%fused_computation.1.clone.1 | loop fusion | flops 442368 | bytes 1328646 | tf_op jit(solution)/shard_map/while/body/eval_jaxpr/jit(_where)/select_n | solution.py:36
  101.1 1.4 %fusion.46 = f32[2,144,384]{2,1,0:T(8,128)S(1)} fusion(f32[8,2,144,384]{3,2,1,0:T(8,128)} %get-tuple-element.196, s32[]{:T(128)} %get-tuple-element.185, f32[2,144,384]{2,1,0:T(8,128)S(1)} %get-tuple-element.186, f32[384]{0:T(512)S(1)} %dynamic-slice_reduce_fusion.2, pred[]{:T(512)S(6)} %compare.4, pred[]{:T(512)S(6)} %lt.22), kind=kLoop, calls=%fused_computation.1.clone.1 | loop fusion | flops 442368 | bytes 1328646 | tf_op jit(solution)/shard_map/while/body/eval_jaxpr/jit(_where)/select_n | solution.py:36
  102.5 1.4 %fusion.46 = f32[2,144,384]{2,1,0:T(8,128)S(1)} fusion(f32[8,2,144,384]{3,2,1,0:T(8,128)} %get-tuple-element.196, s32[]{:T(128)} %get-tuple-element.185, f32[2,144,384]{2,1,0:T(8,128)S(1)} %get-tuple-element.186, f32[384]{0:T(512)S(1)} %dynamic-slice_reduce_fusion.2, pred[]{:T(512)S(6)} %compare.4, pred[]{:T(512)S(6)} %lt.22), kind=kLoop, calls=%fused_computation.1.clone.1 | loop fusion | flops 442368 | bytes 1328646 | tf_op jit(solution)/shard_map/while/body/eval_jaxpr/jit(_where)/select_n | solution.py:36
  104.0 1.4 %fusion.46 = f32[2,144,384]{2,1,0:T(8,128)S(1)} fusion(f32[8,2,144,384]{3,2,1,0:T(8,128)} %get-tuple-element.196, s32[]{:T(128)} %get-tuple-element.185, f32[2,144,384]{2,1,0:T(8,128)S(1)} %get-tuple-element.186, f32[384]{0:T(512)S(1)} %dynamic-slice_reduce_fusion.2, pred[]{:T(512)S(6)} %compare.4, pred[]{:T(512)S(6)} %lt.22), kind=kLoop, calls=%fused_computation.1.clone.1 | loop fusion | flops 442368 | bytes 1328646 | tf_op jit(solution)/shard_map/while/body/eval_jaxpr/jit(_where)/select_n | solution.py:36
  105.4 1.4 %fusion.46 = f32[2,144,384]{2,1,0:T(8,128)S(1)} fusion(f32[8,2,144,384]{3,2,1,0:T(8,128)} %get-tuple-element.196, s32[]{:T(128)} %get-tuple-element.185, f32[2,144,384]{2,1,0:T(8,128)S(1)} %get-tuple-element.186, f32[384]{0:T(512)S(1)} %dynamic-slice_reduce_fusion.2, pred[]{:T(512)S(6)} %compare.4, pred[]{:T(512)S(6)} %lt.22), kind=kLoop, calls=%fused_computation.1.clone.1 | loop fusion | flops 442368 | bytes 1328646 | tf_op jit(solution)/shard_map/while/body/eval_jaxpr/jit(_where)/select_n | solution.py:36
  106.7 0.0 copy-done.2
  106.8 1.9 %maximum_add_fusion = f32[3,2,144,384]{3,2,1,0:T(8,128)} fusion(f32[1,2,144,384]{3,2,1,0:T(8,128)S(1)} %copy-done.2, f32[1,2,144,384]{3,2,1,0:T(8,128)S(1)} %get-tuple-element.134, f32[1,2,144,384]{3,2,1,0:T(8,128)S(1)} %get-tuple-element.135, f32[2,144,384]{2,1,0:T(8,128)S(1)} %get-tuple-element.99, f32[3,384]{1,0:T(4,128)} %pad_maximum_fusion.4), kind=kLoop, calls=%fused_computation.20 | loop fusion | flops 1327104 | bytes 3101184 | tf_op jit(solution)/shard_map/add | solution.py:84
  (12 shorter events, 0.2 us)
Async XLA Ops:
  6.5 12.1 %copy-start = (bf16[3,2,384,384]{3,2,1,0:T(8,128)(2,1)S(1)}, bf16[3,2,384,384]{3,2,1,0:T(8,128)(2,1)}, u32[]{:S(2)}) copy-start(bf16[3,2,384,384]{3,2,1,0:T(8,128)(2,1)} %param.12) | copy-start | bytes 5308420
  6.5 5.4 %copy-start.1 = (bf16[3,2,144,384]{3,2,1,0:T(8,128)(2,1)S(1)}, bf16[3,2,144,384]{3,2,1,0:T(8,128)(2,1)}, u32[]{:S(2)}) copy-start(bf16[3,2,144,384]{3,2,1,0:T(8,128)(2,1)} %param.9) | copy-start | bytes 1990660
  6.5 5.3 %copy-start.5 = (s32[4,3,2,144]{3,2,1,0:T(2,128)S(1)}, s32[4,3,2,144]{3,2,1,0:T(2,128)}, u32[]{:S(2)}) copy-start(s32[4,3,2,144]{3,2,1,0:T(2,128)} %param.10) | copy-start | bytes 41476
  6.5 5.3 %copy-start.6 = (f32[3,384]{1,0:T(4,128)S(1)}, f32[3,384]{1,0:T(4,128)}, u32[]{:S(2)}) copy-start(f32[3,384]{1,0:T(4,128)} %param.13) | copy-start | bytes 13828
  6.5 5.6 %copy-start.4 = (bf16[3,2,144,384]{3,2,1,0:T(8,128)(2,1)S(1)}, bf16[3,2,144,384]{3,2,1,0:T(8,128)(2,1)}, u32[]{:S(2)}) copy-start(bf16[3,2,144,384]{3,2,1,0:T(8,128)(2,1)} %param.8) | copy-start | bytes 1990660
  6.5 88.8 %all-gather.3.cloned.1.call-start = ((), (), s32[]{:S(2)}) async-start(), calls=%async_computation | async-start | bytes 3981312 | tf_op jit(solution)/shard_map/all_gather | solution.py:26
  6.6 5.5 %copy-start.3 = (bf16[4,384,384]{2,1,0:T(8,128)(2,1)S(1)}, bf16[4,384,384]{2,1,0:T(8,128)(2,1)}, u32[]{:S(2)}) copy-start(bf16[4,384,384]{2,1,0:T(8,128)(2,1)} %param.11) | copy-start | bytes 3538948
  8.0 4.1 %collective-permute-start = (bf16[3,1,146,384]{3,2,1,0:T(8,128)(2,1)S(1)}, bf16[3,1,146,384]{3,2,1,0:T(8,128)(2,1)S(1)}, u32[]{:S(2)}, u32[]{:S(2)}) collective-permute-start(bf16[3,1,146,384]{3,2,1,0:T(8,128)(2,1)S(1)} %get-tuple-element.137), channel_id=1, source_target_pairs={{0,1},{1,2},{2,3},{4,5},{5,6},{6,7},{8,9},{9,10},{10,11},{12,13},{... | collective-permute-start | bytes 1009160 | tf_op jit(solution)/shard_map/ppermute | solution.py:15
  10.5 5.6 %collective-permute-start.1 = (bf16[3,1,146,384]{3,2,1,0:T(8,128)(2,1)S(1)}, bf16[3,1,146,384]{3,2,1,0:T(8,128)(2,1)S(1)}, u32[]{:S(2)}, u32[]{:S(2)}) collective-permute-start(bf16[3,1,146,384]{3,2,1,0:T(8,128)(2,1)S(1)} %get-tuple-element.136), channel_id=1, source_target_pairs={{1,0},{2,1},{3,2},{5,4},{6,5},{7,6},{9,8},{10,9},{11,10},{13,12},{... | collective-permute-start | bytes 1009160 | tf_op jit(solution)/shard_map/ppermute | solution.py:17
  95.4 11.4 %copy-start.2 = (f32[1,2,144,384]{3,2,1,0:T(8,128)S(1)}, f32[1,2,144,384]{3,2,1,0:T(8,128)}, u32[]{:S(2)}) copy-start(f32[1,2,144,384]{3,2,1,0:T(8,128)} %get-tuple-element.133) | copy-start | bytes 1327108
Sparse Core Ops, SparseCore 0:
  24.5 70.8 all-gather.2
where the time goes:
time: 116 us; the launch traced here: 115 us
  waiting for transfers between devices  47.4 us (41%)
  blocking collectives  26.4 us (23%)
  other arithmetic  15.7 us (14%)
  between operations  13.5 us (12%)
  matrix products  6.75 us (6%)
  starting transfers between devices  3.84 us (3%)
  local copies, waits for them, and re-layouts  1.78 us (2%)
    all_gather x1, waiting for transfers between devices, prefix(): everything = jax.tree.map(lambda part: lax.all_gather(part, axis), array)  44 us
    all_gather x1, blocking collectives, prefix(): everything = jax.tree.map(lambda part: lax.all_gather(part, axis), array)  26.4 us
    select_n x8, other arithmetic, lap(): return jax.tree.map(lambda a, b: jnp.where(reached, a, b), new, before)  11 us
    dot_general x1, matrix products, sweep_terms(): jnp.einsum('labd,lade->labe', source.astype(jnp.bfloat16), inverse, prefe...  3.59 us
    ppermute x1, waiting for transfers between devices, extended(): lax.ppermute(head, axis, [((i + 1) % count, i) for i in range(ends)])  3.35 us
    dot_general x3, matrix products, sweep_terms(): jnp.einsum('labd,de->labe', jump_term, lifting[face_index], preferred_ele...  3.16 us
    ppermute x1, starting transfers between devices, extended(): lax.ppermute(tail, axis, [(i, (i + 1) % count) for i in range(ends)])  2.51 us
  transfers between devices with their start and end apart: 3, of which 2 were waited for; matrix products, arithmetic and copies ran while one was open for 1% of the time, Pallas kernels for 0%

commit v1 on v0

v1 whole, which is shorter than its diff:
```python
import functools

import jax
import jax.numpy as jnp
from jax import lax
from jax.experimental import pallas as pl
from jax.experimental.pallas import tpu as pltpu
from jax.sharding import PartitionSpec as P

GROUP = 4
F32, BF16 = jnp.float32, jnp.bfloat16
VMEM_LIMIT = 48 * 1024 * 1024


def masked_jump(mask, neighbour, center):
    return (mask * (neighbour - center)).astype(BF16)


def along_b(cells):
    rows = lax.broadcasted_iota(jnp.int32, cells.shape, 0)
    last = cells.shape[0] - 1
    lower = jnp.where(rows == 0, 0.0, pltpu.roll(cells, 1, 0))
    upper = jnp.where(rows == last, 0.0, pltpu.roll(cells, last, 0))
    return lower, upper


def mask_columns(mask_ref, layer):
    rows = [mask_ref[face, layer, a : a + 1, :] for face in range(4) for a in range(2)]
    return jnp.concatenate(rows, axis=0).astype(F32).T


def dot(a, b):
    return jnp.dot(a, b, preferred_element_type=F32)


def inner_kernel(place, mask_ref, cells_ref, forcing_ref, halo_ref, lift_ref, inverse_ref, keep_ref, far_ref, near_ref, carry):
    layer = pl.program_id(0)
    odd = place[0]
    near_at, far_at = odd, 1 - odd
    columns = mask_columns(mask_ref, 0)
    is_odd = odd == 1

    def mask(face_even, a_even, face_odd, a_odd):
        even = columns[:, 2 * face_even + a_even : 2 * face_even + a_even + 1]
        other = columns[:, 2 * face_odd + a_odd : 2 * face_odd + a_odd + 1]
        return jnp.where(is_odd, other, even)

    far = cells_ref[0, far_at].astype(F32)
    near = cells_ref[0, near_at].astype(F32)
    halo = halo_ref[0].astype(F32)
    outer_face, inner_face = 1 - odd, odd
    far_low, far_up = along_b(far)
    near_low, near_up = along_b(near)
    far_source = forcing_ref[0, far_at].astype(F32)
    near_source = forcing_ref[0, near_at].astype(F32)
    pairs = (
        (masked_jump(mask(1, 1, 0, 0), halo, far), masked_jump(mask(1, 0, 0, 1), far, near), lift_ref[outer_face]),
        (masked_jump(mask(2, 1, 2, 0), far_low, far), masked_jump(mask(2, 0, 2, 1), near_low, near), lift_ref[2]),
        (masked_jump(mask(3, 1, 3, 0), far_up, far), masked_jump(mask(3, 0, 3, 1), near_up, near), lift_ref[3]),
    )
    far_source = far_source + dot(masked_jump(mask(0, 1, 1, 0), near, far), lift_ref[inner_face])
    for far_jump, near_jump, matrix in pairs:
        far_source = far_source + dot(far_jump, matrix)
        near_source = near_source + dot(near_jump, matrix)
    near_ref[0] = near_source
    solved = dot(far_source.astype(BF16), inverse_ref[0, 0])

    @pl.when(layer == 0)
    def _():
        carry[...] = solved

    @pl.when(layer > 0)
    def _():
        carry[...] = keep_ref[pl.ds(layer, 1), :] * carry[...] + solved

    far_ref[0] = carry[...]


def outer_kernel(place, mask_ref, cells_ref, halo_ref, source_ref, lift_ref, inverse_ref, keep_ref, far_ref, near_ref, p0, p1, p2, p3, carry):
    layer = pl.program_id(0)
    layers = pl.num_programs(0)
    odd = place[0]
    columns = mask_columns(mask_ref, 0)
    mask = jnp.where(odd == 1, columns[:, 3:4], columns[:, 0:1])
    near = cells_ref[0, 0].astype(F32)
    jump = masked_jump(mask, halo_ref[0].astype(F32), near)
    source = source_ref[0] + dot(jump, lift_ref[0])
    solved = dot(source.astype(BF16), inverse_ref[0, 0])
    rows = near.shape[0]
    mine = pl.ds(rows, rows)

    @pl.when(layer == 0)
    def _():
        carry[mine, :] = solved

    @pl.when(layer > 0)
    def _():
        carry[mine, :] = keep_ref[pl.ds(layer, 1), :] * carry[mine, :] + solved

    near_ref[0] = carry[mine, :]

    @pl.when(layer == layers - 1)
    def _():
        carry[pl.ds(0, rows), :] = far_ref[0]
        factor = keep_ref[0:1, :]
        for at in range(1, keep_ref.shape[0]):
            factor = factor * keep_ref[at : at + 1, :]
        high = factor.astype(BF16).astype(F32)
        low = factor - high
        at = lax.broadcasted_iota(jnp.int32, (8, factor.shape[1]), 0)
        extra = jnp.where(at == 0, high, jnp.where(at == 1, low, 0.0))
        piece = 2 * rows // GROUP
        for k, out in enumerate((p0, p1, p2, p3)):
            start = pl.multiple_of((place[1] ^ k) * piece, 8)
            out[...] = jnp.concatenate([carry[pl.ds(start, piece), :], extra], axis=0).astype(BF16)


def final_kernel(place, far_ref, near_ref, keep_ref, e0, e1, e2, e3, out_ref, incoming):
    layer = pl.program_id(0)
    rows = far_ref.shape[1]
    odd = place[0]
    piece = e0.shape[0]

    @pl.when(layer == 0)
    def _():
        for k, part in enumerate((e0, e1, e2, e3)):
            start = pl.multiple_of((place[1] ^ k) * piece, 8)
            incoming[pl.ds(start, piece), :] = part[...].astype(F32)

    incoming[...] = keep_ref[pl.ds(layer, 1), :] * incoming[...]
    out_ref[0, 1 - odd] = far_ref[0] + incoming[pl.ds(0, rows), :]
    out_ref[0, odd] = near_ref[0] + incoming[pl.ds(rows, rows), :]


def call(kernel, place, operands, in_specs, outs, out_specs, layers, scratch, flops, moved):
    return pl.pallas_call(
        kernel,
        out_shape=outs,
        grid_spec=pltpu.PrefetchScalarGridSpec(
            num_scalar_prefetch=1, grid=(layers,), in_specs=in_specs, out_specs=out_specs, scratch_shapes=scratch
        ),
        compiler_params=pltpu.CompilerParams(dimension_semantics=("arbitrary",), vmem_limit_bytes=VMEM_LIMIT),
        cost_estimate=pl.CostEstimate(flops=flops, bytes_accessed=moved, transcendentals=0),
    )(place, *operands)


def body(forcing, cells, face_mask, lifting, inverse, retention):
    layers, _, width, dofs = cells.shape
    crosses, streams = lax.axis_size("cross"), lax.axis_size("stream")
    cross, stream = lax.axis_index("cross"), lax.axis_index("stream")
    odd, member = cross % 2, stream % GROUP
    place = jnp.stack([odd, member]).astype(jnp.int32)

    outward = jnp.where(odd == 1, cells[:, 0], cells[:, 1])
    across = jnp.where(odd == 1, cells[:, 1], cells[:, 0])
    core_halo = lax.ppermute(outward, "cross", [(i, i ^ 1) for i in range(crosses)])
    links = [pair for i in range(1, crosses - 1, 2) for pair in ((i, i + 1), (i + 1, i))]
    chip_halo = lax.ppermute(across, "cross", links)

    row = lambda at: pl.BlockSpec((1, 1, width, dofs), lambda l, s, at=at: (l, at(s), 0, 0))
    both = pl.BlockSpec((1, 2, width, dofs), lambda l, s: (l, 0, 0, 0))
    single = pl.BlockSpec((1, width, dofs), lambda l, s: (l, 0, 0))
    masks = pl.BlockSpec((4, 1, 2, width), lambda l, s: (0, l, 0, 0))
    keeps = pl.BlockSpec((layers, dofs), lambda l, s: (0, 0))
    square = lambda at: pl.BlockSpec((1, 1, dofs, dofs), lambda l, s, at=at: (l, at(s), 0, 0))
    near_at = lambda s: s[0]
    far_at = lambda s: 1 - s[0]
    stack = jax.ShapeDtypeStruct((layers, width, dofs), F32)
    unit = 2 * layers * width * dofs * dofs

    far, near_source = call(
        inner_kernel,
        place,
        (face_mask, cells, forcing, core_halo, lifting, inverse, retention),
        [masks, both, both, single, pl.BlockSpec((4, dofs, dofs), lambda l, s: (0, 0, 0)), square(far_at), keeps],
        (stack, stack),
        (single, single),
        layers,
        [pltpu.VMEM((width, dofs), F32)],
        8 * unit,
        8_000_000,
    )

    piece = 2 * width // GROUP
    payload = jax.ShapeDtypeStruct((piece + 8, dofs), BF16)
    whole = pl.BlockSpec((piece + 8, dofs), lambda l, s: (0, 0))
    near, *pieces = call(
        outer_kernel,
        place,
        (face_mask, cells, chip_halo, near_source, lifting, inverse, retention, far),
        [
            masks,
            row(near_at),
            single,
            single,
            pl.BlockSpec((1, dofs, dofs), lambda l, s: (s[0], 0, 0)),
            square(near_at),
            keeps,
            pl.BlockSpec((1, width, dofs), lambda l, s: (layers - 1, 0, 0)),
        ],
        (stack,) + (payload,) * GROUP,
        (single,) + (whole,) * GROUP,
        layers,
        [pltpu.VMEM((2 * width, dofs), F32)],
        2 * unit,
        3_000_000,
    )

    def swap(part, distance):
        return lax.ppermute(part, "stream", [(i, i ^ distance) for i in range(streams)])

    got = [pieces[0]] + [swap(pieces[k], k) for k in range(1, GROUP)]
    pick = lambda parts, j: functools.reduce(
        lambda rest, k: jnp.where((member ^ k) == j, parts[k], rest), range(1, GROUP), parts[0]
    )
    ordered = [pick(got, j).astype(F32) for j in range(GROUP)]
    values = [part[:piece] for part in ordered]
    factors = [part[piece : piece + 1] + part[piece + 1 : piece + 2] for part in ordered]

    total, total_factor = values[0], factors[0]
    for j in range(1, GROUP):
        total = factors[j] * total + values[j]
        total_factor = total_factor * factors[j]
    before, before_factor = jnp.zeros_like(total), jnp.ones_like(total_factor)
    distance = GROUP
    while distance < streams:
        last = 2 * distance >= streams
        if last:
            met = swap(total.astype(BF16), distance).astype(F32)
        else:
            high = total_factor.astype(BF16)
            low = (total_factor - high.astype(F32)).astype(BF16)
            met = swap(jnp.concatenate([total.astype(BF16), high, low], axis=0), distance).astype(F32)
        later = (stream & distance) != 0
        before = jnp.where(later, before_factor * met[:piece] + before, before)
        if not last:
            met_factor = met[piece : piece + 1] + met[piece + 1 : piece + 2]
            before_factor = jnp.where(later, before_factor * met_factor, before_factor)
            total = jnp.where(later, total_factor * met[:piece] + total, met_factor * total + met[:piece])
            total_factor = total_factor * met_factor
        distance *= 2

    entering = [before]
    for j in range(GROUP - 1):
        entering.append(factors[j] * entering[j] + values[j])
    entering = [part.astype(BF16) for part in entering]
    give = [pick(entering, k) for k in range(GROUP)]
    back = [give[0]] + [swap(give[k], k) for k in range(1, GROUP)]

    part = pl.BlockSpec((piece, dofs), lambda l, s: (0, 0))
    return call(
        final_kernel,
        place,
        (far, near, retention, *back),
        [single, single, keeps] + [part] * GROUP,
        jax.ShapeDtypeStruct((layers, 2, width, dofs), F32),
        both,
        layers,
        [pltpu.VMEM((2 * width, dofs), F32)],
        1_000_000,
        4_000_000,
    )


def solution(mesh):
    return jax.shard_map(
        body,
        mesh=mesh,
        in_specs=(
            P("stream", "cross", None, None),
            P("stream", "cross", None, None),
            P(None, "stream", "cross", None),
            P(),
            P("stream", "cross", None, None),
            P("stream", None),
        ),
        out_specs=P("stream", "cross", None, None),
        check_vma=False,
    )
```

time: 116 us -> 37.3 us (0.32)
  waiting for transfers between devices: 47.4 us -> 11.7 us
  blocking collectives: 26.4 us -> 0 us
  other arithmetic: 15.7 us -> 1.58 us
  between operations: 13.5 us -> 0.1 us
  Pallas kernels: 0 us -> 8.88 us
  starting transfers between devices: 3.84 us -> 12.1 us
  matrix products: 6.75 us -> 0 us
    all_gather x1 -> x0, waiting for transfers between devices: 44 us -> none  [prefix(): everything = jax.tree.map(lambda part: lax.all_gather(part, axis), array)]
    all_gather x1 -> x0, blocking collectives: 26.4 us -> none  [prefix(): everything = jax.tree.map(lambda part: lax.all_gather(part, axis), array)]
    select_n x8 -> x3, other arithmetic: 11 us -> 1.35 us  [the longest x1 1.25 us: body(): across = jnp.where(odd == 1, cells[:, 1], cells[:, 0])]
    pallas_call x0 -> x3, Pallas kernels: none -> 8.88 us  [call(): pl.pallas_call(kernel, out_shape=outs, grid_spec=pltpu.PrefetchScalarGrid...]
    ppermute x2 -> x9, waiting for transfers between devices: 3.35 us -> 11.7 us  [the longest x7 11.2 us: swap(): lax.ppermute(part, 'stream', [(i, i ^ distance) for i in range(streams)])]
    ppermute x2 -> x9, starting transfers between devices: 3.8 us -> 12.1 us  [the longest x7 10.9 us: swap(): lax.ppermute(part, 'stream', [(i, i ^ distance) for i in range(streams)])]
    dot_general x4 -> x0, matrix products: 6.75 us -> none  [the longest x1 3.59 us: sweep_terms(): jnp.einsum('labd,lade->labe', source.astype(jnp.bfloat16), inverse, prefe...]
    add x2 -> x3, other arithmetic: 4 us -> 0.06 us  [body(): part[piece:piece + 1] + part[piece + 1:piece + 2]]
  transfers between devices with their start and end apart: 3 -> 9, of which waited for: 2 -> 8; matrix products, arithmetic and copies ran while one was open for 1% -> 0% of each run, Pallas kernels for 0% -> 11%
where the time goes in v1:
time: 37.3 us; the launch traced here: 37.1 us
  starting transfers between devices  12.1 us (32%)
  waiting for transfers between devices  11.7 us (31%)
  Pallas kernels  8.88 us (24%)
  local copies, waits for them, and re-layouts  2.76 us (7%)
  other arithmetic  1.58 us (4%)
    ppermute x7, waiting for transfers between devices, swap(): lax.ppermute(part, 'stream', [(i, i ^ distance) for i in range(streams)])  11.2 us
    ppermute x7, starting transfers between devices, swap(): lax.ppermute(part, 'stream', [(i, i ^ distance) for i in range(streams)])  10.9 us
    pallas_call x3, Pallas kernels, call(): pl.pallas_call(kernel, out_shape=outs, grid_spec=pltpu.PrefetchScalarGrid...  8.88 us
    unnamed x14, local copies, waits for them, and re-layouts  2.76 us
    select_n x1, other arithmetic, body(): across = jnp.where(odd == 1, cells[:, 1], cells[:, 0])  1.25 us
  transfers between devices with their start and end apart: 9, of which 8 were waited for; matrix products, arithmetic and copies ran while one was open for 0% of the time, Pallas kernels for 11%

profile of v1, /device:TPU:0, one launch (start us, length us, event | category | flops | bytes accessed | tf_op | source)
XLA Modules:
  0.0 37.1 jit_solution(14406397988602963221)
XLA Ops:
  0.0 0.0 copy-start.2
  0.0 0.0 copy-start.6
  0.0 0.0 copy-start.5
  0.0 0.0 copy-start.4
  0.0 1.2 %fusion.1 = (bf16[3,144,384]{2,1,0:T(8,128)(2,1)S(1)}, bf16[3,144,384]{2,1,0:T(8,128)(2,1)S(1)}) fusion(pred[]{:T(512)S(6)} %eq.55, bf16[3,2,144,384]{3,2,1,0:T(8,128)(2,1)} %cells_ref.3), kind=kLoop, calls=%fused_computation.3 | loop fusion | flops 331776 | bytes 1327105 | tf_op jit(solution)/shard_map/jit(_where)/select_n | solution.py:155
  1.3 0.5 %collective-permute-start = (bf16[3,144,384]{2,1,0:T(8,128)(2,1)S(1)}, bf16[3,144,384]{2,1,0:T(8,128)(2,1)S(1)}, u32[]{:S(2)}, u32[]{:S(2)}) collective-permute-start(bf16[3,144,384]{2,1,0:T(8,128)(2,1)S(1)} %get-tuple-element.24), channel_id=1, source_target_pairs={{0,1},{1,0},{2,3},{3,2},{4,5},{5,4},{6,7},{7,6},{8,9},{9,8},{10,11... | collective-permute-start | bytes 995336 | tf_op jit(solution)/shard_map/ppermute | solution.py:156
  1.8 0.7 %collective-permute-start.1 = (bf16[3,144,384]{2,1,0:T(8,128)(2,1)S(1)}, bf16[3,144,384]{2,1,0:T(8,128)(2,1)S(1)}, u32[]{:S(2)}, u32[]{:S(2)}) collective-permute-start(bf16[3,144,384]{2,1,0:T(8,128)(2,1)S(1)} %get-tuple-element.23), channel_id=1, source_target_pairs={{1,2},{2,1},{5,6},{6,5},{9,10},{10,9},{13,14},{14,13},{17,18},{18,... | collective-permute-start | bytes 995336 | tf_op jit(solution)/shard_map/ppermute | solution.py:158
  2.5 0.1 pad_add_fusion.place
  2.6 0.5 %collective-permute-done.halo_ref = bf16[3,144,384]{2,1,0:T(8,128)(2,1)S(1)} collective-permute-done((bf16[3,144,384]{2,1,0:T(8,128)(2,1)S(1)}, bf16[3,144,384]{2,1,0:T(8,128)(2,1)S(1)}, u32[]{:S(2)}, u32[]{:S(2)}) %collective-permute-start) | collective-permute-done | bytes 331808 | tf_op jit(solution)/shard_map/ppermute | solution.py:156
  3.1 0.0 copy-done.2
  3.1 0.0 copy-done.6
  3.1 0.0 copy-done.5
  3.1 0.0 copy-done.4
  3.1 0.0 copy-start
  3.1 1.5 %copy-done = bf16[3,2,384,384]{3,2,1,0:T(8,128)(2,1)S(1)} copy-done((bf16[3,2,384,384]{3,2,1,0:T(8,128)(2,1)S(1)}, bf16[3,2,384,384]{3,2,1,0:T(8,128)(2,1)}, u32[]{:S(2)}) %copy-start) | copy-done | bytes 1769496
  4.6 0.0 copy-start.3
  4.6 1.3 %copy-done.3 = bf16[4,384,384]{2,1,0:T(8,128)(2,1)S(1)} copy-done((bf16[4,384,384]{2,1,0:T(8,128)(2,1)S(1)}, bf16[4,384,384]{2,1,0:T(8,128)(2,1)}, u32[]{:S(2)}) %copy-start.3) | copy-done | bytes 1179672
  5.8 0.0 copy-start.1
  5.8 4.0 %shard_map.64 = (f32[3,144,384]{2,1,0:T(8,128)S(1)}, f32[3,144,384]{2,1,0:T(8,128)S(1)}) custom-call(s32[2]{0:T(128)S(1)} %pad_add_fusion.place, s32[4,3,2,144]{3,2,1,0:T(2,128)S(1)} %copy-done.5, bf16[3,2,144,384]{3,2,1,0:T(8,128)(2,1)S(1)} %copy-done.2, bf16[3,2,144,384]{3,2,1,0:T(8,128)(2,1)S(1)} %copy-done.4, ...), custom_call_target="tpu_custom_call" | custom-call | flops 1019215872 | bytes 8000000 | tf_op jit(solution)/shard_map/pallas_call | solution.py:136
  9.8 0.0 collective-permute-done.1.halo_ref
  9.8 0.0 copy-done.1
  9.8 2.6 %shard_map.65 = (f32[3,144,384]{2,1,0:T(8,128)S(1)}, bf16[80,384]{1,0:T(8,128)(2,1)S(1)}, bf16[80,384]{1,0:T(8,128)(2,1)S(1)}, bf16[80,384]{1,0:T(8,128)(2,1)S(1)}, bf16[80,384]{1,0:T(8,128)(2,1)S(1)}) custom-call(s32[2]{0:T(128)S(1)} %pad_add_fusion.place, s32[4,3,2,144]{3,2,1,0:T(2,128)S(1)} %copy-done.5, bf16[3,2,144,384]{3,2,1,0:T(8,128)(2,1)S(1)} %copy-done.2, ...), custom_call_target="tpu_custom_call" | custom-call | flops 254803968 | bytes 3000000 | tf_op jit(solution)/shard_map/pallas_call | solution.py:136
  12.4 4.0 %collective-permute-start.2 = (bf16[80,384]{1,0:T(8,128)(2,1)S(1)}, bf16[80,384]{1,0:T(8,128)(2,1)S(1)}, u32[]{:S(2)}, u32[]{:S(2)}) collective-permute-start(bf16[80,384]{1,0:T(8,128)(2,1)S(1)} %get-tuple-element.15), channel_id=1, source_target_pairs={{0,12},{4,8},{8,4},{12,0},{16,28},{20,24},{24,20},{28,16},{1,13},{... | collective-permute-start | bytes 184328 | tf_op jit(solution)/shard_map/ppermute | solution.py:210
  16.4 0.4 %collective-permute-start.3 = (bf16[80,384]{1,0:T(8,128)(2,1)S(1)}, bf16[80,384]{1,0:T(8,128)(2,1)S(1)}, u32[]{:S(2)}, u32[]{:S(2)}) collective-permute-start(bf16[80,384]{1,0:T(8,128)(2,1)S(1)} %get-tuple-element.16), channel_id=1, source_target_pairs={{0,8},{4,12},{8,0},{12,4},{16,24},{20,28},{24,16},{28,20},{1,9},{5... | collective-permute-start | bytes 184328 | tf_op jit(solution)/shard_map/ppermute | solution.py:210
  16.9 0.2 collective-permute-start.4
  17.1 1.6 %collective-permute-done.2 = bf16[80,384]{1,0:T(8,128)(2,1)S(1)} collective-permute-done((bf16[80,384]{1,0:T(8,128)(2,1)S(1)}, bf16[80,384]{1,0:T(8,128)(2,1)S(1)}, u32[]{:S(2)}, u32[]{:S(2)}) %collective-permute-start.2) | collective-permute-done | bytes 61472 | tf_op jit(solution)/shard_map/ppermute | solution.py:210
  18.6 2.2 %collective-permute-done.3 = bf16[80,384]{1,0:T(8,128)(2,1)S(1)} collective-permute-done((bf16[80,384]{1,0:T(8,128)(2,1)S(1)}, bf16[80,384]{1,0:T(8,128)(2,1)S(1)}, u32[]{:S(2)}, u32[]{:S(2)}) %collective-permute-start.3) | collective-permute-done | bytes 61472 | tf_op jit(solution)/shard_map/ppermute | solution.py:210
  20.8 0.6 %collective-permute-done.4 = bf16[80,384]{1,0:T(8,128)(2,1)S(1)} collective-permute-done((bf16[80,384]{1,0:T(8,128)(2,1)S(1)}, bf16[80,384]{1,0:T(8,128)(2,1)S(1)}, u32[]{:S(2)}, u32[]{:S(2)}) %collective-permute-start.4) | collective-permute-done | bytes 61472 | tf_op jit(solution)/shard_map/ppermute | solution.py:210
  21.4 0.1 select_convert_fusion.1
  21.5 2.6 %collective-permute-start.5 = (bf16[72,384]{1,0:T(8,128)(2,1)S(1)}, bf16[72,384]{1,0:T(8,128)(2,1)S(1)}, u32[]{:S(2)}, u32[]{:S(2)}) collective-permute-start(bf16[72,384]{1,0:T(8,128)(2,1)S(1)} %fusion.2), channel_id=1, source_target_pairs={{0,16},{4,20},{8,24},{12,28},{16,0},{20,4},{24,8},{28,12},{1,17},{... | collective-permute-start | bytes 165896 | tf_op jit(solution)/shard_map/ppermute | solution.py:210
  24.2 3.7 %collective-permute-done.5 = bf16[72,384]{1,0:T(8,128)(2,1)S(1)} collective-permute-done((bf16[72,384]{1,0:T(8,128)(2,1)S(1)}, bf16[72,384]{1,0:T(8,128)(2,1)S(1)}, u32[]{:S(2)}, u32[]{:S(2)}) %collective-permute-start.5) | collective-permute-done | bytes 55328 | tf_op jit(solution)/shard_map/ppermute | solution.py:210
  27.8 0.1 select_select_fusion
  27.9 1.3 %collective-permute-start.8 = (bf16[72,384]{1,0:T(8,128)(2,1)S(1)}, bf16[72,384]{1,0:T(8,128)(2,1)S(1)}, u32[]{:S(2)}, u32[]{:S(2)}) collective-permute-start(bf16[72,384]{1,0:T(8,128)(2,1)S(1)} %get-tuple-element.19), channel_id=1, source_target_pairs={{0,12},{4,8},{8,4},{12,0},{16,28},{20,24},{24,20},{28,16},{1,13},{... | collective-permute-start | bytes 165896 | tf_op jit(solution)/shard_map/ppermute | solution.py:210
  29.2 1.4 %collective-permute-start.7 = (bf16[72,384]{1,0:T(8,128)(2,1)S(1)}, bf16[72,384]{1,0:T(8,128)(2,1)S(1)}, u32[]{:S(2)}, u32[]{:S(2)}) collective-permute-start(bf16[72,384]{1,0:T(8,128)(2,1)S(1)} %get-tuple-element.29), channel_id=1, source_target_pairs={{0,8},{4,12},{8,0},{12,4},{16,24},{20,28},{24,16},{28,20},{1,9},{5... | collective-permute-start | bytes 165896 | tf_op jit(solution)/shard_map/ppermute | solution.py:210
  30.7 0.9 %collective-permute-start.6 = (bf16[72,384]{1,0:T(8,128)(2,1)S(1)}, bf16[72,384]{1,0:T(8,128)(2,1)S(1)}, u32[]{:S(2)}, u32[]{:S(2)}) collective-permute-start(bf16[72,384]{1,0:T(8,128)(2,1)S(1)} %get-tuple-element.30), channel_id=1, source_target_pairs={{0,4},{4,0},{8,12},{12,8},{16,20},{20,16},{24,28},{28,24},{1,5},{5... | collective-permute-start | bytes 165896 | tf_op jit(solution)/shard_map/ppermute | solution.py:210
  31.6 1.5 %collective-permute-done.8.e3 = bf16[72,384]{1,0:T(8,128)(2,1)S(1)} collective-permute-done((bf16[72,384]{1,0:T(8,128)(2,1)S(1)}, bf16[72,384]{1,0:T(8,128)(2,1)S(1)}, u32[]{:S(2)}, u32[]{:S(2)}) %collective-permute-start.8) | collective-permute-done | bytes 55328 | tf_op jit(solution)/shard_map/ppermute | solution.py:210
  33.0 0.4 %collective-permute-done.7.e2 = bf16[72,384]{1,0:T(8,128)(2,1)S(1)} collective-permute-done((bf16[72,384]{1,0:T(8,128)(2,1)S(1)}, bf16[72,384]{1,0:T(8,128)(2,1)S(1)}, u32[]{:S(2)}, u32[]{:S(2)}) %collective-permute-start.7) | collective-permute-done | bytes 55328 | tf_op jit(solution)/shard_map/ppermute | solution.py:210
  33.5 1.4 %collective-permute-done.6.e1 = bf16[72,384]{1,0:T(8,128)(2,1)S(1)} collective-permute-done((bf16[72,384]{1,0:T(8,128)(2,1)S(1)}, bf16[72,384]{1,0:T(8,128)(2,1)S(1)}, u32[]{:S(2)}, u32[]{:S(2)}) %collective-permute-start.6) | collective-permute-done | bytes 55328 | tf_op jit(solution)/shard_map/ppermute | solution.py:210
  34.8 2.3 %shard_map.66 = f32[3,2,144,384]{3,2,1,0:T(8,128)} custom-call(s32[2]{0:T(128)S(1)} %pad_add_fusion.place, f32[3,144,384]{2,1,0:T(8,128)S(1)} %get-tuple-element.12.far_ref, f32[3,144,384]{2,1,0:T(8,128)S(1)} %get-tuple-element.14.near_ref, f32[3,384]{1,0:T(4,128)S(1)} %copy-done.6, bf16[72,384]{1,0:T(8,128)(2,1)S(1)} %get-tuple-element.31.e0, ...), custom_call_target="tpu_custom_call" | custom-call | flops 1000000 | bytes 4000000 | tf_op jit(solution)/shard_map/pallas_call | solution.py:136
  (5 shorter events, 0.2 us)
Async XLA Ops:
  0.0 3.1 %copy-start.2 = (bf16[3,2,144,384]{3,2,1,0:T(8,128)(2,1)S(1)}, bf16[3,2,144,384]{3,2,1,0:T(8,128)(2,1)}, u32[]{:S(2)}) copy-start(bf16[3,2,144,384]{3,2,1,0:T(8,128)(2,1)} %cells_ref.3) | copy-start | bytes 1990660
  0.0 3.1 %copy-start.6 = (f32[3,384]{1,0:T(4,128)S(1)}, f32[3,384]{1,0:T(4,128)}, u32[]{:S(2)}) copy-start(f32[3,384]{1,0:T(4,128)} %keep_ref.5) | copy-start | bytes 13828
  0.0 3.1 %copy-start.5 = (s32[4,3,2,144]{3,2,1,0:T(2,128)S(1)}, s32[4,3,2,144]{3,2,1,0:T(2,128)}, u32[]{:S(2)}) copy-start(s32[4,3,2,144]{3,2,1,0:T(2,128)} %mask_ref.3) | copy-start | bytes 41476
  0.0 3.1 %copy-start.4 = (bf16[3,2,144,384]{3,2,1,0:T(8,128)(2,1)S(1)}, bf16[3,2,144,384]{3,2,1,0:T(8,128)(2,1)}, u32[]{:S(2)}) copy-start(bf16[3,2,144,384]{3,2,1,0:T(8,128)(2,1)} %forcing_ref.1) | copy-start | bytes 1990660
  1.3 1.8 %collective-permute-start = (bf16[3,144,384]{2,1,0:T(8,128)(2,1)S(1)}, bf16[3,144,384]{2,1,0:T(8,128)(2,1)S(1)}, u32[]{:S(2)}, u32[]{:S(2)}) collective-permute-start(bf16[3,144,384]{2,1,0:T(8,128)(2,1)S(1)} %get-tuple-element.24), channel_id=1, source_target_pairs={{0,1},{1,0},{2,3},{3,2},{4,5},{5,4},{6,7},{7,6},{8,9},{9,8},{10,11... | collective-permute-start | bytes 995336 | tf_op jit(solution)/shard_map/ppermute | solution.py:156
  1.8 8.0 %collective-permute-start.1 = (bf16[3,144,384]{2,1,0:T(8,128)(2,1)S(1)}, bf16[3,144,384]{2,1,0:T(8,128)(2,1)S(1)}, u32[]{:S(2)}, u32[]{:S(2)}) collective-permute-start(bf16[3,144,384]{2,1,0:T(8,128)(2,1)S(1)} %get-tuple-element.23), channel_id=1, source_target_pairs={{1,2},{2,1},{5,6},{6,5},{9,10},{10,9},{13,14},{14,13},{17,18},{18,... | collective-permute-start | bytes 995336 | tf_op jit(solution)/shard_map/ppermute | solution.py:158
  3.1 1.5 %copy-start = (bf16[3,2,384,384]{3,2,1,0:T(8,128)(2,1)S(1)}, bf16[3,2,384,384]{3,2,1,0:T(8,128)(2,1)}, u32[]{:S(2)}) copy-start(bf16[3,2,384,384]{3,2,1,0:T(8,128)(2,1)} %inverse_ref.3) | copy-start | bytes 5308420
  4.6 1.3 %copy-start.3 = (bf16[4,384,384]{2,1,0:T(8,128)(2,1)S(1)}, bf16[4,384,384]{2,1,0:T(8,128)(2,1)}, u32[]{:S(2)}) copy-start(bf16[4,384,384]{2,1,0:T(8,128)(2,1)} %lift_ref.3) | copy-start | bytes 3538948
  5.8 4.0 %copy-start.1 = (bf16[3,2,384,384]{3,2,1,0:T(8,128)(2,1)S(1)}, bf16[3,2,384,384]{3,2,1,0:T(8,128)(2,1)}, u32[]{:S(2)}) copy-start(bf16[3,2,384,384]{3,2,1,0:T(8,128)(2,1)} %inverse_ref.3) | copy-start | bytes 5308420
  12.4 6.2 %collective-permute-start.2 = (bf16[80,384]{1,0:T(8,128)(2,1)S(1)}, bf16[80,384]{1,0:T(8,128)(2,1)S(1)}, u32[]{:S(2)}, u32[]{:S(2)}) collective-permute-start(bf16[80,384]{1,0:T(8,128)(2,1)S(1)} %get-tuple-element.15), channel_id=1, source_target_pairs={{0,12},{4,8},{8,4},{12,0},{16,28},{20,24},{24,20},{28,16},{1,13},{... | collective-permute-start | bytes 184328 | tf_op jit(solution)/shard_map/ppermute | solution.py:210
  16.4 4.4 %collective-permute-start.3 = (bf16[80,384]{1,0:T(8,128)(2,1)S(1)}, bf16[80,384]{1,0:T(8,128)(2,1)S(1)}, u32[]{:S(2)}, u32[]{:S(2)}) collective-permute-start(bf16[80,384]{1,0:T(8,128)(2,1)S(1)} %get-tuple-element.16), channel_id=1, source_target_pairs={{0,8},{4,12},{8,0},{12,4},{16,24},{20,28},{24,16},{28,20},{1,9},{5... | collective-permute-start | bytes 184328 | tf_op jit(solution)/shard_map/ppermute | solution.py:210
  16.9 4.5 %collective-permute-start.4 = (bf16[80,384]{1,0:T(8,128)(2,1)S(1)}, bf16[80,384]{1,0:T(8,128)(2,1)S(1)}, u32[]{:S(2)}, u32[]{:S(2)}) collective-permute-start(bf16[80,384]{1,0:T(8,128)(2,1)S(1)} %get-tuple-element.17), channel_id=1, source_target_pairs={{0,4},{4,0},{8,12},{12,8},{16,20},{20,16},{24,28},{28,24},{1,5},{5... | collective-permute-start | bytes 184328 | tf_op jit(solution)/shard_map/ppermute | solution.py:210
  21.5 6.3 %collective-permute-start.5 = (bf16[72,384]{1,0:T(8,128)(2,1)S(1)}, bf16[72,384]{1,0:T(8,128)(2,1)S(1)}, u32[]{:S(2)}, u32[]{:S(2)}) collective-permute-start(bf16[72,384]{1,0:T(8,128)(2,1)S(1)} %fusion.2), channel_id=1, source_target_pairs={{0,16},{4,20},{8,24},{12,28},{16,0},{20,4},{24,8},{28,12},{1,17},{... | collective-permute-start | bytes 165896 | tf_op jit(solution)/shard_map/ppermute | solution.py:210
  27.9 5.1 %collective-permute-start.8 = (bf16[72,384]{1,0:T(8,128)(2,1)S(1)}, bf16[72,384]{1,0:T(8,128)(2,1)S(1)}, u32[]{:S(2)}, u32[]{:S(2)}) collective-permute-start(bf16[72,384]{1,0:T(8,128)(2,1)S(1)} %get-tuple-element.19), channel_id=1, source_target_pairs={{0,12},{4,8},{8,4},{12,0},{16,28},{20,24},{24,20},{28,16},{1,13},{... | collective-permute-start | bytes 165896 | tf_op jit(solution)/shard_map/ppermute | solution.py:210
  29.2 4.2 %collective-permute-start.7 = (bf16[72,384]{1,0:T(8,128)(2,1)S(1)}, bf16[72,384]{1,0:T(8,128)(2,1)S(1)}, u32[]{:S(2)}, u32[]{:S(2)}) collective-permute-start(bf16[72,384]{1,0:T(8,128)(2,1)S(1)} %get-tuple-element.29), channel_id=1, source_target_pairs={{0,8},{4,12},{8,0},{12,4},{16,24},{20,28},{24,16},{28,20},{1,9},{5... | collective-permute-start | bytes 165896 | tf_op jit(solution)/shard_map/ppermute | solution.py:210
  30.7 4.2 %collective-permute-start.6 = (bf16[72,384]{1,0:T(8,128)(2,1)S(1)}, bf16[72,384]{1,0:T(8,128)(2,1)S(1)}, u32[]{:S(2)}, u32[]{:S(2)}) collective-permute-start(bf16[72,384]{1,0:T(8,128)(2,1)S(1)} %get-tuple-element.30), channel_id=1, source_target_pairs={{0,4},{4,0},{8,12},{12,8},{16,20},{20,16},{24,28},{28,24},{1,5},{5... | collective-permute-start | bytes 165896 | tf_op jit(solution)/shard_map/ppermute | solution.py:210

commit v2 on v1

v2 whole, which is shorter than its diff:
```python
import functools

import jax
import jax.numpy as jnp
from jax import lax
from jax.experimental import pallas as pl
from jax.experimental.pallas import tpu as pltpu
from jax.sharding import PartitionSpec as P

GROUP = 4
F32, BF16 = jnp.float32, jnp.bfloat16
VMEM_LIMIT = 24 * 1024 * 1024
MASK_COST = 10_000_000_000


def masked_jump(mask, neighbour, center):
    return (mask * (neighbour - center)).astype(BF16)


def along_b(cells):
    rows = lax.broadcasted_iota(jnp.int32, cells.shape, 0)
    last = cells.shape[0] - 1
    lower = jnp.where(rows == 0, 0.0, pltpu.roll(cells, 1, 0))
    upper = jnp.where(rows == last, 0.0, pltpu.roll(cells, last, 0))
    return lower, upper


def mask_columns(mask_ref, layer):
    rows = [mask_ref[face, layer, a : a + 1, :] for face in range(4) for a in range(2)]
    rows.append(jnp.zeros((120, rows[0].shape[1]), rows[0].dtype))
    return jnp.concatenate(rows, axis=0).astype(F32).T


def dot(a, b):
    return jnp.dot(a, b, preferred_element_type=F32)


def mask_kernel(place, mask_ref, after, columns_ref):
    for l in range(columns_ref.shape[0]):
        columns_ref[l] = mask_columns(mask_ref, l)


def inner_kernel(place, columns_ref, halo_ref, keep_ref, near_row, far_row, forcing, lift, inverse, far_ref, source_ref):
    layers, width, dofs = near_row.shape
    odd = place[0]
    near_at, far_at = odd, 1 - odd
    is_odd = odd == 1
    carry = None
    for l in range(layers):
        columns = columns_ref[l]
        column = lambda face, even, other: jnp.where(
            is_odd, columns[:, 2 * face[1] + other : 2 * face[1] + other + 1], columns[:, 2 * face[0] + even : 2 * face[0] + even + 1]
        )
        near, far = near_row[l].astype(F32), far_row[l].astype(F32)
        near_low, near_up = along_b(near)
        far_low, far_up = along_b(far)
        halo = halo_ref[l].astype(F32)
        far_source = forcing[l, far_at].astype(F32)
        near_source = forcing[l, near_at].astype(F32)
        pairs = (
            (masked_jump(column((1, 0), 1, 0), halo, far), masked_jump(column((1, 0), 0, 1), far, near), lift[1 - odd]),
            (masked_jump(column((2, 2), 1, 0), far_low, far), masked_jump(column((2, 2), 0, 1), near_low, near), lift[2]),
            (masked_jump(column((3, 3), 1, 0), far_up, far), masked_jump(column((3, 3), 0, 1), near_up, near), lift[3]),
        )
        lifted = sum(dot(jnp.concatenate(pair[:2], axis=0), pair[2]) for pair in pairs)
        inner = masked_jump(column((0, 1), 1, 0), near, far)
        far_source = far_source + lifted[:width] + dot(inner, lift[odd])
        source_ref[l] = near_source + lifted[width:]
        solved = dot(far_source.astype(BF16), inverse[l, far_at])
        carry = solved if l == 0 else keep_ref[l : l + 1, :] * carry + solved
        far_ref[l] = carry


def outer_kernel(place, halo_ref, columns_ref, near_row, source_ref, lift, inverse, keep_ref, far_ref, near_ref, p0, p1, p2, p3, carry):
    layers, width, dofs = near_row.shape
    odd = place[0]
    inside = place[2] == 0
    jumps = []
    for l in range(layers):
        edge = jnp.where(odd == 1, columns_ref[l, :, 3:4], columns_ref[l, :, 0:1])
        halo = jnp.where(inside, halo_ref[l].astype(F32), 0.0)
        jumps.append(masked_jump(edge, halo, near_row[l].astype(F32)))
    lifted = dot(jnp.concatenate(jumps, axis=0), lift[odd])
    total = None
    for l in range(layers):
        source = source_ref[l] + lifted[l * width : (l + 1) * width]
        solved = dot(source.astype(BF16), inverse[l, odd])
        total = solved if l == 0 else keep_ref[l : l + 1, :] * total + solved
        near_ref[l] = total
    carry[pl.ds(0, width), :] = far_ref[layers - 1]
    carry[pl.ds(width, width), :] = total
    factor = keep_ref[0:1, :]
    for l in range(1, layers):
        factor = factor * keep_ref[l : l + 1, :]
    high = factor.astype(BF16).astype(F32)
    low = factor - high
    at = lax.broadcasted_iota(jnp.int32, (8, dofs), 0)
    extra = jnp.where(at == 0, high, jnp.where(at == 1, low, 0.0))
    piece = 2 * width // GROUP
    for k, out in enumerate((p0, p1, p2, p3)):
        start = pl.multiple_of((place[1] ^ k) * piece, 8)
        out[...] = jnp.concatenate([carry[pl.ds(start, piece), :], extra], axis=0).astype(BF16)


def final_kernel(place, far_ref, near_ref, keep_ref, e0, e1, e2, e3, out_hbm, incoming, out, sem):
    layers, width, dofs = far_ref.shape
    odd = place[0]
    piece = e0.shape[0]
    for k, part in enumerate((e0, e1, e2, e3)):
        start = pl.multiple_of((place[1] ^ k) * piece, 8)
        incoming[pl.ds(start, piece), :] = part[...].astype(F32)
    copies = []
    factor = None
    for l in range(layers):
        factor = keep_ref[l : l + 1, :] if l == 0 else factor * keep_ref[l : l + 1, :]
        out[l, 1 - odd] = far_ref[l] + factor * incoming[pl.ds(0, width), :]
        out[l, odd] = near_ref[l] + factor * incoming[pl.ds(width, width), :]
        copies.append(pltpu.make_async_copy(out.at[l], out_hbm.at[l], sem.at[l]))
        copies[-1].start()
    for copy in copies:
        copy.wait()


def call(kernel, place, operands, in_specs, outs, out_specs, scratch, flops, moved):
    return pl.pallas_call(
        kernel,
        out_shape=outs,
        in_specs=[pl.BlockSpec(memory_space=pltpu.SMEM)] + in_specs,
        out_specs=out_specs,
        scratch_shapes=scratch,
        compiler_params=pltpu.CompilerParams(vmem_limit_bytes=VMEM_LIMIT),
        cost_estimate=pl.CostEstimate(flops=flops, bytes_accessed=moved, transcendentals=0),
    )(place, *operands)


def body(forcing, cells, face_mask, lifting, inverse, retention):
    layers, _, width, dofs = cells.shape
    crosses, streams = lax.axis_size("cross"), lax.axis_size("stream")
    cross, stream = lax.axis_index("cross"), lax.axis_index("stream")
    odd, member = cross % 2, stream % GROUP
    at_end = (cross == 0) | (cross == crosses - 1)
    place = jnp.stack([odd, member, at_end.astype(jnp.int32)]).astype(jnp.int32)

    links = []
    for s in range(streams):
        for c in range(crosses):
            other = (s ^ 1, c) if c in (0, crosses - 1) else (s, c + 1 if c % 2 else c - 1)
            links.append((s * crosses + c, other[0] * crosses + other[1]))
    vmem, hbm = pl.BlockSpec(memory_space=pltpu.VMEM), pl.BlockSpec(memory_space=pl.ANY)
    like = jax.ShapeDtypeStruct
    stack = like((layers, width, dofs), F32)
    slab = like((layers, width, dofs), BF16)
    unit = 2 * layers * width * dofs * dofs

    near_row = lax.dynamic_index_in_dim(cells, odd, 1, False)
    far_row = lax.dynamic_index_in_dim(cells, 1 - odd, 1, False)
    core_halo = lax.ppermute(far_row, "cross", [(i, i ^ 1) for i in range(crosses)])
    chip_halo = lax.ppermute(near_row, ("stream", "cross"), links)
    columns = call(
        mask_kernel, place, (face_mask, near_row), [vmem, hbm], like((layers, width, 128), F32), vmem, [], MASK_COST, 20_000_000
    )
    far, near_source = call(
        inner_kernel,
        place,
        (columns, core_halo, retention, near_row, far_row, forcing, lifting, inverse),
        [vmem] * 8,
        (stack, stack),
        (vmem,) * 2,
        [],
        9 * unit,
        5_000_000,
    )

    piece = 2 * width // GROUP
    near, *pieces = call(
        outer_kernel,
        place,
        (chip_halo, columns, near_row, near_source, lifting, inverse, retention, far),
        [vmem] * 8,
        (stack,) + (like((piece + 8, dofs), BF16),) * GROUP,
        (vmem,) * (1 + GROUP),
        [pltpu.VMEM((2 * width, dofs), F32)],
        2 * unit,
        3_000_000,
    )

    def swap(part, distance):
        return lax.ppermute(part, "stream", [(i, i ^ distance) for i in range(streams)])

    got = [pieces[0]] + [swap(pieces[k], k) for k in range(1, GROUP)]
    pick = lambda parts, j: functools.reduce(
        lambda rest, k: jnp.where((member ^ k) == j, parts[k], rest), range(1, GROUP), parts[0]
    )
    ordered = [pick(got, j).astype(F32) for j in range(GROUP)]
    values = [part[:piece] for part in ordered]
    factors = [part[piece : piece + 1] + part[piece + 1 : piece + 2] for part in ordered]

    total, total_factor = values[0], factors[0]
    for j in range(1, GROUP):
        total = factors[j] * total + values[j]
        total_factor = total_factor * factors[j]
    before, before_factor = jnp.zeros_like(total), jnp.ones_like(total_factor)
    distance = GROUP
    while distance < streams:
        last = 2 * distance >= streams
        if last:
            met = swap(total.astype(BF16), distance).astype(F32)
        else:
            high = total_factor.astype(BF16)
            low = (total_factor - high.astype(F32)).astype(BF16)
            met = swap(jnp.concatenate([total.astype(BF16), high, low], axis=0), distance).astype(F32)
        later = (stream & distance) != 0
        before = jnp.where(later, before_factor * met[:piece] + before, before)
        if not last:
            met_factor = met[piece : piece + 1] + met[piece + 1 : piece + 2]
            before_factor = jnp.where(later, before_factor * met_factor, before_factor)
            total = jnp.where(later, total_factor * met[:piece] + total, met_factor * total + met[:piece])
            total_factor = total_factor * met_factor
        distance *= 2

    entering = [before]
    for j in range(GROUP - 1):
        entering.append(factors[j] * entering[j] + values[j])
    entering = [part.astype(BF16) for part in entering]
    give = [pick(entering, k) for k in range(GROUP)]
    back = [give[0]] + [swap(give[k], k) for k in range(1, GROUP)]

    return call(
        final_kernel,
        place,
        (far, near, retention, *back),
        [vmem] * (3 + GROUP),
        like(cells.shape, F32),
        hbm,
        [pltpu.VMEM((2 * width, dofs), F32), pltpu.VMEM(cells.shape, F32), pltpu.SemaphoreType.DMA((layers,))],
        1_000_000,
        4_000_000,
    )


def solution(mesh):
    return jax.shard_map(
        body,
        mesh=mesh,
        in_specs=(
            P("stream", "cross", None, None),
            P("stream", "cross", None, None),
            P(None, "stream", "cross", None),
            P(),
            P("stream", "cross", None, None),
            P("stream", None),
        ),
        out_specs=P("stream", "cross", None, None),
        check_vma=False,
    )
```

time: 37.3 us -> 33 us (0.88)
  Pallas kernels: 8.88 us -> 6.99 us
  waiting for transfers between devices: 11.7 us -> 10.2 us
  other arithmetic: 1.58 us -> 0.34 us
  starting transfers between devices: 12.1 us -> 12.9 us
    ppermute x2, starting transfers between devices: 1.21 us -> 3.11 us  [the longest x1 2.59 us: body(): chip_halo = lax.ppermute(near_row, ('stream', 'cross'), links)]
    pallas_call x3 -> x4, Pallas kernels: 8.88 us -> 6.99 us  [call(): pl.pallas_call(kernel, out_shape=outs, in_specs=[pl.BlockSpec(memory_spac...]
    unnamed x14 -> x10, local copies, waits for them, and re-layouts: 2.76 us -> 1.28 us
    select_n x1 -> x0, other arithmetic: 1.25 us -> none  [body(): across = jnp.where(odd == 1, cells[:, 1], cells[:, 0])]
    squeeze x0 -> x1, local copies, waits for them, and re-layouts: none -> 1.15 us  [body(): far_row = lax.dynamic_index_in_dim(cells, 1 - odd, 1, False)]
    ppermute x7, starting transfers between devices: 10.9 us -> 9.77 us  [swap(): lax.ppermute(part, 'stream', [(i, i ^ distance) for i in range(streams)])]
    ppermute x7, waiting for transfers between devices: 11.2 us -> 10.2 us  [swap(): lax.ppermute(part, 'stream', [(i, i ^ distance) for i in range(streams)])]
    ppermute x2, waiting for transfers between devices: 0.5 us -> 0.01 us  [the longest x1 0.01 us: body(): lax.ppermute(far_row, 'cross', [(i, i ^ 1) for i in range(crosses)])]
  transfers between devices with their start and end apart: 9 -> 9, of which waited for: 8 -> 7; matrix products, arithmetic and copies ran while one was open for 0% -> 0% of each run, Pallas kernels for 11% -> 12%
where the time goes in v2:
time: 33 us; the launch traced here: 32.9 us
  starting transfers between devices  12.9 us (39%)
  waiting for transfers between devices  10.2 us (31%)
  Pallas kernels  6.99 us (21%)
  local copies, waits for them, and re-layouts  2.43 us (7%)
  other arithmetic  0.34 us (1%)
    ppermute x7, waiting for transfers between devices, swap(): lax.ppermute(part, 'stream', [(i, i ^ distance) for i in range(streams)])  10.2 us
    ppermute x7, starting transfers between devices, swap(): lax.ppermute(part, 'stream', [(i, i ^ distance) for i in range(streams)])  9.77 us
    pallas_call x4, Pallas kernels, call(): pl.pallas_call(kernel, out_shape=outs, in_specs=[pl.BlockSpec(memory_spac...  6.99 us
    ppermute x1, starting transfers between devices, body(): chip_halo = lax.ppermute(near_row, ('stream', 'cross'), links)  2.59 us
    unnamed x10, local copies, waits for them, and re-layouts  1.28 us
    squeeze x1, local copies, waits for them, and re-layouts, body(): far_row = lax.dynamic_index_in_dim(cells, 1 - odd, 1, False)  1.15 us
  transfers between devices with their start and end apart: 9, of which 7 were waited for; matrix products, arithmetic and copies ran while one was open for 0% of the time, Pallas kernels for 12%

profile of v2, /device:TPU:0, one launch (start us, length us, event | category | flops | bytes accessed | tf_op | source)
XLA Modules:
  0.0 32.9 jit_solution(4555052051988767388)
XLA Ops:
  0.0 0.0 copy-start.4
  0.0 1.1 %dynamic-slice_bitcast_fusion = (bf16[3,144,384]{2,1,0:T(8,128)(2,1)S(1)}, bf16[3,144,384]{2,1,0:T(8,128)(2,1)S(1)}) fusion(bf16[3,2,144,384]{3,2,1,0:T(8,128)(2,1)} %param.7, s32[]{:T(128)S(6)} %select_n.177, s32[]{:T(128)S(6)} %select_n.176), kind=kLoop, calls=%fused_computation | loop fusion | bytes 1327112 | tf_op jit(solution)/shard_map/jit(dynamic_index_in_dim)/squeeze | solution.py:156
  1.2 0.5 %collective-permute-start = (bf16[3,144,384]{2,1,0:T(8,128)(2,1)S(1)}, bf16[3,144,384]{2,1,0:T(8,128)(2,1)S(1)}, u32[]{:S(2)}, u32[]{:S(2)}) collective-permute-start(bf16[3,144,384]{2,1,0:T(8,128)(2,1)S(1)} %get-tuple-element.23.far_row), channel_id=1, source_target_pairs={{0,1},{1,0},{2,3},{3,2},{4,5},{5,4},{6,7},{7,6},{8,9},{9,8},{10,11... | collective-permute-start | bytes 995336 | tf_op jit(solution)/shard_map/ppermute | solution.py:157
  1.7 2.6 %collective-permute-start.1 = (bf16[3,144,384]{2,1,0:T(8,128)(2,1)S(1)}, bf16[3,144,384]{2,1,0:T(8,128)(2,1)S(1)}, u32[]{:S(2)}, u32[]{:S(2)}) collective-permute-start(bf16[3,144,384]{2,1,0:T(8,128)(2,1)S(1)} %get-tuple-element.24.after.near_row), channel_id=1, source_target_pairs={{0,4},{1,2},{2,1},{3,7},{4,0},{5,6},{6,5},{7,3},{8,12},{9,10},{10,... | collective-permute-start | bytes 995336 | tf_op jit(solution)/shard_map/ppermute | solution.py:158
  4.3 0.1 pad_add_fusion.place
  4.3 0.0 copy-done.4
  4.3 0.0 copy-start
  4.3 0.0 copy-start.1
  4.3 0.0 copy-start.2
  4.4 0.0 copy-start.3
  4.4 0.7 %shard_map.64.columns_ref = f32[3,144,128]{2,1,0:T(8,128)S(1)} custom-call(s32[3]{0:T(128)S(1)} %pad_add_fusion.place, s32[4,3,2,144]{3,2,1,0:T(2,128)S(1)} %copy-done.4, bf16[3,144,384]{2,1,0:T(8,128)(2,1)S(1)} %get-tuple-element.24.after.near_row), custom_call_target="tpu_custom_call" | custom-call | flops 10000000000 | bytes 20000000 | tf_op jit(solution)/shard_map/pallas_call | solution.py:125
  5.0 0.0 collective-permute-done.halo_ref
  5.1 0.8 %copy-done = bf16[3,2,384,384]{3,2,1,0:T(8,128)(2,1)S(1)} copy-done((bf16[3,2,384,384]{3,2,1,0:T(8,128)(2,1)S(1)}, bf16[3,2,384,384]{3,2,1,0:T(8,128)(2,1)}, u32[]{:S(2)}) %copy-start) | copy-done | bytes 1769496
  5.8 0.3 copy-done.1
  6.2 0.2 copy-done.2
  6.3 0.0 copy-done.3
  6.3 3.2 %shard_map.65 = (f32[3,144,384]{2,1,0:T(8,128)S(1)}, f32[3,144,384]{2,1,0:T(8,128)S(1)}) custom-call(s32[3]{0:T(128)S(1)} %pad_add_fusion.place, f32[3,144,128]{2,1,0:T(8,128)S(1)} %shard_map.64.columns_ref, bf16[3,144,384]{2,1,0:T(8,128)(2,1)S(1)} %collective-permute-done.halo_ref, f32[3,384]{1,0:T(4,128)S(1)} %copy-done.3, ...), custom_call_target="tpu_custom_call" | custom-call | flops 1146617856 | bytes 5000000 | tf_op jit(solution)/shard_map/pallas_call | solution.py:125
  9.5 0.0 collective-permute-done.1.halo_ref
  9.5 1.4 %shard_map.66 = (f32[3,144,384]{2,1,0:T(8,128)S(1)}, bf16[80,384]{1,0:T(8,128)(2,1)S(1)}, bf16[80,384]{1,0:T(8,128)(2,1)S(1)}, bf16[80,384]{1,0:T(8,128)(2,1)S(1)}, bf16[80,384]{1,0:T(8,128)(2,1)S(1)}) custom-call(s32[3]{0:T(128)S(1)} %pad_add_fusion.place, bf16[3,144,384]{2,1,0:T(8,128)(2,1)S(1)} %collective-permute-done.1.halo_ref, ...), custom_call_target="tpu_custom_call" | custom-call | flops 254803968 | bytes 3000000 | tf_op jit(solution)/shard_map/pallas_call | solution.py:125
  10.9 2.9 %collective-permute-start.2 = (bf16[80,384]{1,0:T(8,128)(2,1)S(1)}, bf16[80,384]{1,0:T(8,128)(2,1)S(1)}, u32[]{:S(2)}, u32[]{:S(2)}) collective-permute-start(bf16[80,384]{1,0:T(8,128)(2,1)S(1)} %get-tuple-element.15), channel_id=1, source_target_pairs={{0,12},{4,8},{8,4},{12,0},{16,28},{20,24},{24,20},{28,16},{1,13},{... | collective-permute-start | bytes 184328 | tf_op jit(solution)/shard_map/ppermute | solution.py:188
  13.9 0.5 %collective-permute-start.3 = (bf16[80,384]{1,0:T(8,128)(2,1)S(1)}, bf16[80,384]{1,0:T(8,128)(2,1)S(1)}, u32[]{:S(2)}, u32[]{:S(2)}) collective-permute-start(bf16[80,384]{1,0:T(8,128)(2,1)S(1)} %get-tuple-element.16), channel_id=1, source_target_pairs={{0,8},{4,12},{8,0},{12,4},{16,24},{20,28},{24,16},{28,20},{1,9},{5... | collective-permute-start | bytes 184328 | tf_op jit(solution)/shard_map/ppermute | solution.py:188
  14.3 0.2 collective-permute-start.4
  14.5 1.6 %collective-permute-done.2 = bf16[80,384]{1,0:T(8,128)(2,1)S(1)} collective-permute-done((bf16[80,384]{1,0:T(8,128)(2,1)S(1)}, bf16[80,384]{1,0:T(8,128)(2,1)S(1)}, u32[]{:S(2)}, u32[]{:S(2)}) %collective-permute-start.2) | collective-permute-done | bytes 61472 | tf_op jit(solution)/shard_map/ppermute | solution.py:188
  16.2 1.9 %collective-permute-done.3 = bf16[80,384]{1,0:T(8,128)(2,1)S(1)} collective-permute-done((bf16[80,384]{1,0:T(8,128)(2,1)S(1)}, bf16[80,384]{1,0:T(8,128)(2,1)S(1)}, u32[]{:S(2)}, u32[]{:S(2)}) %collective-permute-start.3) | collective-permute-done | bytes 61472 | tf_op jit(solution)/shard_map/ppermute | solution.py:188
  18.1 0.5 %collective-permute-done.4 = bf16[80,384]{1,0:T(8,128)(2,1)S(1)} collective-permute-done((bf16[80,384]{1,0:T(8,128)(2,1)S(1)}, bf16[80,384]{1,0:T(8,128)(2,1)S(1)}, u32[]{:S(2)}, u32[]{:S(2)}) %collective-permute-start.4) | collective-permute-done | bytes 61472 | tf_op jit(solution)/shard_map/ppermute | solution.py:188
  18.5 0.1 select_convert_fusion.1
  18.7 2.7 %collective-permute-start.5 = (bf16[72,384]{1,0:T(8,128)(2,1)S(1)}, bf16[72,384]{1,0:T(8,128)(2,1)S(1)}, u32[]{:S(2)}, u32[]{:S(2)}) collective-permute-start(bf16[72,384]{1,0:T(8,128)(2,1)S(1)} %fusion), channel_id=1, source_target_pairs={{0,16},{4,20},{8,24},{12,28},{16,0},{20,4},{24,8},{28,12},{1,17},{... | collective-permute-start | bytes 165896 | tf_op jit(solution)/shard_map/ppermute | solution.py:188
  21.4 2.4 %collective-permute-done.5 = bf16[72,384]{1,0:T(8,128)(2,1)S(1)} collective-permute-done((bf16[72,384]{1,0:T(8,128)(2,1)S(1)}, bf16[72,384]{1,0:T(8,128)(2,1)S(1)}, u32[]{:S(2)}, u32[]{:S(2)}) %collective-permute-start.5) | collective-permute-done | bytes 55328 | tf_op jit(solution)/shard_map/ppermute | solution.py:188
  23.8 0.1 select_select_fusion
  23.9 0.6 %collective-permute-start.6 = (bf16[72,384]{1,0:T(8,128)(2,1)S(1)}, bf16[72,384]{1,0:T(8,128)(2,1)S(1)}, u32[]{:S(2)}, u32[]{:S(2)}) collective-permute-start(bf16[72,384]{1,0:T(8,128)(2,1)S(1)} %get-tuple-element.30), channel_id=1, source_target_pairs={{0,4},{4,0},{8,12},{12,8},{16,20},{20,16},{24,28},{28,24},{1,5},{5... | collective-permute-start | bytes 165896 | tf_op jit(solution)/shard_map/ppermute | solution.py:188
  24.5 1.6 %collective-permute-start.7 = (bf16[72,384]{1,0:T(8,128)(2,1)S(1)}, bf16[72,384]{1,0:T(8,128)(2,1)S(1)}, u32[]{:S(2)}, u32[]{:S(2)}) collective-permute-start(bf16[72,384]{1,0:T(8,128)(2,1)S(1)} %get-tuple-element.29), channel_id=1, source_target_pairs={{0,8},{4,12},{8,0},{12,4},{16,24},{20,28},{24,16},{28,20},{1,9},{5... | collective-permute-start | bytes 165896 | tf_op jit(solution)/shard_map/ppermute | solution.py:188
  26.1 1.4 %collective-permute-start.8 = (bf16[72,384]{1,0:T(8,128)(2,1)S(1)}, bf16[72,384]{1,0:T(8,128)(2,1)S(1)}, u32[]{:S(2)}, u32[]{:S(2)}) collective-permute-start(bf16[72,384]{1,0:T(8,128)(2,1)S(1)} %get-tuple-element.19), channel_id=1, source_target_pairs={{0,12},{4,8},{8,4},{12,0},{16,28},{20,24},{24,20},{28,16},{1,13},{... | collective-permute-start | bytes 165896 | tf_op jit(solution)/shard_map/ppermute | solution.py:188
  27.5 1.0 %collective-permute-done.6.e1 = bf16[72,384]{1,0:T(8,128)(2,1)S(1)} collective-permute-done((bf16[72,384]{1,0:T(8,128)(2,1)S(1)}, bf16[72,384]{1,0:T(8,128)(2,1)S(1)}, u32[]{:S(2)}, u32[]{:S(2)}) %collective-permute-start.6) | collective-permute-done | bytes 55328 | tf_op jit(solution)/shard_map/ppermute | solution.py:188
  28.5 0.2 collective-permute-done.7.e2
  28.7 2.5 %collective-permute-done.8.e3 = bf16[72,384]{1,0:T(8,128)(2,1)S(1)} collective-permute-done((bf16[72,384]{1,0:T(8,128)(2,1)S(1)}, bf16[72,384]{1,0:T(8,128)(2,1)S(1)}, u32[]{:S(2)}, u32[]{:S(2)}) %collective-permute-start.8) | collective-permute-done | bytes 55328 | tf_op jit(solution)/shard_map/ppermute | solution.py:188
  31.2 1.7 %shard_map.67 = f32[3,2,144,384]{3,2,1,0:T(8,128)} custom-call(s32[3]{0:T(128)S(1)} %pad_add_fusion.place, f32[3,144,384]{2,1,0:T(8,128)S(1)} %get-tuple-element.12.far_ref, f32[3,144,384]{2,1,0:T(8,128)S(1)} %get-tuple-element.14.near_ref, f32[3,384]{1,0:T(4,128)S(1)} %copy-done.3, bf16[72,384]{1,0:T(8,128)(2,1)S(1)} %get-tuple-element.31.e0, ...), custom_call_target="tpu_custom_call" | custom-call | flops 1000000 | bytes 4000000 | tf_op jit(solution)/shard_map/pallas_call | solution.py:125
  (5 shorter events, 0.2 us)
Async XLA Ops:
  0.0 4.3 %copy-start.4 = (s32[4,3,2,144]{3,2,1,0:T(2,128)S(1)}, s32[4,3,2,144]{3,2,1,0:T(2,128)}, u32[]{:S(2)}) copy-start(s32[4,3,2,144]{3,2,1,0:T(2,128)} %mask_ref.1) | copy-start | bytes 41476
  1.2 3.9 %collective-permute-start = (bf16[3,144,384]{2,1,0:T(8,128)(2,1)S(1)}, bf16[3,144,384]{2,1,0:T(8,128)(2,1)S(1)}, u32[]{:S(2)}, u32[]{:S(2)}) collective-permute-start(bf16[3,144,384]{2,1,0:T(8,128)(2,1)S(1)} %get-tuple-element.23.far_row), channel_id=1, source_target_pairs={{0,1},{1,0},{2,3},{3,2},{4,5},{5,4},{6,7},{7,6},{8,9},{9,8},{10,11... | collective-permute-start | bytes 995336 | tf_op jit(solution)/shard_map/ppermute | solution.py:157
  1.7 7.9 %collective-permute-start.1 = (bf16[3,144,384]{2,1,0:T(8,128)(2,1)S(1)}, bf16[3,144,384]{2,1,0:T(8,128)(2,1)S(1)}, u32[]{:S(2)}, u32[]{:S(2)}) collective-permute-start(bf16[3,144,384]{2,1,0:T(8,128)(2,1)S(1)} %get-tuple-element.24.after.near_row), channel_id=1, source_target_pairs={{0,4},{1,2},{2,1},{3,7},{4,0},{5,6},{6,5},{7,3},{8,12},{9,10},{10,... | collective-permute-start | bytes 995336 | tf_op jit(solution)/shard_map/ppermute | solution.py:158
  4.3 1.5 %copy-start = (bf16[3,2,384,384]{3,2,1,0:T(8,128)(2,1)S(1)}, bf16[3,2,384,384]{3,2,1,0:T(8,128)(2,1)}, u32[]{:S(2)}) copy-start(bf16[3,2,384,384]{3,2,1,0:T(8,128)(2,1)} %inverse.3) | copy-start | bytes 5308420
  4.3 1.8 %copy-start.1 = (bf16[4,384,384]{2,1,0:T(8,128)(2,1)S(1)}, bf16[4,384,384]{2,1,0:T(8,128)(2,1)}, u32[]{:S(2)}) copy-start(bf16[4,384,384]{2,1,0:T(8,128)(2,1)} %lift.3) | copy-start | bytes 3538948
  4.3 2.0 %copy-start.2 = (bf16[3,2,144,384]{3,2,1,0:T(8,128)(2,1)S(1)}, bf16[3,2,144,384]{3,2,1,0:T(8,128)(2,1)}, u32[]{:S(2)}) copy-start(bf16[3,2,144,384]{3,2,1,0:T(8,128)(2,1)} %forcing.1) | copy-start | bytes 1990660
  4.4 2.0 %copy-start.3 = (f32[3,384]{1,0:T(4,128)S(1)}, f32[3,384]{1,0:T(4,128)}, u32[]{:S(2)}) copy-start(f32[3,384]{1,0:T(4,128)} %keep_ref.5) | copy-start | bytes 13828
  10.9 5.2 %collective-permute-start.2 = (bf16[80,384]{1,0:T(8,128)(2,1)S(1)}, bf16[80,384]{1,0:T(8,128)(2,1)S(1)}, u32[]{:S(2)}, u32[]{:S(2)}) collective-permute-start(bf16[80,384]{1,0:T(8,128)(2,1)S(1)} %get-tuple-element.15), channel_id=1, source_target_pairs={{0,12},{4,8},{8,4},{12,0},{16,28},{20,24},{24,20},{28,16},{1,13},{... | collective-permute-start | bytes 184328 | tf_op jit(solution)/shard_map/ppermute | solution.py:188
  13.9 4.2 %collective-permute-start.3 = (bf16[80,384]{1,0:T(8,128)(2,1)S(1)}, bf16[80,384]{1,0:T(8,128)(2,1)S(1)}, u32[]{:S(2)}, u32[]{:S(2)}) collective-permute-start(bf16[80,384]{1,0:T(8,128)(2,1)S(1)} %get-tuple-element.16), channel_id=1, source_target_pairs={{0,8},{4,12},{8,0},{12,4},{16,24},{20,28},{24,16},{28,20},{1,9},{5... | collective-permute-start | bytes 184328 | tf_op jit(solution)/shard_map/ppermute | solution.py:188
  14.3 4.2 %collective-permute-start.4 = (bf16[80,384]{1,0:T(8,128)(2,1)S(1)}, bf16[80,384]{1,0:T(8,128)(2,1)S(1)}, u32[]{:S(2)}, u32[]{:S(2)}) collective-permute-start(bf16[80,384]{1,0:T(8,128)(2,1)S(1)} %get-tuple-element.17), channel_id=1, source_target_pairs={{0,4},{4,0},{8,12},{12,8},{16,20},{20,16},{24,28},{28,24},{1,5},{5... | collective-permute-start | bytes 184328 | tf_op jit(solution)/shard_map/ppermute | solution.py:188
  18.7 5.1 %collective-permute-start.5 = (bf16[72,384]{1,0:T(8,128)(2,1)S(1)}, bf16[72,384]{1,0:T(8,128)(2,1)S(1)}, u32[]{:S(2)}, u32[]{:S(2)}) collective-permute-start(bf16[72,384]{1,0:T(8,128)(2,1)S(1)} %fusion), channel_id=1, source_target_pairs={{0,16},{4,20},{8,24},{12,28},{16,0},{20,4},{24,8},{28,12},{1,17},{... | collective-permute-start | bytes 165896 | tf_op jit(solution)/shard_map/ppermute | solution.py:188
  23.9 4.5 %collective-permute-start.6 = (bf16[72,384]{1,0:T(8,128)(2,1)S(1)}, bf16[72,384]{1,0:T(8,128)(2,1)S(1)}, u32[]{:S(2)}, u32[]{:S(2)}) collective-permute-start(bf16[72,384]{1,0:T(8,128)(2,1)S(1)} %get-tuple-element.30), channel_id=1, source_target_pairs={{0,4},{4,0},{8,12},{12,8},{16,20},{20,16},{24,28},{28,24},{1,5},{5... | collective-permute-start | bytes 165896 | tf_op jit(solution)/shard_map/ppermute | solution.py:188
  24.5 4.2 %collective-permute-start.7 = (bf16[72,384]{1,0:T(8,128)(2,1)S(1)}, bf16[72,384]{1,0:T(8,128)(2,1)S(1)}, u32[]{:S(2)}, u32[]{:S(2)}) collective-permute-start(bf16[72,384]{1,0:T(8,128)(2,1)S(1)} %get-tuple-element.29), channel_id=1, source_target_pairs={{0,8},{4,12},{8,0},{12,4},{16,24},{20,28},{24,16},{28,20},{1,9},{5... | collective-permute-start | bytes 165896 | tf_op jit(solution)/shard_map/ppermute | solution.py:188
  26.1 5.1 %collective-permute-start.8 = (bf16[72,384]{1,0:T(8,128)(2,1)S(1)}, bf16[72,384]{1,0:T(8,128)(2,1)S(1)}, u32[]{:S(2)}, u32[]{:S(2)}) collective-permute-start(bf16[72,384]{1,0:T(8,128)(2,1)S(1)} %get-tuple-element.19), channel_id=1, source_target_pairs={{0,12},{4,8},{8,4},{12,0},{16,28},{20,24},{24,20},{28,16},{1,13},{... | collective-permute-start | bytes 165896 | tf_op jit(solution)/shard_map/ppermute | solution.py:188

commit v3 on v2

--- a/solution.py
+++ b/solution.py
@@ -40,11 +40,14 @@
         columns_ref[l] = mask_columns(mask_ref, l)
 
 
-def inner_kernel(place, columns_ref, halo_ref, keep_ref, near_row, far_row, forcing, lift, inverse, far_ref, source_ref):
+def inner_kernel(place, columns_ref, halo_ref, keep_ref, near_row, far_row, forcing, lift, inverse, far_ref, source_ref, jumps):
     layers, width, dofs = near_row.shape
     odd = place[0]
     near_at, far_at = odd, 1 - odd
     is_odd = odd == 1
+    outward = pl.ds(pl.multiple_of((1 - odd) * dofs, 128), dofs)
+    inward = pl.ds(pl.multiple_of(odd * dofs, 128), dofs)
+    weights = lift[...].reshape(4 * dofs, dofs)
     carry = None
     for l in range(layers):
         columns = columns_ref[l]
@@ -52,26 +55,26 @@
             is_odd, columns[:, 2 * face[1] + other : 2 * face[1] + other + 1], columns[:, 2 * face[0] + even : 2 * face[0] + even + 1]
         )
         near, far = near_row[l].astype(F32), far_row[l].astype(F32)
-        near_low, near_up = along_b(near)
-        far_low, far_up = along_b(far)
-        halo = halo_ref[l].astype(F32)
-        far_source = forcing[l, far_at].astype(F32)
-        near_source = forcing[l, near_at].astype(F32)
-        pairs = (
-            (masked_jump(column((1, 0), 1, 0), halo, far), masked_jump(column((1, 0), 0, 1), far, near), lift[1 - odd]),
-            (masked_jump(column((2, 2), 1, 0), far_low, far), masked_jump(column((2, 2), 0, 1), near_low, near), lift[2]),
-            (masked_jump(column((3, 3), 1, 0), far_up, far), masked_jump(column((3, 3), 0, 1), near_up, near), lift[3]),
-        )
-        lifted = sum(dot(jnp.concatenate(pair[:2], axis=0), pair[2]) for pair in pairs)
-        inner = masked_jump(column((0, 1), 1, 0), near, far)
-        far_source = far_source + lifted[:width] + dot(inner, lift[odd])
-        source_ref[l] = near_source + lifted[width:]
+        far_at_rows = pl.ds(2 * l * width, width)
+        near_at_rows = pl.ds((2 * l + 1) * width, width)
+        step = near - far
+        jumps[far_at_rows, outward] = masked_jump(column((1, 0), 1, 0), halo_ref[l].astype(F32), far)
+        jumps[far_at_rows, inward] = (column((0, 1), 1, 0) * step).astype(BF16)
+        jumps[near_at_rows, outward] = (column((1, 0), 0, 1) * -step).astype(BF16)
+        jumps[near_at_rows, inward] = jnp.zeros((width, dofs), BF16)
+        for at, cells, even in ((far_at_rows, far, 1), (near_at_rows, near, 0)):
+            low, up = along_b(cells)
+            jumps[at, pl.ds(2 * dofs, dofs)] = masked_jump(column((2, 2), even, 1 - even), low, cells)
+            jumps[at, pl.ds(3 * dofs, dofs)] = masked_jump(column((3, 3), even, 1 - even), up, cells)
+        lifted = dot(jumps[pl.ds(2 * l * width, 2 * width), :], weights)
+        source_ref[l] = forcing[l, near_at].astype(F32) + lifted[width:]
+        far_source = forcing[l, far_at].astype(F32) + lifted[:width]
         solved = dot(far_source.astype(BF16), inverse[l, far_at])
         carry = solved if l == 0 else keep_ref[l : l + 1, :] * carry + solved
         far_ref[l] = carry
 
 
-def outer_kernel(place, halo_ref, columns_ref, near_row, source_ref, lift, inverse, keep_ref, far_ref, near_ref, p0, p1, p2, p3, carry):
+def outer_kernel(place, halo_ref, columns_ref, near_row, source_ref, lift, inverse, keep_ref, far_ref, near_ref, p0, p3, p2, p1, carry):
     layers, width, dofs = near_row.shape
     odd = place[0]
     inside = place[2] == 0
@@ -102,7 +105,7 @@
         out[...] = jnp.concatenate([carry[pl.ds(start, piece), :], extra], axis=0).astype(BF16)
 
 
-def final_kernel(place, far_ref, near_ref, keep_ref, e0, e1, e2, e3, out_hbm, incoming, out, sem):
+def final_kernel(place, far_ref, near_ref, keep_ref, e3, e2, e1, e0, out_hbm, incoming, out, sem):
     layers, width, dofs = far_ref.shape
     odd = place[0]
     piece = e0.shape[0]
@@ -153,9 +156,9 @@
     unit = 2 * layers * width * dofs * dofs
 
     near_row = lax.dynamic_index_in_dim(cells, odd, 1, False)
-    far_row = lax.dynamic_index_in_dim(cells, 1 - odd, 1, False)
+    far_row = lax.dynamic_index_in_dim(lax.optimization_barrier(cells), 1 - odd, 1, False)
+    chip_halo = lax.ppermute(near_row, ("stream", "cross"), links)
     core_halo = lax.ppermute(far_row, "cross", [(i, i ^ 1) for i in range(crosses)])
-    chip_halo = lax.ppermute(near_row, ("stream", "cross"), links)
     columns = call(
         mask_kernel, place, (face_mask, near_row), [vmem, hbm], like((layers, width, 128), F32), vmem, [], MASK_COST, 20_000_000
     )
@@ -166,13 +169,13 @@
         [vmem] * 8,
         (stack, stack),
         (vmem,) * 2,
-        [],
+        [pltpu.VMEM((2 * layers * width, 4 * dofs), BF16)],
         9 * unit,
         5_000_000,
     )
 
     piece = 2 * width // GROUP
-    near, *pieces = call(
+    near, piece0, piece3, piece2, piece1 = call(
         outer_kernel,
         place,
         (chip_halo, columns, near_row, near_source, lifting, inverse, retention, far),
@@ -187,7 +190,7 @@
     def swap(part, distance):
         return lax.ppermute(part, "stream", [(i, i ^ distance) for i in range(streams)])
 
-    got = [pieces[0]] + [swap(pieces[k], k) for k in range(1, GROUP)]
+    got = [piece0, swap(piece1, 1), swap(piece2, 2), swap(piece3, 3)]
     pick = lambda parts, j: functools.reduce(
         lambda rest, k: jnp.where((member ^ k) == j, parts[k], rest), range(1, GROUP), parts[0]
     )
@@ -228,7 +231,7 @@
     return call(
         final_kernel,
         place,
-        (far, near, retention, *back),
+        (far, near, retention, *back[::-1]),
         [vmem] * (3 + GROUP),
         like(cells.shape, F32),
         hbm,

time: 33 us -> 32.1 us (0.973)
  waiting for transfers between devices: 10.2 us -> 9.05 us
    ppermute x7, waiting for transfers between devices: 10.2 us -> 9.04 us  [swap(): lax.ppermute(part, 'stream', [(i, i ^ distance) for i in range(streams)])]
    unnamed x10 -> x12, local copies, waits for them, and re-layouts: 1.28 us -> 2.37 us
    squeeze x1 -> x2, local copies, waits for them, and re-layouts: 1.15 us -> 0.07 us  [the longest x1 0.03 us: body(): near_row = lax.dynamic_index_in_dim(cells, odd, 1, False)]
  transfers between devices with their start and end apart: 9 -> 9, of which waited for: 7 -> 7; matrix products, arithmetic and copies ran while one was open for 0% -> 0% of each run, Pallas kernels for 12% -> 13%
where the time goes in v3:
time: 32.1 us; the launch traced here: 31.9 us
  starting transfers between devices  12.9 us (40%)
  waiting for transfers between devices  9.05 us (28%)
  Pallas kernels  7.11 us (22%)
  local copies, waits for them, and re-layouts  2.43 us (8%)
  other arithmetic  0.35 us (1%)
    ppermute x7, starting transfers between devices, swap(): lax.ppermute(part, 'stream', [(i, i ^ distance) for i in range(streams)])  9.76 us
    ppermute x7, waiting for transfers between devices, swap(): lax.ppermute(part, 'stream', [(i, i ^ distance) for i in range(streams)])  9.04 us
    pallas_call x4, Pallas kernels, call(): pl.pallas_call(kernel, out_shape=outs, in_specs=[pl.BlockSpec(memory_spac...  7.11 us
    ppermute x1, starting transfers between devices, body(): chip_halo = lax.ppermute(near_row, ('stream', 'cross'), links)  2.61 us
    unnamed x12, local copies, waits for them, and re-layouts  2.37 us
  transfers between devices with their start and end apart: 9, of which 7 were waited for; matrix products, arithmetic and copies ran while one was open for 0% of the time, Pallas kernels for 13%

profile of v3, /device:TPU:0, one launch (start us, length us, event | category | flops | bytes accessed | tf_op | source)
XLA Modules:
  0.0 31.9 jit_solution(8569770107528228994)
XLA Ops:
  0.0 0.0 copy-start
  0.0 0.0 copy-start.5
  0.0 1.1 %copy-done = bf16[3,2,144,384]{3,2,1,0:T(8,128)(2,1)S(1)} copy-done((bf16[3,2,144,384]{3,2,1,0:T(8,128)(2,1)S(1)}, bf16[3,2,144,384]{3,2,1,0:T(8,128)(2,1)}, u32[]{:S(2)}) %copy-start) | copy-done | bytes 663576
  1.1 0.5 %collective-permute-start = (bf16[3,144,384]{2,1,0:T(8,128)(2,1)S(1)}, bf16[3,144,384]{2,1,0:T(8,128)(2,1)S(1)}, u32[]{:S(2)}, u32[]{:S(2)}) collective-permute-start(bf16[3,144,384]{2,1,0:T(8,128)(2,1)S(1)} %dynamic-slice_bitcast_fusion.far_row), channel_id=1, source_target_pairs={{0,1},{1,0},{2,3},{3,2},{4,5},{5,4},{6,7},{7,6},{8,9},{9,8},{10,11... | collective-permute-start | bytes 995336 | tf_op jit(solution)/shard_map/ppermute | solution.py:161
  1.7 2.6 %collective-permute-start.1 = (bf16[3,144,384]{2,1,0:T(8,128)(2,1)S(1)}, bf16[3,144,384]{2,1,0:T(8,128)(2,1)S(1)}, u32[]{:S(2)}, u32[]{:S(2)}) collective-permute-start(bf16[3,144,384]{2,1,0:T(8,128)(2,1)S(1)} %dynamic-slice_bitcast_fusion.1.after.near_row), channel_id=1, source_target_pairs={{0,4},{1,2},{2,1},{3,7},{4,0},{5,6},{6,5},{7,3},{8,12},{9,10},{10,... | collective-permute-start | bytes 995336 | tf_op jit(solution)/shard_map/ppermute | solution.py:160
  4.3 0.1 pad_add_fusion.place
  4.4 0.0 copy-done.5
  4.4 0.0 copy-start.1
  4.4 0.0 copy-start.2
  4.4 0.0 copy-start.3
  4.4 0.0 copy-start.4
  4.4 0.7 %shard_map.64.columns_ref = f32[3,144,128]{2,1,0:T(8,128)S(1)} custom-call(s32[3]{0:T(128)S(1)} %pad_add_fusion.place, s32[4,3,2,144]{3,2,1,0:T(2,128)S(1)} %copy-done.5, bf16[3,144,384]{2,1,0:T(8,128)(2,1)S(1)} %dynamic-slice_bitcast_fusion.1.after.near_row), custom_call_target="tpu_custom_call" | custom-call | flops 10000000000 | bytes 20000000 | tf_op jit(solution)/shard_map/pallas_call | solution.py:128
  5.1 0.0 collective-permute-done.halo_ref
  5.1 0.8 %copy-done.1 = bf16[3,2,384,384]{3,2,1,0:T(8,128)(2,1)S(1)} copy-done((bf16[3,2,384,384]{3,2,1,0:T(8,128)(2,1)S(1)}, bf16[3,2,384,384]{3,2,1,0:T(8,128)(2,1)}, u32[]{:S(2)}) %copy-start.1) | copy-done | bytes 1769496
  5.9 0.3 %copy-done.2 = bf16[4,384,384]{2,1,0:T(8,128)(2,1)S(1)} copy-done((bf16[4,384,384]{2,1,0:T(8,128)(2,1)S(1)}, bf16[4,384,384]{2,1,0:T(8,128)(2,1)}, u32[]{:S(2)}) %copy-start.2) | copy-done | bytes 1179672
  6.2 0.2 copy-done.3
  6.4 0.0 copy-done.4
  6.4 3.3 %shard_map.65 = (f32[3,144,384]{2,1,0:T(8,128)S(1)}, f32[3,144,384]{2,1,0:T(8,128)S(1)}) custom-call(s32[3]{0:T(128)S(1)} %pad_add_fusion.place, f32[3,144,128]{2,1,0:T(8,128)S(1)} %shard_map.64.columns_ref, bf16[3,144,384]{2,1,0:T(8,128)(2,1)S(1)} %collective-permute-done.halo_ref, f32[3,384]{1,0:T(4,128)S(1)} %copy-done.4, ...), custom_call_target="tpu_custom_call" | custom-call | flops 1146617856 | bytes 5000000 | tf_op jit(solution)/shard_map/pallas_call | solution.py:128
  9.7 0.0 collective-permute-done.1.halo_ref
  9.7 1.4 %shard_map.66 = (f32[3,144,384]{2,1,0:T(8,128)S(1)}, bf16[80,384]{1,0:T(8,128)(2,1)S(1)}, bf16[80,384]{1,0:T(8,128)(2,1)S(1)}, bf16[80,384]{1,0:T(8,128)(2,1)S(1)}, bf16[80,384]{1,0:T(8,128)(2,1)S(1)}) custom-call(s32[3]{0:T(128)S(1)} %pad_add_fusion.place, bf16[3,144,384]{2,1,0:T(8,128)(2,1)S(1)} %collective-permute-done.1.halo_ref, ...), custom_call_target="tpu_custom_call" | custom-call | flops 254803968 | bytes 3000000 | tf_op jit(solution)/shard_map/pallas_call | solution.py:128
  11.1 2.8 %collective-permute-start.2 = (bf16[80,384]{1,0:T(8,128)(2,1)S(1)}, bf16[80,384]{1,0:T(8,128)(2,1)S(1)}, u32[]{:S(2)}, u32[]{:S(2)}) collective-permute-start(bf16[80,384]{1,0:T(8,128)(2,1)S(1)} %get-tuple-element.15), channel_id=1, source_target_pairs={{0,12},{4,8},{8,4},{12,0},{16,28},{20,24},{24,20},{28,16},{1,13},{... | collective-permute-start | bytes 184328 | tf_op jit(solution)/shard_map/ppermute | solution.py:191
  13.9 0.4 %collective-permute-start.3 = (bf16[80,384]{1,0:T(8,128)(2,1)S(1)}, bf16[80,384]{1,0:T(8,128)(2,1)S(1)}, u32[]{:S(2)}, u32[]{:S(2)}) collective-permute-start(bf16[80,384]{1,0:T(8,128)(2,1)S(1)} %get-tuple-element.16), channel_id=1, source_target_pairs={{0,8},{4,12},{8,0},{12,4},{16,24},{20,28},{24,16},{28,20},{1,9},{5... | collective-permute-start | bytes 184328 | tf_op jit(solution)/shard_map/ppermute | solution.py:191
  14.3 0.3 collective-permute-start.4
  14.7 1.7 %collective-permute-done.2 = bf16[80,384]{1,0:T(8,128)(2,1)S(1)} collective-permute-done((bf16[80,384]{1,0:T(8,128)(2,1)S(1)}, bf16[80,384]{1,0:T(8,128)(2,1)S(1)}, u32[]{:S(2)}, u32[]{:S(2)}) %collective-permute-start.2) | collective-permute-done | bytes 61472 | tf_op jit(solution)/shard_map/ppermute | solution.py:191
  16.4 1.8 %collective-permute-done.3 = bf16[80,384]{1,0:T(8,128)(2,1)S(1)} collective-permute-done((bf16[80,384]{1,0:T(8,128)(2,1)S(1)}, bf16[80,384]{1,0:T(8,128)(2,1)S(1)}, u32[]{:S(2)}, u32[]{:S(2)}) %collective-permute-start.3) | collective-permute-done | bytes 61472 | tf_op jit(solution)/shard_map/ppermute | solution.py:191
  18.1 0.4 %collective-permute-done.4 = bf16[80,384]{1,0:T(8,128)(2,1)S(1)} collective-permute-done((bf16[80,384]{1,0:T(8,128)(2,1)S(1)}, bf16[80,384]{1,0:T(8,128)(2,1)S(1)}, u32[]{:S(2)}, u32[]{:S(2)}) %collective-permute-start.4) | collective-permute-done | bytes 61472 | tf_op jit(solution)/shard_map/ppermute | solution.py:191
  18.6 0.1 select_convert_fusion.1
  18.7 2.7 %collective-permute-start.5 = (bf16[72,384]{1,0:T(8,128)(2,1)S(1)}, bf16[72,384]{1,0:T(8,128)(2,1)S(1)}, u32[]{:S(2)}, u32[]{:S(2)}) collective-permute-start(bf16[72,384]{1,0:T(8,128)(2,1)S(1)} %fusion), channel_id=1, source_target_pairs={{0,16},{4,20},{8,24},{12,28},{16,0},{20,4},{24,8},{28,12},{1,17},{... | collective-permute-start | bytes 165896 | tf_op jit(solution)/shard_map/ppermute | solution.py:191
  21.4 2.4 %collective-permute-done.5 = bf16[72,384]{1,0:T(8,128)(2,1)S(1)} collective-permute-done((bf16[72,384]{1,0:T(8,128)(2,1)S(1)}, bf16[72,384]{1,0:T(8,128)(2,1)S(1)}, u32[]{:S(2)}, u32[]{:S(2)}) %collective-permute-start.5) | collective-permute-done | bytes 55328 | tf_op jit(solution)/shard_map/ppermute | solution.py:191
  23.8 0.1 select_select_fusion
  24.0 1.6 %collective-permute-start.6 = (bf16[72,384]{1,0:T(8,128)(2,1)S(1)}, bf16[72,384]{1,0:T(8,128)(2,1)S(1)}, u32[]{:S(2)}, u32[]{:S(2)}) collective-permute-start(bf16[72,384]{1,0:T(8,128)(2,1)S(1)} %get-tuple-element.29), channel_id=1, source_target_pairs={{0,12},{4,8},{8,4},{12,0},{16,28},{20,24},{24,20},{28,16},{1,13},{... | collective-permute-start | bytes 165896 | tf_op jit(solution)/shard_map/ppermute | solution.py:191
  25.6 0.4 %collective-permute-start.7 = (bf16[72,384]{1,0:T(8,128)(2,1)S(1)}, bf16[72,384]{1,0:T(8,128)(2,1)S(1)}, u32[]{:S(2)}, u32[]{:S(2)}) collective-permute-start(bf16[72,384]{1,0:T(8,128)(2,1)S(1)} %get-tuple-element.28), channel_id=1, source_target_pairs={{0,8},{4,12},{8,0},{12,4},{16,24},{20,28},{24,16},{28,20},{1,9},{5... | collective-permute-start | bytes 165896 | tf_op jit(solution)/shard_map/ppermute | solution.py:191
  26.0 1.5 %collective-permute-start.8 = (bf16[72,384]{1,0:T(8,128)(2,1)S(1)}, bf16[72,384]{1,0:T(8,128)(2,1)S(1)}, u32[]{:S(2)}, u32[]{:S(2)}) collective-permute-start(bf16[72,384]{1,0:T(8,128)(2,1)S(1)} %get-tuple-element.27), channel_id=1, source_target_pairs={{0,4},{4,0},{8,12},{12,8},{16,20},{20,16},{24,28},{28,24},{1,5},{5... | collective-permute-start | bytes 165896 | tf_op jit(solution)/shard_map/ppermute | solution.py:191
  27.5 1.6 %collective-permute-done.6.e3 = bf16[72,384]{1,0:T(8,128)(2,1)S(1)} collective-permute-done((bf16[72,384]{1,0:T(8,128)(2,1)S(1)}, bf16[72,384]{1,0:T(8,128)(2,1)S(1)}, u32[]{:S(2)}, u32[]{:S(2)}) %collective-permute-start.6) | collective-permute-done | bytes 55328 | tf_op jit(solution)/shard_map/ppermute | solution.py:191
  29.1 0.7 %collective-permute-done.7.e2 = bf16[72,384]{1,0:T(8,128)(2,1)S(1)} collective-permute-done((bf16[72,384]{1,0:T(8,128)(2,1)S(1)}, bf16[72,384]{1,0:T(8,128)(2,1)S(1)}, u32[]{:S(2)}, u32[]{:S(2)}) %collective-permute-start.7) | collective-permute-done | bytes 55328 | tf_op jit(solution)/shard_map/ppermute | solution.py:191
  29.8 0.4 %collective-permute-done.8.e1 = bf16[72,384]{1,0:T(8,128)(2,1)S(1)} collective-permute-done((bf16[72,384]{1,0:T(8,128)(2,1)S(1)}, bf16[72,384]{1,0:T(8,128)(2,1)S(1)}, u32[]{:S(2)}, u32[]{:S(2)}) %collective-permute-start.8) | collective-permute-done | bytes 55328 | tf_op jit(solution)/shard_map/ppermute | solution.py:191
  30.2 1.7 %shard_map.67 = f32[3,2,144,384]{3,2,1,0:T(8,128)} custom-call(s32[3]{0:T(128)S(1)} %pad_add_fusion.place, f32[3,144,384]{2,1,0:T(8,128)S(1)} %get-tuple-element.12.far_ref, f32[3,144,384]{2,1,0:T(8,128)S(1)} %get-tuple-element.14.near_ref, f32[3,384]{1,0:T(4,128)S(1)} %copy-done.4, bf16[72,384]{1,0:T(8,128)(2,1)S(1)} %collective-permute-done.6.e3, ...), custom_call_target="tpu_custom_call" | custom-call | flops 1000000 | bytes 4000000 | tf_op jit(solution)/shard_map/pallas_call | solution.py:128
  (7 shorter events, 0.2 us)
Async XLA Ops:
  0.0 1.1 %copy-start = (bf16[3,2,144,384]{3,2,1,0:T(8,128)(2,1)S(1)}, bf16[3,2,144,384]{3,2,1,0:T(8,128)(2,1)}, u32[]{:S(2)}) copy-start(bf16[3,2,144,384]{3,2,1,0:T(8,128)(2,1)} %param.7) | copy-start | bytes 1990660
  0.0 4.4 %copy-start.5 = (s32[4,3,2,144]{3,2,1,0:T(2,128)S(1)}, s32[4,3,2,144]{3,2,1,0:T(2,128)}, u32[]{:S(2)}) copy-start(s32[4,3,2,144]{3,2,1,0:T(2,128)} %mask_ref.1) | copy-start | bytes 41476
  1.1 4.0 %collective-permute-start = (bf16[3,144,384]{2,1,0:T(8,128)(2,1)S(1)}, bf16[3,144,384]{2,1,0:T(8,128)(2,1)S(1)}, u32[]{:S(2)}, u32[]{:S(2)}) collective-permute-start(bf16[3,144,384]{2,1,0:T(8,128)(2,1)S(1)} %dynamic-slice_bitcast_fusion.far_row), channel_id=1, source_target_pairs={{0,1},{1,0},{2,3},{3,2},{4,5},{5,4},{6,7},{7,6},{8,9},{9,8},{10,11... | collective-permute-start | bytes 995336 | tf_op jit(solution)/shard_map/ppermute | solution.py:161
  1.7 8.0 %collective-permute-start.1 = (bf16[3,144,384]{2,1,0:T(8,128)(2,1)S(1)}, bf16[3,144,384]{2,1,0:T(8,128)(2,1)S(1)}, u32[]{:S(2)}, u32[]{:S(2)}) collective-permute-start(bf16[3,144,384]{2,1,0:T(8,128)(2,1)S(1)} %dynamic-slice_bitcast_fusion.1.after.near_row), channel_id=1, source_target_pairs={{0,4},{1,2},{2,1},{3,7},{4,0},{5,6},{6,5},{7,3},{8,12},{9,10},{10,... | collective-permute-start | bytes 995336 | tf_op jit(solution)/shard_map/ppermute | solution.py:160
  4.4 1.5 %copy-start.1 = (bf16[3,2,384,384]{3,2,1,0:T(8,128)(2,1)S(1)}, bf16[3,2,384,384]{3,2,1,0:T(8,128)(2,1)}, u32[]{:S(2)}) copy-start(bf16[3,2,384,384]{3,2,1,0:T(8,128)(2,1)} %inverse.3) | copy-start | bytes 5308420
  4.4 1.8 %copy-start.2 = (bf16[4,384,384]{2,1,0:T(8,128)(2,1)S(1)}, bf16[4,384,384]{2,1,0:T(8,128)(2,1)}, u32[]{:S(2)}) copy-start(bf16[4,384,384]{2,1,0:T(8,128)(2,1)} %lift.3) | copy-start | bytes 3538948
  4.4 2.0 %copy-start.3 = (bf16[3,2,144,384]{3,2,1,0:T(8,128)(2,1)S(1)}, bf16[3,2,144,384]{3,2,1,0:T(8,128)(2,1)}, u32[]{:S(2)}) copy-start(bf16[3,2,144,384]{3,2,1,0:T(8,128)(2,1)} %forcing.1) | copy-start | bytes 1990660
  4.4 2.0 %copy-start.4 = (f32[3,384]{1,0:T(4,128)S(1)}, f32[3,384]{1,0:T(4,128)}, u32[]{:S(2)}) copy-start(f32[3,384]{1,0:T(4,128)} %keep_ref.5) | copy-start | bytes 13828
  11.1 5.3 %collective-permute-start.2 = (bf16[80,384]{1,0:T(8,128)(2,1)S(1)}, bf16[80,384]{1,0:T(8,128)(2,1)S(1)}, u32[]{:S(2)}, u32[]{:S(2)}) collective-permute-start(bf16[80,384]{1,0:T(8,128)(2,1)S(1)} %get-tuple-element.15), channel_id=1, source_target_pairs={{0,12},{4,8},{8,4},{12,0},{16,28},{20,24},{24,20},{28,16},{1,13},{... | collective-permute-start | bytes 184328 | tf_op jit(solution)/shard_map/ppermute | solution.py:191
  13.9 4.2 %collective-permute-start.3 = (bf16[80,384]{1,0:T(8,128)(2,1)S(1)}, bf16[80,384]{1,0:T(8,128)(2,1)S(1)}, u32[]{:S(2)}, u32[]{:S(2)}) collective-permute-start(bf16[80,384]{1,0:T(8,128)(2,1)S(1)} %get-tuple-element.16), channel_id=1, source_target_pairs={{0,8},{4,12},{8,0},{12,4},{16,24},{20,28},{24,16},{28,20},{1,9},{5... | collective-permute-start | bytes 184328 | tf_op jit(solution)/shard_map/ppermute | solution.py:191
  14.3 4.2 %collective-permute-start.4 = (bf16[80,384]{1,0:T(8,128)(2,1)S(1)}, bf16[80,384]{1,0:T(8,128)(2,1)S(1)}, u32[]{:S(2)}, u32[]{:S(2)}) collective-permute-start(bf16[80,384]{1,0:T(8,128)(2,1)S(1)} %get-tuple-element.17), channel_id=1, source_target_pairs={{0,4},{4,0},{8,12},{12,8},{16,20},{20,16},{24,28},{28,24},{1,5},{5... | collective-permute-start | bytes 184328 | tf_op jit(solution)/shard_map/ppermute | solution.py:191
  18.7 5.1 %collective-permute-start.5 = (bf16[72,384]{1,0:T(8,128)(2,1)S(1)}, bf16[72,384]{1,0:T(8,128)(2,1)S(1)}, u32[]{:S(2)}, u32[]{:S(2)}) collective-permute-start(bf16[72,384]{1,0:T(8,128)(2,1)S(1)} %fusion), channel_id=1, source_target_pairs={{0,16},{4,20},{8,24},{12,28},{16,0},{20,4},{24,8},{28,12},{1,17},{... | collective-permute-start | bytes 165896 | tf_op jit(solution)/shard_map/ppermute | solution.py:191
  24.0 5.1 %collective-permute-start.6 = (bf16[72,384]{1,0:T(8,128)(2,1)S(1)}, bf16[72,384]{1,0:T(8,128)(2,1)S(1)}, u32[]{:S(2)}, u32[]{:S(2)}) collective-permute-start(bf16[72,384]{1,0:T(8,128)(2,1)S(1)} %get-tuple-element.29), channel_id=1, source_target_pairs={{0,12},{4,8},{8,4},{12,0},{16,28},{20,24},{24,20},{28,16},{1,13},{... | collective-permute-start | bytes 165896 | tf_op jit(solution)/shard_map/ppermute | solution.py:191
  25.6 4.2 %collective-permute-start.7 = (bf16[72,384]{1,0:T(8,128)(2,1)S(1)}, bf16[72,384]{1,0:T(8,128)(2,1)S(1)}, u32[]{:S(2)}, u32[]{:S(2)}) collective-permute-start(bf16[72,384]{1,0:T(8,128)(2,1)S(1)} %get-tuple-element.28), channel_id=1, source_target_pairs={{0,8},{4,12},{8,0},{12,4},{16,24},{20,28},{24,16},{28,20},{1,9},{5... | collective-permute-start | bytes 165896 | tf_op jit(solution)/shard_map/ppermute | solution.py:191
  26.0 4.2 %collective-permute-start.8 = (bf16[72,384]{1,0:T(8,128)(2,1)S(1)}, bf16[72,384]{1,0:T(8,128)(2,1)S(1)}, u32[]{:S(2)}, u32[]{:S(2)}) collective-permute-start(bf16[72,384]{1,0:T(8,128)(2,1)S(1)} %get-tuple-element.27), channel_id=1, source_target_pairs={{0,4},{4,0},{8,12},{12,8},{16,20},{20,16},{24,28},{28,24},{1,5},{5... | collective-permute-start | bytes 165896 | tf_op jit(solution)/shard_map/ppermute | solution.py:191

commit v4 on v3

--- a/solution.py
+++ b/solution.py
@@ -35,14 +35,14 @@
     return jnp.dot(a, b, preferred_element_type=F32)
 
 
-def mask_kernel(place, mask_ref, after, columns_ref):
+def mask_kernel(mask_ref, after, columns_ref):
     for l in range(columns_ref.shape[0]):
         columns_ref[l] = mask_columns(mask_ref, l)
 
 
-def inner_kernel(place, columns_ref, halo_ref, keep_ref, near_row, far_row, forcing, lift, inverse, far_ref, source_ref, jumps):
+def inner_kernel(columns_ref, halo_ref, keep_ref, near_row, far_row, forcing, lift, inverse, far_ref, source_ref, jumps):
     layers, width, dofs = near_row.shape
-    odd = place[0]
+    odd = lax.axis_index("cross") & 1
     near_at, far_at = odd, 1 - odd
     is_odd = odd == 1
     outward = pl.ds(pl.multiple_of((1 - odd) * dofs, 128), dofs)
@@ -74,10 +74,11 @@
         far_ref[l] = carry
 
 
-def outer_kernel(place, halo_ref, columns_ref, near_row, source_ref, lift, inverse, keep_ref, far_ref, near_ref, p0, p3, p2, p1, carry):
+def outer_kernel(halo_ref, columns_ref, near_row, source_ref, lift, inverse, keep_ref, far_ref, near_ref, p0, p3, p2, p1, carry):
     layers, width, dofs = near_row.shape
-    odd = place[0]
-    inside = place[2] == 0
+    odd = lax.axis_index("cross") & 1
+    cross = lax.axis_index("cross")
+    inside = (cross != 0) & (cross != lax.axis_size("cross") - 1)
     jumps = []
     for l in range(layers):
         edge = jnp.where(odd == 1, columns_ref[l, :, 3:4], columns_ref[l, :, 0:1])
@@ -100,17 +101,19 @@
     at = lax.broadcasted_iota(jnp.int32, (8, dofs), 0)
     extra = jnp.where(at == 0, high, jnp.where(at == 1, low, 0.0))
     piece = 2 * width // GROUP
+    member = lax.axis_index("stream") & (GROUP - 1)
     for k, out in enumerate((p0, p1, p2, p3)):
-        start = pl.multiple_of((place[1] ^ k) * piece, 8)
+        start = pl.multiple_of((member ^ k) * piece, 8)
         out[...] = jnp.concatenate([carry[pl.ds(start, piece), :], extra], axis=0).astype(BF16)
 
 
-def final_kernel(place, far_ref, near_ref, keep_ref, e3, e2, e1, e0, out_hbm, incoming, out, sem):
+def final_kernel(far_ref, near_ref, keep_ref, e3, e2, e1, e0, out_hbm, incoming, out, sem):
     layers, width, dofs = far_ref.shape
-    odd = place[0]
+    odd = lax.axis_index("cross") & 1
     piece = e0.shape[0]
+    member = lax.axis_index("stream") & (GROUP - 1)
     for k, part in enumerate((e0, e1, e2, e3)):
-        start = pl.multiple_of((place[1] ^ k) * piece, 8)
+        start = pl.multiple_of((member ^ k) * piece, 8)
         incoming[pl.ds(start, piece), :] = part[...].astype(F32)
     copies = []
     factor = None
@@ -124,16 +127,16 @@
         copy.wait()
 
 
-def call(kernel, place, operands, in_specs, outs, out_specs, scratch, flops, moved):
+def call(kernel, operands, in_specs, outs, out_specs, scratch, flops, moved):
     return pl.pallas_call(
         kernel,
         out_shape=outs,
-        in_specs=[pl.BlockSpec(memory_space=pltpu.SMEM)] + in_specs,
+        in_specs=in_specs,
         out_specs=out_specs,
         scratch_shapes=scratch,
         compiler_params=pltpu.CompilerParams(vmem_limit_bytes=VMEM_LIMIT),
         cost_estimate=pl.CostEstimate(flops=flops, bytes_accessed=moved, transcendentals=0),
-    )(place, *operands)
+    )(*operands)
 
 
 def body(forcing, cells, face_mask, lifting, inverse, retention):
@@ -141,8 +144,6 @@
     crosses, streams = lax.axis_size("cross"), lax.axis_size("stream")
     cross, stream = lax.axis_index("cross"), lax.axis_index("stream")
     odd, member = cross % 2, stream % GROUP
-    at_end = (cross == 0) | (cross == crosses - 1)
-    place = jnp.stack([odd, member, at_end.astype(jnp.int32)]).astype(jnp.int32)
 
     links = []
     for s in range(streams):
@@ -160,11 +161,10 @@
     chip_halo = lax.ppermute(near_row, ("stream", "cross"), links)
     core_halo = lax.ppermute(far_row, "cross", [(i, i ^ 1) for i in range(crosses)])
     columns = call(
-        mask_kernel, place, (face_mask, near_row), [vmem, hbm], like((layers, width, 128), F32), vmem, [], MASK_COST, 20_000_000
+        mask_kernel, (face_mask, near_row), [vmem, hbm], like((layers, width, 128), F32), vmem, [], MASK_COST, 20_000_000
     )
     far, near_source = call(
         inner_kernel,
-        place,
         (columns, core_halo, retention, near_row, far_row, forcing, lifting, inverse),
         [vmem] * 8,
         (stack, stack),
@@ -177,7 +177,6 @@
     piece = 2 * width // GROUP
     near, piece0, piece3, piece2, piece1 = call(
         outer_kernel,
-        place,
         (chip_halo, columns, near_row, near_source, lifting, inverse, retention, far),
         [vmem] * 8,
         (stack,) + (like((piece + 8, dofs), BF16),) * GROUP,
@@ -230,7 +229,6 @@
 
     return call(
         final_kernel,
-        place,
         (far, near, retention, *back[::-1]),
         [vmem] * (3 + GROUP),
         like(cells.shape, F32),

time: 32.1 us -> 31.1 us (0.969)
  waiting for transfers between devices: 9.05 us -> 11.5 us
  Pallas kernels: 7.11 us -> 4.8 us
  local copies, waits for them, and re-layouts: 2.43 us -> 1.19 us
    pallas_call x4, Pallas kernels: 7.11 us -> 4.8 us  [call(): pl.pallas_call(kernel, out_shape=outs, in_specs=in_specs, out_specs=out_s...]
    ppermute x1, waiting for transfers between devices: 0.01 us -> 2.31 us  [body(): chip_halo = lax.ppermute(near_row, ('stream', 'cross'), links)]
    unnamed x12, local copies, waits for them, and re-layouts: 2.37 us -> 1.12 us
  transfers between devices with their start and end apart: 9 -> 9, of which waited for: 7 -> 8; matrix products, arithmetic and copies ran while one was open for 0% -> 0% of each run, Pallas kernels for 13% -> 9%
where the time goes in v4:
time: 31.1 us; the launch traced here: 30.9 us
  starting transfers between devices  13.1 us (42%)
  waiting for transfers between devices  11.5 us (37%)
  Pallas kernels  4.8 us (15%)
  local copies, waits for them, and re-layouts  1.19 us (4%)
    ppermute x7, starting transfers between devices, swap(): lax.ppermute(part, 'stream', [(i, i ^ distance) for i in range(streams)])  9.94 us
    ppermute x7, waiting for transfers between devices, swap(): lax.ppermute(part, 'stream', [(i, i ^ distance) for i in range(streams)])  9.17 us
    pallas_call x4, Pallas kernels, call(): pl.pallas_call(kernel, out_shape=outs, in_specs=in_specs, out_specs=out_s...  4.8 us
    ppermute x1, starting transfers between devices, body(): chip_halo = lax.ppermute(near_row, ('stream', 'cross'), links)  2.61 us
    ppermute x1, waiting for transfers between devices, body(): chip_halo = lax.ppermute(near_row, ('stream', 'cross'), links)  2.31 us
    unnamed x12, local copies, waits for them, and re-layouts  1.12 us
  transfers between devices with their start and end apart: 9, of which 8 were waited for; matrix products, arithmetic and copies ran while one was open for 0% of the time, Pallas kernels for 9%

profile of v4, /device:TPU:0, one launch (start us, length us, event | category | flops | bytes accessed | tf_op | source)
XLA Modules:
  0.0 30.9 jit_solution(13823976406569780680)
XLA Ops:
  0.0 0.0 copy-start
  0.0 0.0 copy-start.5
  0.0 1.1 %copy-done = bf16[3,2,144,384]{3,2,1,0:T(8,128)(2,1)S(1)} copy-done((bf16[3,2,144,384]{3,2,1,0:T(8,128)(2,1)S(1)}, bf16[3,2,144,384]{3,2,1,0:T(8,128)(2,1)}, u32[]{:S(2)}) %copy-start) | copy-done | bytes 663576
  1.1 0.5 %collective-permute-start = (bf16[3,144,384]{2,1,0:T(8,128)(2,1)S(1)}, bf16[3,144,384]{2,1,0:T(8,128)(2,1)S(1)}, u32[]{:S(2)}, u32[]{:S(2)}) collective-permute-start(bf16[3,144,384]{2,1,0:T(8,128)(2,1)S(1)} %dynamic-slice_bitcast_fusion.far_row), channel_id=1, source_target_pairs={{0,1},{1,0},{2,3},{3,2},{4,5},{5,4},{6,7},{7,6},{8,9},{9,8},{10,11... | collective-permute-start | bytes 995336 | tf_op jit(solution)/shard_map/ppermute | solution.py:162
  1.7 0.0 copy-start.1
  1.7 0.0 copy-start.2
  1.7 0.0 copy-start.3
  1.7 0.0 copy-start.4
  1.7 2.6 %collective-permute-start.1 = (bf16[3,144,384]{2,1,0:T(8,128)(2,1)S(1)}, bf16[3,144,384]{2,1,0:T(8,128)(2,1)S(1)}, u32[]{:S(2)}, u32[]{:S(2)}) collective-permute-start(bf16[3,144,384]{2,1,0:T(8,128)(2,1)S(1)} %dynamic-slice_bitcast_fusion.1.after.near_row), channel_id=1, source_target_pairs={{0,4},{1,2},{2,1},{3,7},{4,0},{5,6},{6,5},{7,3},{8,12},{9,10},{10,... | collective-permute-start | bytes 995336 | tf_op jit(solution)/shard_map/ppermute | solution.py:161
  4.3 0.0 copy-done.5
  4.3 0.1 shard_map.64.columns_ref
  4.5 0.0 collective-permute-done.halo_ref
  4.5 0.0 copy-done.1
  4.5 0.0 copy-done.2
  4.5 0.0 copy-done.3
  4.5 0.0 copy-done.4
  4.5 2.6 %shard_map.65 = (f32[3,144,384]{2,1,0:T(8,128)S(1)}, f32[3,144,384]{2,1,0:T(8,128)S(1)}) custom-call(f32[3,144,128]{2,1,0:T(8,128)S(1)} %shard_map.64.columns_ref, bf16[3,144,384]{2,1,0:T(8,128)(2,1)S(1)} %collective-permute-done.halo_ref, f32[3,384]{1,0:T(4,128)S(1)} %copy-done.4, bf16[3,144,384]{2,1,0:T(8,128)(2,1)S(1)} %dynamic-slice_bitcast_fusion.1.after.near_row, ...), custom_call_target="tpu_custom_call" | custom-call | flops 1146617856 | bytes 5000000 | tf_op jit(solution)/shard_map/pallas_call | solution.py:131
  7.1 2.3 %collective-permute-done.1.halo_ref = bf16[3,144,384]{2,1,0:T(8,128)(2,1)S(1)} collective-permute-done((bf16[3,144,384]{2,1,0:T(8,128)(2,1)S(1)}, bf16[3,144,384]{2,1,0:T(8,128)(2,1)S(1)}, u32[]{:S(2)}, u32[]{:S(2)}) %collective-permute-start.1) | collective-permute-done | bytes 331808 | tf_op jit(solution)/shard_map/ppermute | solution.py:161
  9.4 0.9 %shard_map.66 = (f32[3,144,384]{2,1,0:T(8,128)S(1)}, bf16[80,384]{1,0:T(8,128)(2,1)S(1)}, bf16[80,384]{1,0:T(8,128)(2,1)S(1)}, bf16[80,384]{1,0:T(8,128)(2,1)S(1)}, bf16[80,384]{1,0:T(8,128)(2,1)S(1)}) custom-call(bf16[3,144,384]{2,1,0:T(8,128)(2,1)S(1)} %collective-permute-done.1.halo_ref, f32[3,144,128]{2,1,0:T(8,128)S(1)} %shard_map.64.columns_ref, ...), custom_call_target="tpu_custom_call" | custom-call | flops 254803968 | bytes 3000000 | tf_op jit(solution)/shard_map/pallas_call | solution.py:131
  10.4 3.1 %collective-permute-start.2 = (bf16[80,384]{1,0:T(8,128)(2,1)S(1)}, bf16[80,384]{1,0:T(8,128)(2,1)S(1)}, u32[]{:S(2)}, u32[]{:S(2)}) collective-permute-start(bf16[80,384]{1,0:T(8,128)(2,1)S(1)} %get-tuple-element.15), channel_id=1, source_target_pairs={{0,12},{4,8},{8,4},{12,0},{16,28},{20,24},{24,20},{28,16},{1,13},{... | collective-permute-start | bytes 184328 | tf_op jit(solution)/shard_map/ppermute | solution.py:190
  13.4 0.5 %collective-permute-start.3 = (bf16[80,384]{1,0:T(8,128)(2,1)S(1)}, bf16[80,384]{1,0:T(8,128)(2,1)S(1)}, u32[]{:S(2)}, u32[]{:S(2)}) collective-permute-start(bf16[80,384]{1,0:T(8,128)(2,1)S(1)} %get-tuple-element.16), channel_id=1, source_target_pairs={{0,8},{4,12},{8,0},{12,4},{16,24},{20,28},{24,16},{28,20},{1,9},{5... | collective-permute-start | bytes 184328 | tf_op jit(solution)/shard_map/ppermute | solution.py:190
  13.9 0.2 collective-permute-start.4
  14.1 1.6 %collective-permute-done.2 = bf16[80,384]{1,0:T(8,128)(2,1)S(1)} collective-permute-done((bf16[80,384]{1,0:T(8,128)(2,1)S(1)}, bf16[80,384]{1,0:T(8,128)(2,1)S(1)}, u32[]{:S(2)}, u32[]{:S(2)}) %collective-permute-start.2) | collective-permute-done | bytes 61472 | tf_op jit(solution)/shard_map/ppermute | solution.py:190
  15.7 1.9 %collective-permute-done.3 = bf16[80,384]{1,0:T(8,128)(2,1)S(1)} collective-permute-done((bf16[80,384]{1,0:T(8,128)(2,1)S(1)}, bf16[80,384]{1,0:T(8,128)(2,1)S(1)}, u32[]{:S(2)}, u32[]{:S(2)}) %collective-permute-start.3) | collective-permute-done | bytes 61472 | tf_op jit(solution)/shard_map/ppermute | solution.py:190
  17.7 0.5 %collective-permute-done.4 = bf16[80,384]{1,0:T(8,128)(2,1)S(1)} collective-permute-done((bf16[80,384]{1,0:T(8,128)(2,1)S(1)}, bf16[80,384]{1,0:T(8,128)(2,1)S(1)}, u32[]{:S(2)}, u32[]{:S(2)}) %collective-permute-start.4) | collective-permute-done | bytes 61472 | tf_op jit(solution)/shard_map/ppermute | solution.py:190
  18.1 0.1 select_convert_fusion.1
  18.3 2.6 %collective-permute-start.5 = (bf16[72,384]{1,0:T(8,128)(2,1)S(1)}, bf16[72,384]{1,0:T(8,128)(2,1)S(1)}, u32[]{:S(2)}, u32[]{:S(2)}) collective-permute-start(bf16[72,384]{1,0:T(8,128)(2,1)S(1)} %fusion), channel_id=1, source_target_pairs={{0,16},{4,20},{8,24},{12,28},{16,0},{20,4},{24,8},{28,12},{1,17},{... | collective-permute-start | bytes 165896 | tf_op jit(solution)/shard_map/ppermute | solution.py:190
  20.9 2.5 %collective-permute-done.5 = bf16[72,384]{1,0:T(8,128)(2,1)S(1)} collective-permute-done((bf16[72,384]{1,0:T(8,128)(2,1)S(1)}, bf16[72,384]{1,0:T(8,128)(2,1)S(1)}, u32[]{:S(2)}, u32[]{:S(2)}) %collective-permute-start.5) | collective-permute-done | bytes 55328 | tf_op jit(solution)/shard_map/ppermute | solution.py:190
  23.4 0.1 select_select_fusion
  23.5 1.6 %collective-permute-start.6 = (bf16[72,384]{1,0:T(8,128)(2,1)S(1)}, bf16[72,384]{1,0:T(8,128)(2,1)S(1)}, u32[]{:S(2)}, u32[]{:S(2)}) collective-permute-start(bf16[72,384]{1,0:T(8,128)(2,1)S(1)} %get-tuple-element.29), channel_id=1, source_target_pairs={{0,12},{4,8},{8,4},{12,0},{16,28},{20,24},{24,20},{28,16},{1,13},{... | collective-permute-start | bytes 165896 | tf_op jit(solution)/shard_map/ppermute | solution.py:190
  25.2 0.4 %collective-permute-start.7 = (bf16[72,384]{1,0:T(8,128)(2,1)S(1)}, bf16[72,384]{1,0:T(8,128)(2,1)S(1)}, u32[]{:S(2)}, u32[]{:S(2)}) collective-permute-start(bf16[72,384]{1,0:T(8,128)(2,1)S(1)} %get-tuple-element.28), channel_id=1, source_target_pairs={{0,8},{4,12},{8,0},{12,4},{16,24},{20,28},{24,16},{28,20},{1,9},{5... | collective-permute-start | bytes 165896 | tf_op jit(solution)/shard_map/ppermute | solution.py:190
  25.6 1.5 %collective-permute-start.8 = (bf16[72,384]{1,0:T(8,128)(2,1)S(1)}, bf16[72,384]{1,0:T(8,128)(2,1)S(1)}, u32[]{:S(2)}, u32[]{:S(2)}) collective-permute-start(bf16[72,384]{1,0:T(8,128)(2,1)S(1)} %get-tuple-element.27), channel_id=1, source_target_pairs={{0,4},{4,0},{8,12},{12,8},{16,20},{20,16},{24,28},{28,24},{1,5},{5... | collective-permute-start | bytes 165896 | tf_op jit(solution)/shard_map/ppermute | solution.py:190
  27.1 1.6 %collective-permute-done.6.e3 = bf16[72,384]{1,0:T(8,128)(2,1)S(1)} collective-permute-done((bf16[72,384]{1,0:T(8,128)(2,1)S(1)}, bf16[72,384]{1,0:T(8,128)(2,1)S(1)}, u32[]{:S(2)}, u32[]{:S(2)}) %collective-permute-start.6) | collective-permute-done | bytes 55328 | tf_op jit(solution)/shard_map/ppermute | solution.py:190
  28.6 0.7 %collective-permute-done.7.e2 = bf16[72,384]{1,0:T(8,128)(2,1)S(1)} collective-permute-done((bf16[72,384]{1,0:T(8,128)(2,1)S(1)}, bf16[72,384]{1,0:T(8,128)(2,1)S(1)}, u32[]{:S(2)}, u32[]{:S(2)}) %collective-permute-start.7) | collective-permute-done | bytes 55328 | tf_op jit(solution)/shard_map/ppermute | solution.py:190
  29.3 0.4 %collective-permute-done.8.e1 = bf16[72,384]{1,0:T(8,128)(2,1)S(1)} collective-permute-done((bf16[72,384]{1,0:T(8,128)(2,1)S(1)}, bf16[72,384]{1,0:T(8,128)(2,1)S(1)}, u32[]{:S(2)}, u32[]{:S(2)}) %collective-permute-start.8) | collective-permute-done | bytes 55328 | tf_op jit(solution)/shard_map/ppermute | solution.py:190
  29.8 1.2 %shard_map.67 = f32[3,2,144,384]{3,2,1,0:T(8,128)} custom-call(f32[3,144,384]{2,1,0:T(8,128)S(1)} %get-tuple-element.12.far_ref, f32[3,144,384]{2,1,0:T(8,128)S(1)} %get-tuple-element.14.near_ref, f32[3,384]{1,0:T(4,128)S(1)} %copy-done.4, bf16[72,384]{1,0:T(8,128)(2,1)S(1)} %collective-permute-done.6.e3, bf16[72,384]{1,0:T(8,128)(2,1)S(1)} %collective-permute-done.7.e2, ...), custom_call_target="tpu_custom_call" | custom-call | flops 1000000 | bytes 4000000 | tf_op jit(solution)/shard_map/pallas_call | solution.py:131
  (7 shorter events, 0.2 us)
Async XLA Ops:
  0.0 1.1 %copy-start = (bf16[3,2,144,384]{3,2,1,0:T(8,128)(2,1)S(1)}, bf16[3,2,144,384]{3,2,1,0:T(8,128)(2,1)}, u32[]{:S(2)}) copy-start(bf16[3,2,144,384]{3,2,1,0:T(8,128)(2,1)} %param.7) | copy-start | bytes 1990660
  0.0 4.3 %copy-start.5 = (s32[4,3,2,144]{3,2,1,0:T(2,128)S(1)}, s32[4,3,2,144]{3,2,1,0:T(2,128)}, u32[]{:S(2)}) copy-start(s32[4,3,2,144]{3,2,1,0:T(2,128)} %mask_ref.1) | copy-start | bytes 41476
  1.1 3.4 %collective-permute-start = (bf16[3,144,384]{2,1,0:T(8,128)(2,1)S(1)}, bf16[3,144,384]{2,1,0:T(8,128)(2,1)S(1)}, u32[]{:S(2)}, u32[]{:S(2)}) collective-permute-start(bf16[3,144,384]{2,1,0:T(8,128)(2,1)S(1)} %dynamic-slice_bitcast_fusion.far_row), channel_id=1, source_target_pairs={{0,1},{1,0},{2,3},{3,2},{4,5},{5,4},{6,7},{7,6},{8,9},{9,8},{10,11... | collective-permute-start | bytes 995336 | tf_op jit(solution)/shard_map/ppermute | solution.py:162
  1.7 2.8 %copy-start.1 = (bf16[3,2,384,384]{3,2,1,0:T(8,128)(2,1)S(1)}, bf16[3,2,384,384]{3,2,1,0:T(8,128)(2,1)}, u32[]{:S(2)}) copy-start(bf16[3,2,384,384]{3,2,1,0:T(8,128)(2,1)} %inverse.3) | copy-start | bytes 5308420
  1.7 2.8 %copy-start.2 = (bf16[4,384,384]{2,1,0:T(8,128)(2,1)S(1)}, bf16[4,384,384]{2,1,0:T(8,128)(2,1)}, u32[]{:S(2)}) copy-start(bf16[4,384,384]{2,1,0:T(8,128)(2,1)} %lift.3) | copy-start | bytes 3538948
  1.7 2.8 %copy-start.3 = (bf16[3,2,144,384]{3,2,1,0:T(8,128)(2,1)S(1)}, bf16[3,2,144,384]{3,2,1,0:T(8,128)(2,1)}, u32[]{:S(2)}) copy-start(bf16[3,2,144,384]{3,2,1,0:T(8,128)(2,1)} %forcing.1) | copy-start | bytes 1990660
  1.7 2.8 %copy-start.4 = (f32[3,384]{1,0:T(4,128)S(1)}, f32[3,384]{1,0:T(4,128)}, u32[]{:S(2)}) copy-start(f32[3,384]{1,0:T(4,128)} %keep_ref.5) | copy-start | bytes 13828
  1.7 7.7 %collective-permute-start.1 = (bf16[3,144,384]{2,1,0:T(8,128)(2,1)S(1)}, bf16[3,144,384]{2,1,0:T(8,128)(2,1)S(1)}, u32[]{:S(2)}, u32[]{:S(2)}) collective-permute-start(bf16[3,144,384]{2,1,0:T(8,128)(2,1)S(1)} %dynamic-slice_bitcast_fusion.1.after.near_row), channel_id=1, source_target_pairs={{0,4},{1,2},{2,1},{3,7},{4,0},{5,6},{6,5},{7,3},{8,12},{9,10},{10,... | collective-permute-start | bytes 995336 | tf_op jit(solution)/shard_map/ppermute | solution.py:161
  10.4 5.4 %collective-permute-start.2 = (bf16[80,384]{1,0:T(8,128)(2,1)S(1)}, bf16[80,384]{1,0:T(8,128)(2,1)S(1)}, u32[]{:S(2)}, u32[]{:S(2)}) collective-permute-start(bf16[80,384]{1,0:T(8,128)(2,1)S(1)} %get-tuple-element.15), channel_id=1, source_target_pairs={{0,12},{4,8},{8,4},{12,0},{16,28},{20,24},{24,20},{28,16},{1,13},{... | collective-permute-start | bytes 184328 | tf_op jit(solution)/shard_map/ppermute | solution.py:190
  13.4 4.2 %collective-permute-start.3 = (bf16[80,384]{1,0:T(8,128)(2,1)S(1)}, bf16[80,384]{1,0:T(8,128)(2,1)S(1)}, u32[]{:S(2)}, u32[]{:S(2)}) collective-permute-start(bf16[80,384]{1,0:T(8,128)(2,1)S(1)} %get-tuple-element.16), channel_id=1, source_target_pairs={{0,8},{4,12},{8,0},{12,4},{16,24},{20,28},{24,16},{28,20},{1,9},{5... | collective-permute-start | bytes 184328 | tf_op jit(solution)/shard_map/ppermute | solution.py:190
  13.9 4.2 %collective-permute-start.4 = (bf16[80,384]{1,0:T(8,128)(2,1)S(1)}, bf16[80,384]{1,0:T(8,128)(2,1)S(1)}, u32[]{:S(2)}, u32[]{:S(2)}) collective-permute-start(bf16[80,384]{1,0:T(8,128)(2,1)S(1)} %get-tuple-element.17), channel_id=1, source_target_pairs={{0,4},{4,0},{8,12},{12,8},{16,20},{20,16},{24,28},{28,24},{1,5},{5... | collective-permute-start | bytes 184328 | tf_op jit(solution)/shard_map/ppermute | solution.py:190
  18.3 5.1 %collective-permute-start.5 = (bf16[72,384]{1,0:T(8,128)(2,1)S(1)}, bf16[72,384]{1,0:T(8,128)(2,1)S(1)}, u32[]{:S(2)}, u32[]{:S(2)}) collective-permute-start(bf16[72,384]{1,0:T(8,128)(2,1)S(1)} %fusion), channel_id=1, source_target_pairs={{0,16},{4,20},{8,24},{12,28},{16,0},{20,4},{24,8},{28,12},{1,17},{... | collective-permute-start | bytes 165896 | tf_op jit(solution)/shard_map/ppermute | solution.py:190
  23.5 5.1 %collective-permute-start.6 = (bf16[72,384]{1,0:T(8,128)(2,1)S(1)}, bf16[72,384]{1,0:T(8,128)(2,1)S(1)}, u32[]{:S(2)}, u32[]{:S(2)}) collective-permute-start(bf16[72,384]{1,0:T(8,128)(2,1)S(1)} %get-tuple-element.29), channel_id=1, source_target_pairs={{0,12},{4,8},{8,4},{12,0},{16,28},{20,24},{24,20},{28,16},{1,13},{... | collective-permute-start | bytes 165896 | tf_op jit(solution)/shard_map/ppermute | solution.py:190
  25.2 4.2 %collective-permute-start.7 = (bf16[72,384]{1,0:T(8,128)(2,1)S(1)}, bf16[72,384]{1,0:T(8,128)(2,1)S(1)}, u32[]{:S(2)}, u32[]{:S(2)}) collective-permute-start(bf16[72,384]{1,0:T(8,128)(2,1)S(1)} %get-tuple-element.28), channel_id=1, source_target_pairs={{0,8},{4,12},{8,0},{12,4},{16,24},{20,28},{24,16},{28,20},{1,9},{5... | collective-permute-start | bytes 165896 | tf_op jit(solution)/shard_map/ppermute | solution.py:190
  25.6 4.2 %collective-permute-start.8 = (bf16[72,384]{1,0:T(8,128)(2,1)S(1)}, bf16[72,384]{1,0:T(8,128)(2,1)S(1)}, u32[]{:S(2)}, u32[]{:S(2)}) collective-permute-start(bf16[72,384]{1,0:T(8,128)(2,1)S(1)} %get-tuple-element.27), channel_id=1, source_target_pairs={{0,4},{4,0},{8,12},{12,8},{16,20},{20,16},{24,28},{28,24},{1,5},{5... | collective-permute-start | bytes 165896 | tf_op jit(solution)/shard_map/ppermute | solution.py:190

commit v5 on v4

--- a/solution.py
+++ b/solution.py
@@ -40,7 +40,7 @@
         columns_ref[l] = mask_columns(mask_ref, l)
 
 
-def inner_kernel(columns_ref, halo_ref, keep_ref, near_row, far_row, forcing, lift, inverse, far_ref, source_ref, jumps):
+def inner_kernel(columns_ref, halo_ref, keep_ref, near_row, far_row, forcing, lift, inverse, far_ref, start_ref, matrix_ref, jumps):
     layers, width, dofs = near_row.shape
     odd = lax.axis_index("cross") & 1
     near_at, far_at = odd, 1 - odd
@@ -48,7 +48,7 @@
     outward = pl.ds(pl.multiple_of((1 - odd) * dofs, 128), dofs)
     inward = pl.ds(pl.multiple_of(odd * dofs, 128), dofs)
     weights = lift[...].reshape(4 * dofs, dofs)
-    carry = None
+    far_carry = near_carry = None
     for l in range(layers):
         columns = columns_ref[l]
         column = lambda face, even, other: jnp.where(
@@ -67,30 +67,30 @@
             jumps[at, pl.ds(2 * dofs, dofs)] = masked_jump(column((2, 2), even, 1 - even), low, cells)
             jumps[at, pl.ds(3 * dofs, dofs)] = masked_jump(column((3, 3), even, 1 - even), up, cells)
         lifted = dot(jumps[pl.ds(2 * l * width, 2 * width), :], weights)
-        source_ref[l] = forcing[l, near_at].astype(F32) + lifted[width:]
+        near_source = forcing[l, near_at].astype(F32) + lifted[width:]
         far_source = forcing[l, far_at].astype(F32) + lifted[:width]
-        solved = dot(far_source.astype(BF16), inverse[l, far_at])
-        carry = solved if l == 0 else keep_ref[l : l + 1, :] * carry + solved
-        far_ref[l] = carry
-
-
-def outer_kernel(halo_ref, columns_ref, near_row, source_ref, lift, inverse, keep_ref, far_ref, near_ref, p0, p3, p2, p1, carry):
+        near_solved = dot(near_source.astype(BF16), inverse[l, near_at])
+        far_solved = dot(far_source.astype(BF16), inverse[l, far_at])
+        matrix_ref[l] = dot(lift[odd], inverse[l, near_at]).astype(BF16)
+        far_carry = far_solved if l == 0 else keep_ref[l : l + 1, :] * far_carry + far_solved
+        near_carry = near_solved if l == 0 else keep_ref[l : l + 1, :] * near_carry + near_solved
+        far_ref[l] = far_carry
+        start_ref[l] = near_carry
+
+
+def outer_kernel(halo_ref, columns_ref, near_row, start_ref, matrix_ref, keep_ref, far_ref, near_ref, p0, p3, p2, p1, carry):
     layers, width, dofs = near_row.shape
-    odd = lax.axis_index("cross") & 1
     cross = lax.axis_index("cross")
+    odd = cross & 1
     inside = (cross != 0) & (cross != lax.axis_size("cross") - 1)
-    jumps = []
+    total = None
     for l in range(layers):
         edge = jnp.where(odd == 1, columns_ref[l, :, 3:4], columns_ref[l, :, 0:1])
         halo = jnp.where(inside, halo_ref[l].astype(F32), 0.0)
-        jumps.append(masked_jump(edge, halo, near_row[l].astype(F32)))
-    lifted = dot(jnp.concatenate(jumps, axis=0), lift[odd])
-    total = None
-    for l in range(layers):
-        source = source_ref[l] + lifted[l * width : (l + 1) * width]
-        solved = dot(source.astype(BF16), inverse[l, odd])
+        solved = dot(masked_jump(edge, halo, near_row[l].astype(F32)), matrix_ref[l])
         total = solved if l == 0 else keep_ref[l : l + 1, :] * total + solved
-        near_ref[l] = total
+        near_ref[l] = start_ref[l] + total
+    total = total + start_ref[layers - 1]
     carry[pl.ds(0, width), :] = far_ref[layers - 1]
     carry[pl.ds(width, width), :] = total
     factor = keep_ref[0:1, :]
@@ -157,18 +157,18 @@
     unit = 2 * layers * width * dofs * dofs
 
     near_row = lax.dynamic_index_in_dim(cells, odd, 1, False)
-    far_row = lax.dynamic_index_in_dim(lax.optimization_barrier(cells), 1 - odd, 1, False)
+    far_row = lax.dynamic_index_in_dim(lax.optimization_barrier((cells, near_row))[0], 1 - odd, 1, False)
     chip_halo = lax.ppermute(near_row, ("stream", "cross"), links)
     core_halo = lax.ppermute(far_row, "cross", [(i, i ^ 1) for i in range(crosses)])
     columns = call(
         mask_kernel, (face_mask, near_row), [vmem, hbm], like((layers, width, 128), F32), vmem, [], MASK_COST, 20_000_000
     )
-    far, near_source = call(
+    far, near_start, matrix = call(
         inner_kernel,
         (columns, core_halo, retention, near_row, far_row, forcing, lifting, inverse),
         [vmem] * 8,
-        (stack, stack),
-        (vmem,) * 2,
+        (stack, stack, like((layers, dofs, dofs), BF16)),
+        (vmem,) * 3,
         [pltpu.VMEM((2 * layers * width, 4 * dofs), BF16)],
         9 * unit,
         5_000_000,
@@ -177,8 +177,8 @@
     piece = 2 * width // GROUP
     near, piece0, piece3, piece2, piece1 = call(
         outer_kernel,
-        (chip_halo, columns, near_row, near_source, lifting, inverse, retention, far),
-        [vmem] * 8,
+        (chip_halo, columns, near_row, near_start, matrix, retention, far),
+        [vmem] * 7,
         (stack,) + (like((piece + 8, dofs), BF16),) * GROUP,
         (vmem,) * (1 + GROUP),
         [pltpu.VMEM((2 * width, dofs), F32)],

time: 31.1 us -> 30.5 us (0.981)
  waiting for transfers between devices: 11.5 us -> 10.3 us
  Pallas kernels: 4.8 us -> 5.36 us
    ppermute x1, waiting for transfers between devices: 2.31 us -> 0.01 us  [body(): chip_halo = lax.ppermute(near_row, ('stream', 'cross'), links)]
    ppermute x1, waiting for transfers between devices: 0.01 us -> 1.41 us  [body(): lax.ppermute(far_row, 'cross', [(i, i ^ 1) for i in range(crosses)])]
    pallas_call x4, Pallas kernels: 4.8 us -> 5.36 us  [call(): pl.pallas_call(kernel, out_shape=outs, in_specs=in_specs, out_specs=out_s...]
    ppermute x1, starting transfers between devices: 2.61 us -> 3.03 us  [body(): chip_halo = lax.ppermute(near_row, ('stream', 'cross'), links)]
    ppermute x1, starting transfers between devices: 0.52 us -> 0.15 us  [body(): lax.ppermute(far_row, 'cross', [(i, i ^ 1) for i in range(crosses)])]
    ppermute x7, waiting for transfers between devices: 9.17 us -> 8.85 us  [swap(): lax.ppermute(part, 'stream', [(i, i ^ distance) for i in range(streams)])]
  transfers between devices with their start and end apart: 9 -> 9, of which waited for: 8 -> 8; matrix products, arithmetic and copies ran while one was open for 0% -> 0% of each run, Pallas kernels for 9% -> 12%
where the time goes in v5:
time: 30.5 us; the launch traced here: 30.3 us
  starting transfers between devices  12.9 us (42%)
  waiting for transfers between devices  10.3 us (34%)
  Pallas kernels  5.36 us (18%)
  local copies, waits for them, and re-layouts  1.41 us (5%)
    ppermute x7, starting transfers between devices, swap(): lax.ppermute(part, 'stream', [(i, i ^ distance) for i in range(streams)])  9.76 us
    ppermute x7, waiting for transfers between devices, swap(): lax.ppermute(part, 'stream', [(i, i ^ distance) for i in range(streams)])  8.85 us
    pallas_call x4, Pallas kernels, call(): pl.pallas_call(kernel, out_shape=outs, in_specs=in_specs, out_specs=out_s...  5.36 us
    ppermute x1, starting transfers between devices, body(): chip_halo = lax.ppermute(near_row, ('stream', 'cross'), links)  3.03 us
    ppermute x1, waiting for transfers between devices, body(): lax.ppermute(far_row, 'cross', [(i, i ^ 1) for i in range(crosses)])  1.41 us
    unnamed x12, local copies, waits for them, and re-layouts  1.34 us
  transfers between devices with their start and end apart: 9, of which 8 were waited for; matrix products, arithmetic and copies ran while one was open for 0% of the time, Pallas kernels for 12%

profile of v5, /device:TPU:0, one launch (start us, length us, event | category | flops | bytes accessed | tf_op | source)
XLA Modules:
  0.0 30.3 jit_solution(5517358122491864898)
XLA Ops:
  0.0 0.0 copy-start
  0.0 0.0 copy-start.5
  0.0 1.1 %copy-done = bf16[3,2,144,384]{3,2,1,0:T(8,128)(2,1)S(1)} copy-done((bf16[3,2,144,384]{3,2,1,0:T(8,128)(2,1)S(1)}, bf16[3,2,144,384]{3,2,1,0:T(8,128)(2,1)}, u32[]{:S(2)}) %copy-start) | copy-done | bytes 663576
  1.1 3.0 %collective-permute-start.1 = (bf16[3,144,384]{2,1,0:T(8,128)(2,1)S(1)}, bf16[3,144,384]{2,1,0:T(8,128)(2,1)S(1)}, u32[]{:S(2)}, u32[]{:S(2)}) collective-permute-start(bf16[3,144,384]{2,1,0:T(8,128)(2,1)S(1)} %dynamic-slice_bitcast_fusion.1.after.near_row), channel_id=1, source_target_pairs={{0,4},{1,2},{2,1},{3,7},{4,0},{5,6},{6,5},{7,3},{8,12},{9,10},{10,... | collective-permute-start | bytes 995336 | tf_op jit(solution)/shard_map/ppermute | solution.py:161
  4.2 0.0 copy-start.1
  4.2 0.0 copy-start.2
  4.2 0.0 copy-start.3
  4.2 0.0 copy-start.4
  4.2 0.2 collective-permute-start
  4.4 0.0 copy-done.5
  4.4 0.1 shard_map.64.columns_ref
  4.5 1.4 %collective-permute-done.halo_ref = bf16[3,144,384]{2,1,0:T(8,128)(2,1)S(1)} collective-permute-done((bf16[3,144,384]{2,1,0:T(8,128)(2,1)S(1)}, bf16[3,144,384]{2,1,0:T(8,128)(2,1)S(1)}, u32[]{:S(2)}, u32[]{:S(2)}) %collective-permute-start) | collective-permute-done | bytes 331808 | tf_op jit(solution)/shard_map/ppermute | solution.py:162
  5.9 0.0 copy-done.1
  6.0 0.1 copy-done.2
  6.0 0.2 copy-done.3
  6.2 0.0 copy-done.4
  6.2 3.4 %shard_map.65 = (f32[3,144,384]{2,1,0:T(8,128)S(1)}, f32[3,144,384]{2,1,0:T(8,128)S(1)}, bf16[3,384,384]{2,1,0:T(8,128)(2,1)S(1)}) custom-call(f32[3,144,128]{2,1,0:T(8,128)S(1)} %shard_map.64.columns_ref, bf16[3,144,384]{2,1,0:T(8,128)(2,1)S(1)} %collective-permute-done.halo_ref, f32[3,384]{1,0:T(4,128)S(1)} %copy-done.4, ...), custom_call_target="tpu_custom_call" | custom-call | flops 1146617856 | bytes 5000000 | tf_op jit(solution)/shard_map/pallas_call | solution.py:131
  9.6 0.0 collective-permute-done.1.halo_ref
  9.6 0.6 %shard_map.66 = (f32[3,144,384]{2,1,0:T(8,128)S(1)}, bf16[80,384]{1,0:T(8,128)(2,1)S(1)}, bf16[80,384]{1,0:T(8,128)(2,1)S(1)}, bf16[80,384]{1,0:T(8,128)(2,1)S(1)}, bf16[80,384]{1,0:T(8,128)(2,1)S(1)}) custom-call(bf16[3,144,384]{2,1,0:T(8,128)(2,1)S(1)} %collective-permute-done.1.halo_ref, f32[3,144,128]{2,1,0:T(8,128)S(1)} %shard_map.64.columns_ref, ...), custom_call_target="tpu_custom_call" | custom-call | flops 254803968 | bytes 3000000 | tf_op jit(solution)/shard_map/pallas_call | solution.py:131
  10.3 2.8 %collective-permute-start.2 = (bf16[80,384]{1,0:T(8,128)(2,1)S(1)}, bf16[80,384]{1,0:T(8,128)(2,1)S(1)}, u32[]{:S(2)}, u32[]{:S(2)}) collective-permute-start(bf16[80,384]{1,0:T(8,128)(2,1)S(1)} %get-tuple-element.19), channel_id=1, source_target_pairs={{0,12},{4,8},{8,4},{12,0},{16,28},{20,24},{24,20},{28,16},{1,13},{... | collective-permute-start | bytes 184328 | tf_op jit(solution)/shard_map/ppermute | solution.py:190
  13.0 0.4 %collective-permute-start.3 = (bf16[80,384]{1,0:T(8,128)(2,1)S(1)}, bf16[80,384]{1,0:T(8,128)(2,1)S(1)}, u32[]{:S(2)}, u32[]{:S(2)}) collective-permute-start(bf16[80,384]{1,0:T(8,128)(2,1)S(1)} %get-tuple-element.20), channel_id=1, source_target_pairs={{0,8},{4,12},{8,0},{12,4},{16,24},{20,28},{24,16},{28,20},{1,9},{5... | collective-permute-start | bytes 184328 | tf_op jit(solution)/shard_map/ppermute | solution.py:190
  13.5 0.4 %collective-permute-start.4 = (bf16[80,384]{1,0:T(8,128)(2,1)S(1)}, bf16[80,384]{1,0:T(8,128)(2,1)S(1)}, u32[]{:S(2)}, u32[]{:S(2)}) collective-permute-start(bf16[80,384]{1,0:T(8,128)(2,1)S(1)} %get-tuple-element.21), channel_id=1, source_target_pairs={{0,4},{4,0},{8,12},{12,8},{16,20},{20,16},{24,28},{28,24},{1,5},{5... | collective-permute-start | bytes 184328 | tf_op jit(solution)/shard_map/ppermute | solution.py:190
  13.8 2.0 %collective-permute-done.2 = bf16[80,384]{1,0:T(8,128)(2,1)S(1)} collective-permute-done((bf16[80,384]{1,0:T(8,128)(2,1)S(1)}, bf16[80,384]{1,0:T(8,128)(2,1)S(1)}, u32[]{:S(2)}, u32[]{:S(2)}) %collective-permute-start.2) | collective-permute-done | bytes 61472 | tf_op jit(solution)/shard_map/ppermute | solution.py:190
  15.8 1.5 %collective-permute-done.3 = bf16[80,384]{1,0:T(8,128)(2,1)S(1)} collective-permute-done((bf16[80,384]{1,0:T(8,128)(2,1)S(1)}, bf16[80,384]{1,0:T(8,128)(2,1)S(1)}, u32[]{:S(2)}, u32[]{:S(2)}) %collective-permute-start.3) | collective-permute-done | bytes 61472 | tf_op jit(solution)/shard_map/ppermute | solution.py:190
  17.2 0.4 %collective-permute-done.4 = bf16[80,384]{1,0:T(8,128)(2,1)S(1)} collective-permute-done((bf16[80,384]{1,0:T(8,128)(2,1)S(1)}, bf16[80,384]{1,0:T(8,128)(2,1)S(1)}, u32[]{:S(2)}, u32[]{:S(2)}) %collective-permute-start.4) | collective-permute-done | bytes 61472 | tf_op jit(solution)/shard_map/ppermute | solution.py:190
  17.7 0.1 select_convert_fusion.1
  17.8 2.7 %collective-permute-start.5 = (bf16[72,384]{1,0:T(8,128)(2,1)S(1)}, bf16[72,384]{1,0:T(8,128)(2,1)S(1)}, u32[]{:S(2)}, u32[]{:S(2)}) collective-permute-start(bf16[72,384]{1,0:T(8,128)(2,1)S(1)} %fusion), channel_id=1, source_target_pairs={{0,16},{4,20},{8,24},{12,28},{16,0},{20,4},{24,8},{28,12},{1,17},{... | collective-permute-start | bytes 165896 | tf_op jit(solution)/shard_map/ppermute | solution.py:190
  20.5 2.4 %collective-permute-done.5 = bf16[72,384]{1,0:T(8,128)(2,1)S(1)} collective-permute-done((bf16[72,384]{1,0:T(8,128)(2,1)S(1)}, bf16[72,384]{1,0:T(8,128)(2,1)S(1)}, u32[]{:S(2)}, u32[]{:S(2)}) %collective-permute-start.5) | collective-permute-done | bytes 55328 | tf_op jit(solution)/shard_map/ppermute | solution.py:190
  22.9 0.1 select_select_fusion
  23.1 1.6 %collective-permute-start.6 = (bf16[72,384]{1,0:T(8,128)(2,1)S(1)}, bf16[72,384]{1,0:T(8,128)(2,1)S(1)}, u32[]{:S(2)}, u32[]{:S(2)}) collective-permute-start(bf16[72,384]{1,0:T(8,128)(2,1)S(1)} %get-tuple-element.33), channel_id=1, source_target_pairs={{0,12},{4,8},{8,4},{12,0},{16,28},{20,24},{24,20},{28,16},{1,13},{... | collective-permute-start | bytes 165896 | tf_op jit(solution)/shard_map/ppermute | solution.py:190
  24.7 0.4 %collective-permute-start.7 = (bf16[72,384]{1,0:T(8,128)(2,1)S(1)}, bf16[72,384]{1,0:T(8,128)(2,1)S(1)}, u32[]{:S(2)}, u32[]{:S(2)}) collective-permute-start(bf16[72,384]{1,0:T(8,128)(2,1)S(1)} %get-tuple-element.32), channel_id=1, source_target_pairs={{0,8},{4,12},{8,0},{12,4},{16,24},{20,28},{24,16},{28,20},{1,9},{5... | collective-permute-start | bytes 165896 | tf_op jit(solution)/shard_map/ppermute | solution.py:190
  25.0 1.6 %collective-permute-start.8 = (bf16[72,384]{1,0:T(8,128)(2,1)S(1)}, bf16[72,384]{1,0:T(8,128)(2,1)S(1)}, u32[]{:S(2)}, u32[]{:S(2)}) collective-permute-start(bf16[72,384]{1,0:T(8,128)(2,1)S(1)} %get-tuple-element.31), channel_id=1, source_target_pairs={{0,4},{4,0},{8,12},{12,8},{16,20},{20,16},{24,28},{28,24},{1,5},{5... | collective-permute-start | bytes 165896 | tf_op jit(solution)/shard_map/ppermute | solution.py:190
  26.6 1.6 %collective-permute-done.6.e3 = bf16[72,384]{1,0:T(8,128)(2,1)S(1)} collective-permute-done((bf16[72,384]{1,0:T(8,128)(2,1)S(1)}, bf16[72,384]{1,0:T(8,128)(2,1)S(1)}, u32[]{:S(2)}, u32[]{:S(2)}) %collective-permute-start.6) | collective-permute-done | bytes 55328 | tf_op jit(solution)/shard_map/ppermute | solution.py:190
  28.2 0.6 %collective-permute-done.7.e2 = bf16[72,384]{1,0:T(8,128)(2,1)S(1)} collective-permute-done((bf16[72,384]{1,0:T(8,128)(2,1)S(1)}, bf16[72,384]{1,0:T(8,128)(2,1)S(1)}, u32[]{:S(2)}, u32[]{:S(2)}) %collective-permute-start.7) | collective-permute-done | bytes 55328 | tf_op jit(solution)/shard_map/ppermute | solution.py:190
  28.8 0.4 %collective-permute-done.8.e1 = bf16[72,384]{1,0:T(8,128)(2,1)S(1)} collective-permute-done((bf16[72,384]{1,0:T(8,128)(2,1)S(1)}, bf16[72,384]{1,0:T(8,128)(2,1)S(1)}, u32[]{:S(2)}, u32[]{:S(2)}) %collective-permute-start.8) | collective-permute-done | bytes 55328 | tf_op jit(solution)/shard_map/ppermute | solution.py:190
  29.2 1.2 %shard_map.67 = f32[3,2,144,384]{3,2,1,0:T(8,128)} custom-call(f32[3,144,384]{2,1,0:T(8,128)S(1)} %get-tuple-element.15.far_ref, f32[3,144,384]{2,1,0:T(8,128)S(1)} %get-tuple-element.18.near_ref, f32[3,384]{1,0:T(4,128)S(1)} %copy-done.4, bf16[72,384]{1,0:T(8,128)(2,1)S(1)} %collective-permute-done.6.e3, bf16[72,384]{1,0:T(8,128)(2,1)S(1)} %collective-permute-done.7.e2, ...), custom_call_target="tpu_custom_call" | custom-call | flops 1000000 | bytes 4000000 | tf_op jit(solution)/shard_map/pallas_call | solution.py:131
  (7 shorter events, 0.2 us)
Async XLA Ops:
  0.0 1.1 %copy-start = (bf16[3,2,144,384]{3,2,1,0:T(8,128)(2,1)S(1)}, bf16[3,2,144,384]{3,2,1,0:T(8,128)(2,1)}, u32[]{:S(2)}) copy-start(bf16[3,2,144,384]{3,2,1,0:T(8,128)(2,1)} %param.7) | copy-start | bytes 1990660
  0.0 4.4 %copy-start.5 = (s32[4,3,2,144]{3,2,1,0:T(2,128)S(1)}, s32[4,3,2,144]{3,2,1,0:T(2,128)}, u32[]{:S(2)}) copy-start(s32[4,3,2,144]{3,2,1,0:T(2,128)} %mask_ref.1) | copy-start | bytes 41476
  1.1 8.5 %collective-permute-start.1 = (bf16[3,144,384]{2,1,0:T(8,128)(2,1)S(1)}, bf16[3,144,384]{2,1,0:T(8,128)(2,1)S(1)}, u32[]{:S(2)}, u32[]{:S(2)}) collective-permute-start(bf16[3,144,384]{2,1,0:T(8,128)(2,1)S(1)} %dynamic-slice_bitcast_fusion.1.after.near_row), channel_id=1, source_target_pairs={{0,4},{1,2},{2,1},{3,7},{4,0},{5,6},{6,5},{7,3},{8,12},{9,10},{10,... | collective-permute-start | bytes 995336 | tf_op jit(solution)/shard_map/ppermute | solution.py:161
  4.2 1.8 %copy-start.1 = (bf16[3,2,384,384]{3,2,1,0:T(8,128)(2,1)S(1)}, bf16[3,2,384,384]{3,2,1,0:T(8,128)(2,1)}, u32[]{:S(2)}) copy-start(bf16[3,2,384,384]{3,2,1,0:T(8,128)(2,1)} %inverse.1) | copy-start | bytes 5308420
  4.2 1.8 %copy-start.2 = (bf16[4,384,384]{2,1,0:T(8,128)(2,1)S(1)}, bf16[4,384,384]{2,1,0:T(8,128)(2,1)}, u32[]{:S(2)}) copy-start(bf16[4,384,384]{2,1,0:T(8,128)(2,1)} %lift.1) | copy-start | bytes 3538948
  4.2 2.0 %copy-start.3 = (bf16[3,2,144,384]{3,2,1,0:T(8,128)(2,1)S(1)}, bf16[3,2,144,384]{3,2,1,0:T(8,128)(2,1)}, u32[]{:S(2)}) copy-start(bf16[3,2,144,384]{3,2,1,0:T(8,128)(2,1)} %forcing.1) | copy-start | bytes 1990660
  4.2 1.9 %copy-start.4 = (f32[3,384]{1,0:T(4,128)S(1)}, f32[3,384]{1,0:T(4,128)}, u32[]{:S(2)}) copy-start(f32[3,384]{1,0:T(4,128)} %keep_ref.5) | copy-start | bytes 13828
  4.2 1.7 %collective-permute-start = (bf16[3,144,384]{2,1,0:T(8,128)(2,1)S(1)}, bf16[3,144,384]{2,1,0:T(8,128)(2,1)S(1)}, u32[]{:S(2)}, u32[]{:S(2)}) collective-permute-start(bf16[3,144,384]{2,1,0:T(8,128)(2,1)S(1)} %dynamic-slice_bitcast_fusion.far_row), channel_id=1, source_target_pairs={{0,1},{1,0},{2,3},{3,2},{4,5},{5,4},{6,7},{7,6},{8,9},{9,8},{10,11... | collective-permute-start | bytes 995336 | tf_op jit(solution)/shard_map/ppermute | solution.py:162
  10.3 5.5 %collective-permute-start.2 = (bf16[80,384]{1,0:T(8,128)(2,1)S(1)}, bf16[80,384]{1,0:T(8,128)(2,1)S(1)}, u32[]{:S(2)}, u32[]{:S(2)}) collective-permute-start(bf16[80,384]{1,0:T(8,128)(2,1)S(1)} %get-tuple-element.19), channel_id=1, source_target_pairs={{0,12},{4,8},{8,4},{12,0},{16,28},{20,24},{24,20},{28,16},{1,13},{... | collective-permute-start | bytes 184328 | tf_op jit(solution)/shard_map/ppermute | solution.py:190
  13.0 4.2 %collective-permute-start.3 = (bf16[80,384]{1,0:T(8,128)(2,1)S(1)}, bf16[80,384]{1,0:T(8,128)(2,1)S(1)}, u32[]{:S(2)}, u32[]{:S(2)}) collective-permute-start(bf16[80,384]{1,0:T(8,128)(2,1)S(1)} %get-tuple-element.20), channel_id=1, source_target_pairs={{0,8},{4,12},{8,0},{12,4},{16,24},{20,28},{24,16},{28,20},{1,9},{5... | collective-permute-start | bytes 184328 | tf_op jit(solution)/shard_map/ppermute | solution.py:190
  13.5 4.2 %collective-permute-start.4 = (bf16[80,384]{1,0:T(8,128)(2,1)S(1)}, bf16[80,384]{1,0:T(8,128)(2,1)S(1)}, u32[]{:S(2)}, u32[]{:S(2)}) collective-permute-start(bf16[80,384]{1,0:T(8,128)(2,1)S(1)} %get-tuple-element.21), channel_id=1, source_target_pairs={{0,4},{4,0},{8,12},{12,8},{16,20},{20,16},{24,28},{28,24},{1,5},{5... | collective-permute-start | bytes 184328 | tf_op jit(solution)/shard_map/ppermute | solution.py:190
  17.8 5.1 %collective-permute-start.5 = (bf16[72,384]{1,0:T(8,128)(2,1)S(1)}, bf16[72,384]{1,0:T(8,128)(2,1)S(1)}, u32[]{:S(2)}, u32[]{:S(2)}) collective-permute-start(bf16[72,384]{1,0:T(8,128)(2,1)S(1)} %fusion), channel_id=1, source_target_pairs={{0,16},{4,20},{8,24},{12,28},{16,0},{20,4},{24,8},{28,12},{1,17},{... | collective-permute-start | bytes 165896 | tf_op jit(solution)/shard_map/ppermute | solution.py:190
  23.1 5.1 %collective-permute-start.6 = (bf16[72,384]{1,0:T(8,128)(2,1)S(1)}, bf16[72,384]{1,0:T(8,128)(2,1)S(1)}, u32[]{:S(2)}, u32[]{:S(2)}) collective-permute-start(bf16[72,384]{1,0:T(8,128)(2,1)S(1)} %get-tuple-element.33), channel_id=1, source_target_pairs={{0,12},{4,8},{8,4},{12,0},{16,28},{20,24},{24,20},{28,16},{1,13},{... | collective-permute-start | bytes 165896 | tf_op jit(solution)/shard_map/ppermute | solution.py:190
  24.7 4.2 %collective-permute-start.7 = (bf16[72,384]{1,0:T(8,128)(2,1)S(1)}, bf16[72,384]{1,0:T(8,128)(2,1)S(1)}, u32[]{:S(2)}, u32[]{:S(2)}) collective-permute-start(bf16[72,384]{1,0:T(8,128)(2,1)S(1)} %get-tuple-element.32), channel_id=1, source_target_pairs={{0,8},{4,12},{8,0},{12,4},{16,24},{20,28},{24,16},{28,20},{1,9},{5... | collective-permute-start | bytes 165896 | tf_op jit(solution)/shard_map/ppermute | solution.py:190
  25.0 4.2 %collective-permute-start.8 = (bf16[72,384]{1,0:T(8,128)(2,1)S(1)}, bf16[72,384]{1,0:T(8,128)(2,1)S(1)}, u32[]{:S(2)}, u32[]{:S(2)}) collective-permute-start(bf16[72,384]{1,0:T(8,128)(2,1)S(1)} %get-tuple-element.31), channel_id=1, source_target_pairs={{0,4},{4,0},{8,12},{12,8},{16,20},{20,16},{24,28},{28,24},{1,5},{5... | collective-permute-start | bytes 165896 | tf_op jit(solution)/shard_map/ppermute | solution.py:190

commit v6 on v5

--- a/solution.py
+++ b/solution.py
@@ -204,19 +204,15 @@
     before, before_factor = jnp.zeros_like(total), jnp.ones_like(total_factor)
     distance = GROUP
     while distance < streams:
-        last = 2 * distance >= streams
-        if last:
-            met = swap(total.astype(BF16), distance).astype(F32)
+        later = (stream & distance) != 0
+        if streams == 2 * GROUP:
+            before = jnp.where(later, swap(total.astype(BF16), distance).astype(F32), before)
         else:
-            high = total_factor.astype(BF16)
-            low = (total_factor - high.astype(F32)).astype(BF16)
-            met = swap(jnp.concatenate([total.astype(BF16), high, low], axis=0), distance).astype(F32)
-        later = (stream & distance) != 0
-        before = jnp.where(later, before_factor * met[:piece] + before, before)
-        if not last:
-            met_factor = met[piece : piece + 1] + met[piece + 1 : piece + 2]
+            met = swap(jnp.concatenate([total, total_factor], axis=0), distance)
+            met, met_factor = met[:piece], met[piece:]
+            before = jnp.where(later, before_factor * met + before, before)
             before_factor = jnp.where(later, before_factor * met_factor, before_factor)
-            total = jnp.where(later, total_factor * met[:piece] + total, met_factor * total + met[:piece])
+            total = jnp.where(later, total_factor * met + total, met_factor * total + met)
             total_factor = total_factor * met_factor
         distance *= 2
 

time: 30.5 us -> 30.5 us (level)
  no operation moved by 1% of the time
where the time goes in v6:
time: 30.5 us; the launch traced here: 30.3 us
  starting transfers between devices  12.9 us (42%)
  waiting for transfers between devices  10.3 us (34%)
  Pallas kernels  5.36 us (18%)
  local copies, waits for them, and re-layouts  1.41 us (5%)
    ppermute x7, starting transfers between devices, swap(): lax.ppermute(part, 'stream', [(i, i ^ distance) for i in range(streams)])  9.76 us
    ppermute x7, waiting for transfers between devices, swap(): lax.ppermute(part, 'stream', [(i, i ^ distance) for i in range(streams)])  8.85 us
    pallas_call x4, Pallas kernels, call(): pl.pallas_call(kernel, out_shape=outs, in_specs=in_specs, out_specs=out_s...  5.36 us
    ppermute x1, starting transfers between devices, body(): chip_halo = lax.ppermute(near_row, ('stream', 'cross'), links)  3.03 us
    ppermute x1, waiting for transfers between devices, body(): lax.ppermute(far_row, 'cross', [(i, i ^ 1) for i in range(crosses)])  1.41 us
    unnamed x12, local copies, waits for them, and re-layouts  1.34 us
  transfers between devices with their start and end apart: 9, of which 8 were waited for; matrix products, arithmetic and copies ran while one was open for 0% of the time, Pallas kernels for 12%

profile of v6, /device:TPU:0, one launch (start us, length us, event | category | flops | bytes accessed | tf_op | source)
XLA Modules:
  0.0 30.3 jit_solution(5517358122491864898)
XLA Ops:
  0.0 0.0 copy-start
  0.0 0.0 copy-start.5
  0.0 1.1 %copy-done = bf16[3,2,144,384]{3,2,1,0:T(8,128)(2,1)S(1)} copy-done((bf16[3,2,144,384]{3,2,1,0:T(8,128)(2,1)S(1)}, bf16[3,2,144,384]{3,2,1,0:T(8,128)(2,1)}, u32[]{:S(2)}) %copy-start) | copy-done | bytes 663576
  1.1 3.0 %collective-permute-start.1 = (bf16[3,144,384]{2,1,0:T(8,128)(2,1)S(1)}, bf16[3,144,384]{2,1,0:T(8,128)(2,1)S(1)}, u32[]{:S(2)}, u32[]{:S(2)}) collective-permute-start(bf16[3,144,384]{2,1,0:T(8,128)(2,1)S(1)} %dynamic-slice_bitcast_fusion.1.after.near_row), channel_id=1, source_target_pairs={{0,4},{1,2},{2,1},{3,7},{4,0},{5,6},{6,5},{7,3},{8,12},{9,10},{10,... | collective-permute-start | bytes 995336 | tf_op jit(solution)/shard_map/ppermute | solution.py:161
  4.2 0.0 copy-start.1
  4.2 0.0 copy-start.2
  4.2 0.0 copy-start.3
  4.2 0.0 copy-start.4
  4.2 0.2 collective-permute-start
  4.4 0.0 copy-done.5
  4.4 0.1 shard_map.64.columns_ref
  4.5 1.4 %collective-permute-done.halo_ref = bf16[3,144,384]{2,1,0:T(8,128)(2,1)S(1)} collective-permute-done((bf16[3,144,384]{2,1,0:T(8,128)(2,1)S(1)}, bf16[3,144,384]{2,1,0:T(8,128)(2,1)S(1)}, u32[]{:S(2)}, u32[]{:S(2)}) %collective-permute-start) | collective-permute-done | bytes 331808 | tf_op jit(solution)/shard_map/ppermute | solution.py:162
  5.9 0.0 copy-done.1
  6.0 0.1 copy-done.2
  6.0 0.2 copy-done.3
  6.2 0.0 copy-done.4
  6.2 3.4 %shard_map.65 = (f32[3,144,384]{2,1,0:T(8,128)S(1)}, f32[3,144,384]{2,1,0:T(8,128)S(1)}, bf16[3,384,384]{2,1,0:T(8,128)(2,1)S(1)}) custom-call(f32[3,144,128]{2,1,0:T(8,128)S(1)} %shard_map.64.columns_ref, bf16[3,144,384]{2,1,0:T(8,128)(2,1)S(1)} %collective-permute-done.halo_ref, f32[3,384]{1,0:T(4,128)S(1)} %copy-done.4, ...), custom_call_target="tpu_custom_call" | custom-call | flops 1146617856 | bytes 5000000 | tf_op jit(solution)/shard_map/pallas_call | solution.py:131
  9.6 0.0 collective-permute-done.1.halo_ref
  9.6 0.6 %shard_map.66 = (f32[3,144,384]{2,1,0:T(8,128)S(1)}, bf16[80,384]{1,0:T(8,128)(2,1)S(1)}, bf16[80,384]{1,0:T(8,128)(2,1)S(1)}, bf16[80,384]{1,0:T(8,128)(2,1)S(1)}, bf16[80,384]{1,0:T(8,128)(2,1)S(1)}) custom-call(bf16[3,144,384]{2,1,0:T(8,128)(2,1)S(1)} %collective-permute-done.1.halo_ref, f32[3,144,128]{2,1,0:T(8,128)S(1)} %shard_map.64.columns_ref, ...), custom_call_target="tpu_custom_call" | custom-call | flops 254803968 | bytes 3000000 | tf_op jit(solution)/shard_map/pallas_call | solution.py:131
  10.3 2.8 %collective-permute-start.2 = (bf16[80,384]{1,0:T(8,128)(2,1)S(1)}, bf16[80,384]{1,0:T(8,128)(2,1)S(1)}, u32[]{:S(2)}, u32[]{:S(2)}) collective-permute-start(bf16[80,384]{1,0:T(8,128)(2,1)S(1)} %get-tuple-element.19), channel_id=1, source_target_pairs={{0,12},{4,8},{8,4},{12,0},{16,28},{20,24},{24,20},{28,16},{1,13},{... | collective-permute-start | bytes 184328 | tf_op jit(solution)/shard_map/ppermute | solution.py:190
  13.0 0.4 %collective-permute-start.3 = (bf16[80,384]{1,0:T(8,128)(2,1)S(1)}, bf16[80,384]{1,0:T(8,128)(2,1)S(1)}, u32[]{:S(2)}, u32[]{:S(2)}) collective-permute-start(bf16[80,384]{1,0:T(8,128)(2,1)S(1)} %get-tuple-element.20), channel_id=1, source_target_pairs={{0,8},{4,12},{8,0},{12,4},{16,24},{20,28},{24,16},{28,20},{1,9},{5... | collective-permute-start | bytes 184328 | tf_op jit(solution)/shard_map/ppermute | solution.py:190
  13.5 0.4 %collective-permute-start.4 = (bf16[80,384]{1,0:T(8,128)(2,1)S(1)}, bf16[80,384]{1,0:T(8,128)(2,1)S(1)}, u32[]{:S(2)}, u32[]{:S(2)}) collective-permute-start(bf16[80,384]{1,0:T(8,128)(2,1)S(1)} %get-tuple-element.21), channel_id=1, source_target_pairs={{0,4},{4,0},{8,12},{12,8},{16,20},{20,16},{24,28},{28,24},{1,5},{5... | collective-permute-start | bytes 184328 | tf_op jit(solution)/shard_map/ppermute | solution.py:190
  13.8 2.0 %collective-permute-done.2 = bf16[80,384]{1,0:T(8,128)(2,1)S(1)} collective-permute-done((bf16[80,384]{1,0:T(8,128)(2,1)S(1)}, bf16[80,384]{1,0:T(8,128)(2,1)S(1)}, u32[]{:S(2)}, u32[]{:S(2)}) %collective-permute-start.2) | collective-permute-done | bytes 61472 | tf_op jit(solution)/shard_map/ppermute | solution.py:190
  15.8 1.5 %collective-permute-done.3 = bf16[80,384]{1,0:T(8,128)(2,1)S(1)} collective-permute-done((bf16[80,384]{1,0:T(8,128)(2,1)S(1)}, bf16[80,384]{1,0:T(8,128)(2,1)S(1)}, u32[]{:S(2)}, u32[]{:S(2)}) %collective-permute-start.3) | collective-permute-done | bytes 61472 | tf_op jit(solution)/shard_map/ppermute | solution.py:190
  17.2 0.4 %collective-permute-done.4 = bf16[80,384]{1,0:T(8,128)(2,1)S(1)} collective-permute-done((bf16[80,384]{1,0:T(8,128)(2,1)S(1)}, bf16[80,384]{1,0:T(8,128)(2,1)S(1)}, u32[]{:S(2)}, u32[]{:S(2)}) %collective-permute-start.4) | collective-permute-done | bytes 61472 | tf_op jit(solution)/shard_map/ppermute | solution.py:190
  17.7 0.1 select_convert_fusion.1
  17.8 2.7 %collective-permute-start.5 = (bf16[72,384]{1,0:T(8,128)(2,1)S(1)}, bf16[72,384]{1,0:T(8,128)(2,1)S(1)}, u32[]{:S(2)}, u32[]{:S(2)}) collective-permute-start(bf16[72,384]{1,0:T(8,128)(2,1)S(1)} %fusion), channel_id=1, source_target_pairs={{0,16},{4,20},{8,24},{12,28},{16,0},{20,4},{24,8},{28,12},{1,17},{... | collective-permute-start | bytes 165896 | tf_op jit(solution)/shard_map/ppermute | solution.py:190
  20.5 2.4 %collective-permute-done.5 = bf16[72,384]{1,0:T(8,128)(2,1)S(1)} collective-permute-done((bf16[72,384]{1,0:T(8,128)(2,1)S(1)}, bf16[72,384]{1,0:T(8,128)(2,1)S(1)}, u32[]{:S(2)}, u32[]{:S(2)}) %collective-permute-start.5) | collective-permute-done | bytes 55328 | tf_op jit(solution)/shard_map/ppermute | solution.py:190
  22.9 0.1 select_select_fusion
  23.1 1.6 %collective-permute-start.6 = (bf16[72,384]{1,0:T(8,128)(2,1)S(1)}, bf16[72,384]{1,0:T(8,128)(2,1)S(1)}, u32[]{:S(2)}, u32[]{:S(2)}) collective-permute-start(bf16[72,384]{1,0:T(8,128)(2,1)S(1)} %get-tuple-element.33), channel_id=1, source_target_pairs={{0,12},{4,8},{8,4},{12,0},{16,28},{20,24},{24,20},{28,16},{1,13},{... | collective-permute-start | bytes 165896 | tf_op jit(solution)/shard_map/ppermute | solution.py:190
  24.7 0.4 %collective-permute-start.7 = (bf16[72,384]{1,0:T(8,128)(2,1)S(1)}, bf16[72,384]{1,0:T(8,128)(2,1)S(1)}, u32[]{:S(2)}, u32[]{:S(2)}) collective-permute-start(bf16[72,384]{1,0:T(8,128)(2,1)S(1)} %get-tuple-element.32), channel_id=1, source_target_pairs={{0,8},{4,12},{8,0},{12,4},{16,24},{20,28},{24,16},{28,20},{1,9},{5... | collective-permute-start | bytes 165896 | tf_op jit(solution)/shard_map/ppermute | solution.py:190
  25.0 1.6 %collective-permute-start.8 = (bf16[72,384]{1,0:T(8,128)(2,1)S(1)}, bf16[72,384]{1,0:T(8,128)(2,1)S(1)}, u32[]{:S(2)}, u32[]{:S(2)}) collective-permute-start(bf16[72,384]{1,0:T(8,128)(2,1)S(1)} %get-tuple-element.31), channel_id=1, source_target_pairs={{0,4},{4,0},{8,12},{12,8},{16,20},{20,16},{24,28},{28,24},{1,5},{5... | collective-permute-start | bytes 165896 | tf_op jit(solution)/shard_map/ppermute | solution.py:190
  26.6 1.6 %collective-permute-done.6.e3 = bf16[72,384]{1,0:T(8,128)(2,1)S(1)} collective-permute-done((bf16[72,384]{1,0:T(8,128)(2,1)S(1)}, bf16[72,384]{1,0:T(8,128)(2,1)S(1)}, u32[]{:S(2)}, u32[]{:S(2)}) %collective-permute-start.6) | collective-permute-done | bytes 55328 | tf_op jit(solution)/shard_map/ppermute | solution.py:190
  28.2 0.6 %collective-permute-done.7.e2 = bf16[72,384]{1,0:T(8,128)(2,1)S(1)} collective-permute-done((bf16[72,384]{1,0:T(8,128)(2,1)S(1)}, bf16[72,384]{1,0:T(8,128)(2,1)S(1)}, u32[]{:S(2)}, u32[]{:S(2)}) %collective-permute-start.7) | collective-permute-done | bytes 55328 | tf_op jit(solution)/shard_map/ppermute | solution.py:190
  28.8 0.4 %collective-permute-done.8.e1 = bf16[72,384]{1,0:T(8,128)(2,1)S(1)} collective-permute-done((bf16[72,384]{1,0:T(8,128)(2,1)S(1)}, bf16[72,384]{1,0:T(8,128)(2,1)S(1)}, u32[]{:S(2)}, u32[]{:S(2)}) %collective-permute-start.8) | collective-permute-done | bytes 55328 | tf_op jit(solution)/shard_map/ppermute | solution.py:190
  29.2 1.2 %shard_map.67 = f32[3,2,144,384]{3,2,1,0:T(8,128)} custom-call(f32[3,144,384]{2,1,0:T(8,128)S(1)} %get-tuple-element.15.far_ref, f32[3,144,384]{2,1,0:T(8,128)S(1)} %get-tuple-element.18.near_ref, f32[3,384]{1,0:T(4,128)S(1)} %copy-done.4, bf16[72,384]{1,0:T(8,128)(2,1)S(1)} %collective-permute-done.6.e3, bf16[72,384]{1,0:T(8,128)(2,1)S(1)} %collective-permute-done.7.e2, ...), custom_call_target="tpu_custom_call" | custom-call | flops 1000000 | bytes 4000000 | tf_op jit(solution)/shard_map/pallas_call | solution.py:131
  (7 shorter events, 0.2 us)
Async XLA Ops:
  0.0 1.1 %copy-start = (bf16[3,2,144,384]{3,2,1,0:T(8,128)(2,1)S(1)}, bf16[3,2,144,384]{3,2,1,0:T(8,128)(2,1)}, u32[]{:S(2)}) copy-start(bf16[3,2,144,384]{3,2,1,0:T(8,128)(2,1)} %param.7) | copy-start | bytes 1990660
  0.0 4.4 %copy-start.5 = (s32[4,3,2,144]{3,2,1,0:T(2,128)S(1)}, s32[4,3,2,144]{3,2,1,0:T(2,128)}, u32[]{:S(2)}) copy-start(s32[4,3,2,144]{3,2,1,0:T(2,128)} %mask_ref.1) | copy-start | bytes 41476
  1.1 8.5 %collective-permute-start.1 = (bf16[3,144,384]{2,1,0:T(8,128)(2,1)S(1)}, bf16[3,144,384]{2,1,0:T(8,128)(2,1)S(1)}, u32[]{:S(2)}, u32[]{:S(2)}) collective-permute-start(bf16[3,144,384]{2,1,0:T(8,128)(2,1)S(1)} %dynamic-slice_bitcast_fusion.1.after.near_row), channel_id=1, source_target_pairs={{0,4},{1,2},{2,1},{3,7},{4,0},{5,6},{6,5},{7,3},{8,12},{9,10},{10,... | collective-permute-start | bytes 995336 | tf_op jit(solution)/shard_map/ppermute | solution.py:161
  4.2 1.8 %copy-start.1 = (bf16[3,2,384,384]{3,2,1,0:T(8,128)(2,1)S(1)}, bf16[3,2,384,384]{3,2,1,0:T(8,128)(2,1)}, u32[]{:S(2)}) copy-start(bf16[3,2,384,384]{3,2,1,0:T(8,128)(2,1)} %inverse.1) | copy-start | bytes 5308420
  4.2 1.8 %copy-start.2 = (bf16[4,384,384]{2,1,0:T(8,128)(2,1)S(1)}, bf16[4,384,384]{2,1,0:T(8,128)(2,1)}, u32[]{:S(2)}) copy-start(bf16[4,384,384]{2,1,0:T(8,128)(2,1)} %lift.1) | copy-start | bytes 3538948
  4.2 2.0 %copy-start.3 = (bf16[3,2,144,384]{3,2,1,0:T(8,128)(2,1)S(1)}, bf16[3,2,144,384]{3,2,1,0:T(8,128)(2,1)}, u32[]{:S(2)}) copy-start(bf16[3,2,144,384]{3,2,1,0:T(8,128)(2,1)} %forcing.1) | copy-start | bytes 1990660
  4.2 1.9 %copy-start.4 = (f32[3,384]{1,0:T(4,128)S(1)}, f32[3,384]{1,0:T(4,128)}, u32[]{:S(2)}) copy-start(f32[3,384]{1,0:T(4,128)} %keep_ref.5) | copy-start | bytes 13828
  4.2 1.7 %collective-permute-start = (bf16[3,144,384]{2,1,0:T(8,128)(2,1)S(1)}, bf16[3,144,384]{2,1,0:T(8,128)(2,1)S(1)}, u32[]{:S(2)}, u32[]{:S(2)}) collective-permute-start(bf16[3,144,384]{2,1,0:T(8,128)(2,1)S(1)} %dynamic-slice_bitcast_fusion.far_row), channel_id=1, source_target_pairs={{0,1},{1,0},{2,3},{3,2},{4,5},{5,4},{6,7},{7,6},{8,9},{9,8},{10,11... | collective-permute-start | bytes 995336 | tf_op jit(solution)/shard_map/ppermute | solution.py:162
  10.3 5.5 %collective-permute-start.2 = (bf16[80,384]{1,0:T(8,128)(2,1)S(1)}, bf16[80,384]{1,0:T(8,128)(2,1)S(1)}, u32[]{:S(2)}, u32[]{:S(2)}) collective-permute-start(bf16[80,384]{1,0:T(8,128)(2,1)S(1)} %get-tuple-element.19), channel_id=1, source_target_pairs={{0,12},{4,8},{8,4},{12,0},{16,28},{20,24},{24,20},{28,16},{1,13},{... | collective-permute-start | bytes 184328 | tf_op jit(solution)/shard_map/ppermute | solution.py:190
  13.0 4.2 %collective-permute-start.3 = (bf16[80,384]{1,0:T(8,128)(2,1)S(1)}, bf16[80,384]{1,0:T(8,128)(2,1)S(1)}, u32[]{:S(2)}, u32[]{:S(2)}) collective-permute-start(bf16[80,384]{1,0:T(8,128)(2,1)S(1)} %get-tuple-element.20), channel_id=1, source_target_pairs={{0,8},{4,12},{8,0},{12,4},{16,24},{20,28},{24,16},{28,20},{1,9},{5... | collective-permute-start | bytes 184328 | tf_op jit(solution)/shard_map/ppermute | solution.py:190
  13.5 4.2 %collective-permute-start.4 = (bf16[80,384]{1,0:T(8,128)(2,1)S(1)}, bf16[80,384]{1,0:T(8,128)(2,1)S(1)}, u32[]{:S(2)}, u32[]{:S(2)}) collective-permute-start(bf16[80,384]{1,0:T(8,128)(2,1)S(1)} %get-tuple-element.21), channel_id=1, source_target_pairs={{0,4},{4,0},{8,12},{12,8},{16,20},{20,16},{24,28},{28,24},{1,5},{5... | collective-permute-start | bytes 184328 | tf_op jit(solution)/shard_map/ppermute | solution.py:190
  17.8 5.1 %collective-permute-start.5 = (bf16[72,384]{1,0:T(8,128)(2,1)S(1)}, bf16[72,384]{1,0:T(8,128)(2,1)S(1)}, u32[]{:S(2)}, u32[]{:S(2)}) collective-permute-start(bf16[72,384]{1,0:T(8,128)(2,1)S(1)} %fusion), channel_id=1, source_target_pairs={{0,16},{4,20},{8,24},{12,28},{16,0},{20,4},{24,8},{28,12},{1,17},{... | collective-permute-start | bytes 165896 | tf_op jit(solution)/shard_map/ppermute | solution.py:190
  23.1 5.1 %collective-permute-start.6 = (bf16[72,384]{1,0:T(8,128)(2,1)S(1)}, bf16[72,384]{1,0:T(8,128)(2,1)S(1)}, u32[]{:S(2)}, u32[]{:S(2)}) collective-permute-start(bf16[72,384]{1,0:T(8,128)(2,1)S(1)} %get-tuple-element.33), channel_id=1, source_target_pairs={{0,12},{4,8},{8,4},{12,0},{16,28},{20,24},{24,20},{28,16},{1,13},{... | collective-permute-start | bytes 165896 | tf_op jit(solution)/shard_map/ppermute | solution.py:190
  24.7 4.2 %collective-permute-start.7 = (bf16[72,384]{1,0:T(8,128)(2,1)S(1)}, bf16[72,384]{1,0:T(8,128)(2,1)S(1)}, u32[]{:S(2)}, u32[]{:S(2)}) collective-permute-start(bf16[72,384]{1,0:T(8,128)(2,1)S(1)} %get-tuple-element.32), channel_id=1, source_target_pairs={{0,8},{4,12},{8,0},{12,4},{16,24},{20,28},{24,16},{28,20},{1,9},{5... | collective-permute-start | bytes 165896 | tf_op jit(solution)/shard_map/ppermute | solution.py:190
  25.0 4.2 %collective-permute-start.8 = (bf16[72,384]{1,0:T(8,128)(2,1)S(1)}, bf16[72,384]{1,0:T(8,128)(2,1)S(1)}, u32[]{:S(2)}, u32[]{:S(2)}) collective-permute-start(bf16[72,384]{1,0:T(8,128)(2,1)S(1)} %get-tuple-element.31), channel_id=1, source_target_pairs={{0,4},{4,0},{8,12},{12,8},{16,20},{20,16},{24,28},{28,24},{1,5},{5... | collective-permute-start | bytes 165896 | tf_op jit(solution)/shard_map/ppermute | solution.py:190

commit v7 on v6

--- a/solution.py
+++ b/solution.py
@@ -107,33 +107,38 @@
         out[...] = jnp.concatenate([carry[pl.ds(start, piece), :], extra], axis=0).astype(BF16)
 
 
-def final_kernel(far_ref, near_ref, keep_ref, e3, e2, e1, e0, out_hbm, incoming, out, sem):
+def final_kernel(step, far_ref, near_ref, keep_ref, one, other, *rest):
+    out_hbm, out, sem = rest[-3:]
     layers, width, dofs = far_ref.shape
+    piece = one.shape[0]
     odd = lax.axis_index("cross") & 1
-    piece = e0.shape[0]
     member = lax.axis_index("stream") & (GROUP - 1)
-    for k, part in enumerate((e0, e1, e2, e3)):
-        start = pl.multiple_of((member ^ k) * piece, 8)
-        incoming[pl.ds(start, piece), :] = part[...].astype(F32)
+    low = member < 2
+    at = jnp.where(low, member, 3 - member) if step == 0 else jnp.where(low, 1 - member, member - 2)
+    entering = [part[...].astype(F32) for part in (one, other)]
+    entering = (jnp.where(low, entering[0], entering[1]), jnp.where(low, entering[1], entering[0]))
+    starts = (pl.multiple_of(at * piece, 8), pl.multiple_of((1 - at) * piece, 8))
     copies = []
     factor = None
     for l in range(layers):
         factor = keep_ref[l : l + 1, :] if l == 0 else factor * keep_ref[l : l + 1, :]
-        out[l, 1 - odd] = far_ref[l] + factor * incoming[pl.ds(0, width), :]
-        out[l, odd] = near_ref[l] + factor * incoming[pl.ds(width, width), :]
-        copies.append(pltpu.make_async_copy(out.at[l], out_hbm.at[l], sem.at[l]))
-        copies[-1].start()
+        for i, (part, row) in enumerate(((far_ref, 1 - odd), (near_ref, odd))):
+            span = pl.ds(starts[i], piece)
+            out[l, i] = part[l, span, :] + factor * entering[i]
+            copies.append(pltpu.make_async_copy(out.at[l, i], out_hbm.at[l, row, span, :], sem.at[l, i]))
+            copies[-1].start()
     for copy in copies:
         copy.wait()
 
 
-def call(kernel, operands, in_specs, outs, out_specs, scratch, flops, moved):
+def call(kernel, operands, in_specs, outs, out_specs, scratch, flops, moved, aliases={}):
     return pl.pallas_call(
         kernel,
         out_shape=outs,
         in_specs=in_specs,
         out_specs=out_specs,
         scratch_shapes=scratch,
+        input_output_aliases=aliases,
         compiler_params=pltpu.CompilerParams(vmem_limit_bytes=VMEM_LIMIT),
         cost_estimate=pl.CostEstimate(flops=flops, bytes_accessed=moved, transcendentals=0),
     )(*operands)
@@ -223,15 +228,21 @@
     give = [pick(entering, k) for k in range(GROUP)]
     back = [give[0]] + [swap(give[k], k) for k in range(1, GROUP)]
 
+    result = like(cells.shape, F32)
+    scratch = [pltpu.VMEM((layers, 2, piece, dofs), F32), pltpu.SemaphoreType.DMA((layers, 2))]
+    half = call(
+        functools.partial(final_kernel, 0), (far, near, retention, back[0], back[3]), [vmem] * 5, result, hbm, scratch, 500_000, 2_000_000
+    )
     return call(
-        final_kernel,
-        (far, near, retention, *back[::-1]),
-        [vmem] * (3 + GROUP),
-        like(cells.shape, F32),
+        functools.partial(final_kernel, 1),
+        (far, near, retention, back[1], back[2], half),
+        [vmem] * 5 + [hbm],
+        result,
         hbm,
-        [pltpu.VMEM((2 * width, dofs), F32), pltpu.VMEM(cells.shape, F32), pltpu.SemaphoreType.DMA((layers,))],
-        1_000_000,
-        4_000_000,
+        scratch,
+        500_000,
+        2_000_000,
+        {5: 0},
     )
 
 

time: 30.5 us -> 30.3 us (level)
  waiting for transfers between devices: 10.3 us -> 9.33 us
  Pallas kernels: 5.36 us -> 6.03 us
    ppermute x7, waiting for transfers between devices: 8.85 us -> 7.92 us  [swap(): lax.ppermute(part, 'stream', [(i, i ^ distance) for i in range(streams)])]
    pallas_call x4 -> x5, Pallas kernels: 5.36 us -> 6.03 us  [call(): pl.pallas_call(kernel, out_shape=outs, in_specs=in_specs, out_specs=out_s...]
  transfers between devices with their start and end apart: 9 -> 9, of which waited for: 8 -> 7; matrix products, arithmetic and copies ran while one was open for 0% -> 0% of each run, Pallas kernels for 12% -> 15%
where the time goes in v7:
time: 30.3 us; the launch traced here: 30.2 us
  starting transfers between devices  13 us (43%)
  waiting for transfers between devices  9.33 us (31%)
  Pallas kernels  6.03 us (20%)
  local copies, waits for them, and re-layouts  1.41 us (5%)
    ppermute x7, starting transfers between devices, swap(): lax.ppermute(part, 'stream', [(i, i ^ distance) for i in range(streams)])  9.83 us
    ppermute x7, waiting for transfers between devices, swap(): lax.ppermute(part, 'stream', [(i, i ^ distance) for i in range(streams)])  7.92 us
    pallas_call x5, Pallas kernels, call(): pl.pallas_call(kernel, out_shape=outs, in_specs=in_specs, out_specs=out_s...  6.03 us
    ppermute x1, starting transfers between devices, body(): chip_halo = lax.ppermute(near_row, ('stream', 'cross'), links)  3.03 us
    ppermute x1, waiting for transfers between devices, body(): lax.ppermute(far_row, 'cross', [(i, i ^ 1) for i in range(crosses)])  1.41 us
    unnamed x12, local copies, waits for them, and re-layouts  1.34 us
  transfers between devices with their start and end apart: 9, of which 7 were waited for; matrix products, arithmetic and copies ran while one was open for 0% of the time, Pallas kernels for 15%

profile of v7, /device:TPU:0, one launch (start us, length us, event | category | flops | bytes accessed | tf_op | source)
XLA Modules:
  0.0 30.2 jit_solution(14627560905274380200)
XLA Ops:
  0.0 0.0 copy-start
  0.0 0.0 copy-start.5
  0.0 1.1 %copy-done = bf16[3,2,144,384]{3,2,1,0:T(8,128)(2,1)S(1)} copy-done((bf16[3,2,144,384]{3,2,1,0:T(8,128)(2,1)S(1)}, bf16[3,2,144,384]{3,2,1,0:T(8,128)(2,1)}, u32[]{:S(2)}) %copy-start) | copy-done | bytes 663576
  1.1 3.0 %collective-permute-start.1 = (bf16[3,144,384]{2,1,0:T(8,128)(2,1)S(1)}, bf16[3,144,384]{2,1,0:T(8,128)(2,1)S(1)}, u32[]{:S(2)}, u32[]{:S(2)}) collective-permute-start(bf16[3,144,384]{2,1,0:T(8,128)(2,1)S(1)} %dynamic-slice_bitcast_fusion.1.after.near_row), channel_id=1, source_target_pairs={{0,4},{1,2},{2,1},{3,7},{4,0},{5,6},{6,5},{7,3},{8,12},{9,10},{10,... | collective-permute-start | bytes 995336 | tf_op jit(solution)/shard_map/ppermute | solution.py:166
  4.2 0.0 copy-start.1
  4.2 0.0 copy-start.2
  4.2 0.0 copy-start.3
  4.2 0.0 copy-start.4
  4.2 0.2 collective-permute-start
  4.4 0.0 copy-done.5
  4.4 0.1 shard_map.64.columns_ref
  4.5 1.4 %collective-permute-done.halo_ref = bf16[3,144,384]{2,1,0:T(8,128)(2,1)S(1)} collective-permute-done((bf16[3,144,384]{2,1,0:T(8,128)(2,1)S(1)}, bf16[3,144,384]{2,1,0:T(8,128)(2,1)S(1)}, u32[]{:S(2)}, u32[]{:S(2)}) %collective-permute-start) | collective-permute-done | bytes 331808 | tf_op jit(solution)/shard_map/ppermute | solution.py:167
  5.9 0.0 copy-done.1
  6.0 0.1 copy-done.2
  6.0 0.2 copy-done.3
  6.2 0.0 copy-done.4
  6.2 3.4 %shard_map.65 = (f32[3,144,384]{2,1,0:T(8,128)S(1)}, f32[3,144,384]{2,1,0:T(8,128)S(1)}, bf16[3,384,384]{2,1,0:T(8,128)(2,1)S(1)}) custom-call(f32[3,144,128]{2,1,0:T(8,128)S(1)} %shard_map.64.columns_ref, bf16[3,144,384]{2,1,0:T(8,128)(2,1)S(1)} %collective-permute-done.halo_ref, f32[3,384]{1,0:T(4,128)S(1)} %copy-done.4, ...), custom_call_target="tpu_custom_call" | custom-call | flops 1146617856 | bytes 5000000 | tf_op jit(solution)/shard_map/pallas_call | solution.py:135
  9.6 0.0 collective-permute-done.1.halo_ref
  9.6 0.7 %shard_map.66 = (f32[3,144,384]{2,1,0:T(8,128)S(1)}, bf16[80,384]{1,0:T(8,128)(2,1)S(1)}, bf16[80,384]{1,0:T(8,128)(2,1)S(1)}, bf16[80,384]{1,0:T(8,128)(2,1)S(1)}, bf16[80,384]{1,0:T(8,128)(2,1)S(1)}) custom-call(bf16[3,144,384]{2,1,0:T(8,128)(2,1)S(1)} %collective-permute-done.1.halo_ref, f32[3,144,128]{2,1,0:T(8,128)S(1)} %shard_map.64.columns_ref, ...), custom_call_target="tpu_custom_call" | custom-call | flops 254803968 | bytes 3000000 | tf_op jit(solution)/shard_map/pallas_call | solution.py:135
  10.3 2.8 %collective-permute-start.2 = (bf16[80,384]{1,0:T(8,128)(2,1)S(1)}, bf16[80,384]{1,0:T(8,128)(2,1)S(1)}, u32[]{:S(2)}, u32[]{:S(2)}) collective-permute-start(bf16[80,384]{1,0:T(8,128)(2,1)S(1)} %get-tuple-element.19), channel_id=1, source_target_pairs={{0,12},{4,8},{8,4},{12,0},{16,28},{20,24},{24,20},{28,16},{1,13},{... | collective-permute-start | bytes 184328 | tf_op jit(solution)/shard_map/ppermute | solution.py:195
  13.0 0.4 %collective-permute-start.3 = (bf16[80,384]{1,0:T(8,128)(2,1)S(1)}, bf16[80,384]{1,0:T(8,128)(2,1)S(1)}, u32[]{:S(2)}, u32[]{:S(2)}) collective-permute-start(bf16[80,384]{1,0:T(8,128)(2,1)S(1)} %get-tuple-element.20), channel_id=1, source_target_pairs={{0,8},{4,12},{8,0},{12,4},{16,24},{20,28},{24,16},{28,20},{1,9},{5... | collective-permute-start | bytes 184328 | tf_op jit(solution)/shard_map/ppermute | solution.py:195
  13.5 0.4 %collective-permute-start.4 = (bf16[80,384]{1,0:T(8,128)(2,1)S(1)}, bf16[80,384]{1,0:T(8,128)(2,1)S(1)}, u32[]{:S(2)}, u32[]{:S(2)}) collective-permute-start(bf16[80,384]{1,0:T(8,128)(2,1)S(1)} %get-tuple-element.21), channel_id=1, source_target_pairs={{0,4},{4,0},{8,12},{12,8},{16,20},{20,16},{24,28},{28,24},{1,5},{5... | collective-permute-start | bytes 184328 | tf_op jit(solution)/shard_map/ppermute | solution.py:195
  13.8 2.0 %collective-permute-done.2 = bf16[80,384]{1,0:T(8,128)(2,1)S(1)} collective-permute-done((bf16[80,384]{1,0:T(8,128)(2,1)S(1)}, bf16[80,384]{1,0:T(8,128)(2,1)S(1)}, u32[]{:S(2)}, u32[]{:S(2)}) %collective-permute-start.2) | collective-permute-done | bytes 61472 | tf_op jit(solution)/shard_map/ppermute | solution.py:195
  15.8 1.5 %collective-permute-done.3 = bf16[80,384]{1,0:T(8,128)(2,1)S(1)} collective-permute-done((bf16[80,384]{1,0:T(8,128)(2,1)S(1)}, bf16[80,384]{1,0:T(8,128)(2,1)S(1)}, u32[]{:S(2)}, u32[]{:S(2)}) %collective-permute-start.3) | collective-permute-done | bytes 61472 | tf_op jit(solution)/shard_map/ppermute | solution.py:195
  17.2 0.4 %collective-permute-done.4 = bf16[80,384]{1,0:T(8,128)(2,1)S(1)} collective-permute-done((bf16[80,384]{1,0:T(8,128)(2,1)S(1)}, bf16[80,384]{1,0:T(8,128)(2,1)S(1)}, u32[]{:S(2)}, u32[]{:S(2)}) %collective-permute-start.4) | collective-permute-done | bytes 61472 | tf_op jit(solution)/shard_map/ppermute | solution.py:195
  17.7 0.1 select_convert_fusion.1
  17.8 2.7 %collective-permute-start.5 = (bf16[72,384]{1,0:T(8,128)(2,1)S(1)}, bf16[72,384]{1,0:T(8,128)(2,1)S(1)}, u32[]{:S(2)}, u32[]{:S(2)}) collective-permute-start(bf16[72,384]{1,0:T(8,128)(2,1)S(1)} %fusion), channel_id=1, source_target_pairs={{0,16},{4,20},{8,24},{12,28},{16,0},{20,4},{24,8},{28,12},{1,17},{... | collective-permute-start | bytes 165896 | tf_op jit(solution)/shard_map/ppermute | solution.py:195
  20.5 2.4 %collective-permute-done.5 = bf16[72,384]{1,0:T(8,128)(2,1)S(1)} collective-permute-done((bf16[72,384]{1,0:T(8,128)(2,1)S(1)}, bf16[72,384]{1,0:T(8,128)(2,1)S(1)}, u32[]{:S(2)}, u32[]{:S(2)}) %collective-permute-start.5) | collective-permute-done | bytes 55328 | tf_op jit(solution)/shard_map/ppermute | solution.py:195
  23.0 0.1 select_select_fusion
  23.0 1.6 %collective-permute-start.8 = (bf16[72,384]{1,0:T(8,128)(2,1)S(1)}, bf16[72,384]{1,0:T(8,128)(2,1)S(1)}, u32[]{:S(2)}, u32[]{:S(2)}) collective-permute-start(bf16[72,384]{1,0:T(8,128)(2,1)S(1)} %get-tuple-element.23), channel_id=1, source_target_pairs={{0,12},{4,8},{8,4},{12,0},{16,28},{20,24},{24,20},{28,16},{1,13},{... | collective-permute-start | bytes 165896 | tf_op jit(solution)/shard_map/ppermute | solution.py:195
  24.7 0.4 %collective-permute-start.7 = (bf16[72,384]{1,0:T(8,128)(2,1)S(1)}, bf16[72,384]{1,0:T(8,128)(2,1)S(1)}, u32[]{:S(2)}, u32[]{:S(2)}) collective-permute-start(bf16[72,384]{1,0:T(8,128)(2,1)S(1)} %get-tuple-element.32), channel_id=1, source_target_pairs={{0,8},{4,12},{8,0},{12,4},{16,24},{20,28},{24,16},{28,20},{1,9},{5... | collective-permute-start | bytes 165896 | tf_op jit(solution)/shard_map/ppermute | solution.py:195
  25.1 1.6 %collective-permute-start.6 = (bf16[72,384]{1,0:T(8,128)(2,1)S(1)}, bf16[72,384]{1,0:T(8,128)(2,1)S(1)}, u32[]{:S(2)}, u32[]{:S(2)}) collective-permute-start(bf16[72,384]{1,0:T(8,128)(2,1)S(1)} %get-tuple-element.33), channel_id=1, source_target_pairs={{0,4},{4,0},{8,12},{12,8},{16,20},{20,16},{24,28},{28,24},{1,5},{5... | collective-permute-start | bytes 165896 | tf_op jit(solution)/shard_map/ppermute | solution.py:195
  26.7 1.5 %collective-permute-done.8.other = bf16[72,384]{1,0:T(8,128)(2,1)S(1)} collective-permute-done((bf16[72,384]{1,0:T(8,128)(2,1)S(1)}, bf16[72,384]{1,0:T(8,128)(2,1)S(1)}, u32[]{:S(2)}, u32[]{:S(2)}) %collective-permute-start.8) | collective-permute-done | bytes 55328 | tf_op jit(solution)/shard_map/ppermute | solution.py:195
  28.1 0.9 %shard_map.67.rest_0_ = f32[3,2,144,384]{3,2,1,0:T(8,128)} custom-call(f32[3,144,384]{2,1,0:T(8,128)S(1)} %get-tuple-element.15.far_ref, f32[3,144,384]{2,1,0:T(8,128)S(1)} %get-tuple-element.18.near_ref, f32[3,384]{1,0:T(4,128)S(1)} %copy-done.4, bf16[72,384]{1,0:T(8,128)(2,1)S(1)} %get-tuple-element.31.one, bf16[72,384]{1,0:T(8,128)(2,1)S(1)} %collective-permute-done.8.other), custom_call_target="tpu_custom_call" | custom-call | flops 500000 | bytes 2000000 | tf_op jit(solution)/shard_map/pallas_call | solution.py:135
  29.1 0.0 collective-permute-done.7.other
  29.1 0.2 collective-permute-done.6.one
  29.2 0.9 %shard_map.68 = f32[3,2,144,384]{3,2,1,0:T(8,128)} custom-call(f32[3,144,384]{2,1,0:T(8,128)S(1)} %get-tuple-element.15.far_ref, f32[3,144,384]{2,1,0:T(8,128)S(1)} %get-tuple-element.18.near_ref, f32[3,384]{1,0:T(4,128)S(1)} %copy-done.4, bf16[72,384]{1,0:T(8,128)(2,1)S(1)} %collective-permute-done.6.one, ...), custom_call_target="tpu_custom_call", output_to_operand_aliasing={{}: (5, {})} | custom-call | flops 500000 | bytes 2000000 | tf_op jit(solution)/shard_map/pallas_call | solution.py:135
  (7 shorter events, 0.2 us)
Async XLA Ops:
  0.0 1.1 %copy-start = (bf16[3,2,144,384]{3,2,1,0:T(8,128)(2,1)S(1)}, bf16[3,2,144,384]{3,2,1,0:T(8,128)(2,1)}, u32[]{:S(2)}) copy-start(bf16[3,2,144,384]{3,2,1,0:T(8,128)(2,1)} %param.7) | copy-start | bytes 1990660
  0.0 4.4 %copy-start.5 = (s32[4,3,2,144]{3,2,1,0:T(2,128)S(1)}, s32[4,3,2,144]{3,2,1,0:T(2,128)}, u32[]{:S(2)}) copy-start(s32[4,3,2,144]{3,2,1,0:T(2,128)} %mask_ref.1) | copy-start | bytes 41476
  1.1 8.5 %collective-permute-start.1 = (bf16[3,144,384]{2,1,0:T(8,128)(2,1)S(1)}, bf16[3,144,384]{2,1,0:T(8,128)(2,1)S(1)}, u32[]{:S(2)}, u32[]{:S(2)}) collective-permute-start(bf16[3,144,384]{2,1,0:T(8,128)(2,1)S(1)} %dynamic-slice_bitcast_fusion.1.after.near_row), channel_id=1, source_target_pairs={{0,4},{1,2},{2,1},{3,7},{4,0},{5,6},{6,5},{7,3},{8,12},{9,10},{10,... | collective-permute-start | bytes 995336 | tf_op jit(solution)/shard_map/ppermute | solution.py:166
  4.2 1.8 %copy-start.1 = (bf16[3,2,384,384]{3,2,1,0:T(8,128)(2,1)S(1)}, bf16[3,2,384,384]{3,2,1,0:T(8,128)(2,1)}, u32[]{:S(2)}) copy-start(bf16[3,2,384,384]{3,2,1,0:T(8,128)(2,1)} %inverse.1) | copy-start | bytes 5308420
  4.2 1.8 %copy-start.2 = (bf16[4,384,384]{2,1,0:T(8,128)(2,1)S(1)}, bf16[4,384,384]{2,1,0:T(8,128)(2,1)}, u32[]{:S(2)}) copy-start(bf16[4,384,384]{2,1,0:T(8,128)(2,1)} %lift.1) | copy-start | bytes 3538948
  4.2 2.0 %copy-start.3 = (bf16[3,2,144,384]{3,2,1,0:T(8,128)(2,1)S(1)}, bf16[3,2,144,384]{3,2,1,0:T(8,128)(2,1)}, u32[]{:S(2)}) copy-start(bf16[3,2,144,384]{3,2,1,0:T(8,128)(2,1)} %forcing.1) | copy-start | bytes 1990660
  4.2 1.9 %copy-start.4 = (f32[3,384]{1,0:T(4,128)S(1)}, f32[3,384]{1,0:T(4,128)}, u32[]{:S(2)}) copy-start(f32[3,384]{1,0:T(4,128)} %keep_ref.7) | copy-start | bytes 13828
  4.2 1.7 %collective-permute-start = (bf16[3,144,384]{2,1,0:T(8,128)(2,1)S(1)}, bf16[3,144,384]{2,1,0:T(8,128)(2,1)S(1)}, u32[]{:S(2)}, u32[]{:S(2)}) collective-permute-start(bf16[3,144,384]{2,1,0:T(8,128)(2,1)S(1)} %dynamic-slice_bitcast_fusion.far_row), channel_id=1, source_target_pairs={{0,1},{1,0},{2,3},{3,2},{4,5},{5,4},{6,7},{7,6},{8,9},{9,8},{10,11... | collective-permute-start | bytes 995336 | tf_op jit(solution)/shard_map/ppermute | solution.py:167
  10.3 5.5 %collective-permute-start.2 = (bf16[80,384]{1,0:T(8,128)(2,1)S(1)}, bf16[80,384]{1,0:T(8,128)(2,1)S(1)}, u32[]{:S(2)}, u32[]{:S(2)}) collective-permute-start(bf16[80,384]{1,0:T(8,128)(2,1)S(1)} %get-tuple-element.19), channel_id=1, source_target_pairs={{0,12},{4,8},{8,4},{12,0},{16,28},{20,24},{24,20},{28,16},{1,13},{... | collective-permute-start | bytes 184328 | tf_op jit(solution)/shard_map/ppermute | solution.py:195
  13.0 4.2 %collective-permute-start.3 = (bf16[80,384]{1,0:T(8,128)(2,1)S(1)}, bf16[80,384]{1,0:T(8,128)(2,1)S(1)}, u32[]{:S(2)}, u32[]{:S(2)}) collective-permute-start(bf16[80,384]{1,0:T(8,128)(2,1)S(1)} %get-tuple-element.20), channel_id=1, source_target_pairs={{0,8},{4,12},{8,0},{12,4},{16,24},{20,28},{24,16},{28,20},{1,9},{5... | collective-permute-start | bytes 184328 | tf_op jit(solution)/shard_map/ppermute | solution.py:195
  13.5 4.2 %collective-permute-start.4 = (bf16[80,384]{1,0:T(8,128)(2,1)S(1)}, bf16[80,384]{1,0:T(8,128)(2,1)S(1)}, u32[]{:S(2)}, u32[]{:S(2)}) collective-permute-start(bf16[80,384]{1,0:T(8,128)(2,1)S(1)} %get-tuple-element.21), channel_id=1, source_target_pairs={{0,4},{4,0},{8,12},{12,8},{16,20},{20,16},{24,28},{28,24},{1,5},{5... | collective-permute-start | bytes 184328 | tf_op jit(solution)/shard_map/ppermute | solution.py:195
  17.8 5.1 %collective-permute-start.5 = (bf16[72,384]{1,0:T(8,128)(2,1)S(1)}, bf16[72,384]{1,0:T(8,128)(2,1)S(1)}, u32[]{:S(2)}, u32[]{:S(2)}) collective-permute-start(bf16[72,384]{1,0:T(8,128)(2,1)S(1)} %fusion), channel_id=1, source_target_pairs={{0,16},{4,20},{8,24},{12,28},{16,0},{20,4},{24,8},{28,12},{1,17},{... | collective-permute-start | bytes 165896 | tf_op jit(solution)/shard_map/ppermute | solution.py:195
  23.0 5.1 %collective-permute-start.8 = (bf16[72,384]{1,0:T(8,128)(2,1)S(1)}, bf16[72,384]{1,0:T(8,128)(2,1)S(1)}, u32[]{:S(2)}, u32[]{:S(2)}) collective-permute-start(bf16[72,384]{1,0:T(8,128)(2,1)S(1)} %get-tuple-element.23), channel_id=1, source_target_pairs={{0,12},{4,8},{8,4},{12,0},{16,28},{20,24},{24,20},{28,16},{1,13},{... | collective-permute-start | bytes 165896 | tf_op jit(solution)/shard_map/ppermute | solution.py:195
  24.7 4.4 %collective-permute-start.7 = (bf16[72,384]{1,0:T(8,128)(2,1)S(1)}, bf16[72,384]{1,0:T(8,128)(2,1)S(1)}, u32[]{:S(2)}, u32[]{:S(2)}) collective-permute-start(bf16[72,384]{1,0:T(8,128)(2,1)S(1)} %get-tuple-element.32), channel_id=1, source_target_pairs={{0,8},{4,12},{8,0},{12,4},{16,24},{20,28},{24,16},{28,20},{1,9},{5... | collective-permute-start | bytes 165896 | tf_op jit(solution)/shard_map/ppermute | solution.py:195
  25.1 4.2 %collective-permute-start.6 = (bf16[72,384]{1,0:T(8,128)(2,1)S(1)}, bf16[72,384]{1,0:T(8,128)(2,1)S(1)}, u32[]{:S(2)}, u32[]{:S(2)}) collective-permute-start(bf16[72,384]{1,0:T(8,128)(2,1)S(1)} %get-tuple-element.33), channel_id=1, source_target_pairs={{0,4},{4,0},{8,12},{12,8},{16,20},{20,16},{24,28},{28,24},{1,5},{5... | collective-permute-start | bytes 165896 | tf_op jit(solution)/shard_map/ppermute | solution.py:195

commit v8 on v7

--- a/solution.py
+++ b/solution.py
@@ -195,17 +195,31 @@
         return lax.ppermute(part, "stream", [(i, i ^ distance) for i in range(streams)])
 
     got = [piece0, swap(piece1, 1), swap(piece2, 2), swap(piece3, 3)]
-    pick = lambda parts, j: functools.reduce(
-        lambda rest, k: jnp.where((member ^ k) == j, parts[k], rest), range(1, GROUP), parts[0]
-    )
-    ordered = [pick(got, j).astype(F32) for j in range(GROUP)]
-    values = [part[:piece] for part in ordered]
-    factors = [part[piece : piece + 1] + part[piece + 1 : piece + 2] for part in ordered]
-
-    total, total_factor = values[0], factors[0]
-    for j in range(1, GROUP):
-        total = factors[j] * total + values[j]
-        total_factor = total_factor * factors[j]
+    even, low = member % 2 == 0, member < 2
+    order = lambda mine, partner: (jnp.where(even, mine, partner), jnp.where(even, partner, mine))
+
+    def unpack(part):
+        part = part.astype(F32)
+        return part[:piece], part[piece : piece + 1] + part[piece + 1 : piece + 2]
+
+    def join(first, second):
+        return second[1] * first[0] + second[0], first[1] * second[1]
+
+    theirs = [unpack(part) for part in order(got[2], got[3])]
+    *theirs_joined, partner = lax.optimization_barrier((*join(*theirs), got[1]))
+    ours = [unpack(part) for part in order(got[0], partner)]
+    ours_joined = join(*ours)
+    total = jnp.where(low, theirs_joined[1] * ours_joined[0] + theirs_joined[0], ours_joined[1] * theirs_joined[0] + ours_joined[0])
+    total_factor = ours_joined[1] * theirs_joined[1]
+
+    def enter(pair, ahead, goes_first):
+        own, share = jnp.where(goes_first, 0.0, ahead[0]), jnp.where(goes_first, 1.0, ahead[1])
+        value, factor = pair[0]
+        return zip(order(own, factor * own + value), order(share, factor * share))
+
+    entries = [*enter(theirs, ours_joined, ~low), *enter(ours, theirs_joined, low)]
+    entries = lax.optimization_barrier(entries)
+
     before, before_factor = jnp.zeros_like(total), jnp.ones_like(total_factor)
     distance = GROUP
     while distance < streams:
@@ -221,11 +235,7 @@
             total_factor = total_factor * met_factor
         distance *= 2
 
-    entering = [before]
-    for j in range(GROUP - 1):
-        entering.append(factors[j] * entering[j] + values[j])
-    entering = [part.astype(BF16) for part in entering]
-    give = [pick(entering, k) for k in range(GROUP)]
+    give = [(own + share * before).astype(BF16) for own, share in entries[2:] + entries[:2]]
     back = [give[0]] + [swap(give[k], k) for k in range(1, GROUP)]
 
     result = like(cells.shape, F32)

time: 30.3 us -> 30.2 us (level)
  transfers between devices with their start and end apart: 9 -> 9, of which waited for: 7 -> 6; matrix products, arithmetic and copies ran while one was open for 0% -> 1% of each run, Pallas kernels for 15% -> 15%
where the time goes in v8:
time: 30.2 us; the launch traced here: 30 us
  starting transfers between devices  12.9 us (43%)
  waiting for transfers between devices  9.13 us (30%)
  Pallas kernels  6.03 us (20%)
  local copies, waits for them, and re-layouts  1.41 us (5%)
  other arithmetic  0.39 us (1%)
    ppermute x7, starting transfers between devices, swap(): lax.ppermute(part, 'stream', [(i, i ^ distance) for i in range(streams)])  9.76 us
    ppermute x7, waiting for transfers between devices, swap(): lax.ppermute(part, 'stream', [(i, i ^ distance) for i in range(streams)])  7.72 us
    pallas_call x5, Pallas kernels, call(): pl.pallas_call(kernel, out_shape=outs, in_specs=in_specs, out_specs=out_s...  6.03 us
    ppermute x1, starting transfers between devices, body(): chip_halo = lax.ppermute(near_row, ('stream', 'cross'), links)  3.03 us
    ppermute x1, waiting for transfers between devices, body(): lax.ppermute(far_row, 'cross', [(i, i ^ 1) for i in range(crosses)])  1.41 us
    unnamed x12, local copies, waits for them, and re-layouts  1.34 us
  transfers between devices with their start and end apart: 9, of which 6 were waited for; matrix products, arithmetic and copies ran while one was open for 1% of the time, Pallas kernels for 15%

profile of v8, /device:TPU:0, one launch (start us, length us, event | category | flops | bytes accessed | tf_op | source)
XLA Modules:
  0.0 30.0 jit_solution(3561383668249953201)
XLA Ops:
  0.0 0.0 copy-start
  0.0 0.0 copy-start.5
  0.0 1.1 %copy-done = bf16[3,2,144,384]{3,2,1,0:T(8,128)(2,1)S(1)} copy-done((bf16[3,2,144,384]{3,2,1,0:T(8,128)(2,1)S(1)}, bf16[3,2,144,384]{3,2,1,0:T(8,128)(2,1)}, u32[]{:S(2)}) %copy-start) | copy-done | bytes 663576
  1.1 3.0 %collective-permute-start.1 = (bf16[3,144,384]{2,1,0:T(8,128)(2,1)S(1)}, bf16[3,144,384]{2,1,0:T(8,128)(2,1)S(1)}, u32[]{:S(2)}, u32[]{:S(2)}) collective-permute-start(bf16[3,144,384]{2,1,0:T(8,128)(2,1)S(1)} %dynamic-slice_bitcast_fusion.1.after.near_row), channel_id=1, source_target_pairs={{0,4},{1,2},{2,1},{3,7},{4,0},{5,6},{6,5},{7,3},{8,12},{9,10},{10,... | collective-permute-start | bytes 995336 | tf_op jit(solution)/shard_map/ppermute | solution.py:166
  4.2 0.0 copy-start.1
  4.2 0.0 copy-start.2
  4.2 0.0 copy-start.3
  4.2 0.0 copy-start.4
  4.2 0.2 collective-permute-start
  4.4 0.0 copy-done.5
  4.4 0.1 shard_map.64.columns_ref
  4.5 1.4 %collective-permute-done.halo_ref = bf16[3,144,384]{2,1,0:T(8,128)(2,1)S(1)} collective-permute-done((bf16[3,144,384]{2,1,0:T(8,128)(2,1)S(1)}, bf16[3,144,384]{2,1,0:T(8,128)(2,1)S(1)}, u32[]{:S(2)}, u32[]{:S(2)}) %collective-permute-start) | collective-permute-done | bytes 331808 | tf_op jit(solution)/shard_map/ppermute | solution.py:167
  5.9 0.0 copy-done.1
  6.0 0.1 copy-done.2
  6.0 0.2 copy-done.3
  6.2 0.0 copy-done.4
  6.2 3.4 %shard_map.65 = (f32[3,144,384]{2,1,0:T(8,128)S(1)}, f32[3,144,384]{2,1,0:T(8,128)S(1)}, bf16[3,384,384]{2,1,0:T(8,128)(2,1)S(1)}) custom-call(f32[3,144,128]{2,1,0:T(8,128)S(1)} %shard_map.64.columns_ref, bf16[3,144,384]{2,1,0:T(8,128)(2,1)S(1)} %collective-permute-done.halo_ref, f32[3,384]{1,0:T(4,128)S(1)} %copy-done.4, ...), custom_call_target="tpu_custom_call" | custom-call | flops 1146617856 | bytes 5000000 | tf_op jit(solution)/shard_map/pallas_call | solution.py:135
  9.6 0.0 collective-permute-done.1.halo_ref
  9.6 0.7 %shard_map.66 = (f32[3,144,384]{2,1,0:T(8,128)S(1)}, bf16[80,384]{1,0:T(8,128)(2,1)S(1)}, bf16[80,384]{1,0:T(8,128)(2,1)S(1)}, bf16[80,384]{1,0:T(8,128)(2,1)S(1)}, bf16[80,384]{1,0:T(8,128)(2,1)S(1)}) custom-call(bf16[3,144,384]{2,1,0:T(8,128)(2,1)S(1)} %collective-permute-done.1.halo_ref, f32[3,144,128]{2,1,0:T(8,128)S(1)} %shard_map.64.columns_ref, ...), custom_call_target="tpu_custom_call" | custom-call | flops 254803968 | bytes 3000000 | tf_op jit(solution)/shard_map/pallas_call | solution.py:135
  10.3 2.8 %collective-permute-start.2 = (bf16[80,384]{1,0:T(8,128)(2,1)S(1)}, bf16[80,384]{1,0:T(8,128)(2,1)S(1)}, u32[]{:S(2)}, u32[]{:S(2)}) collective-permute-start(bf16[80,384]{1,0:T(8,128)(2,1)S(1)} %get-tuple-element.30), channel_id=1, source_target_pairs={{0,12},{4,8},{8,4},{12,0},{16,28},{20,24},{24,20},{28,16},{1,13},{... | collective-permute-start | bytes 184328 | tf_op jit(solution)/shard_map/ppermute | solution.py:195
  13.0 0.4 %collective-permute-start.3 = (bf16[80,384]{1,0:T(8,128)(2,1)S(1)}, bf16[80,384]{1,0:T(8,128)(2,1)S(1)}, u32[]{:S(2)}, u32[]{:S(2)}) collective-permute-start(bf16[80,384]{1,0:T(8,128)(2,1)S(1)} %get-tuple-element.31), channel_id=1, source_target_pairs={{0,8},{4,12},{8,0},{12,4},{16,24},{20,28},{24,16},{28,20},{1,9},{5... | collective-permute-start | bytes 184328 | tf_op jit(solution)/shard_map/ppermute | solution.py:195
  13.5 0.4 %collective-permute-start.4 = (bf16[80,384]{1,0:T(8,128)(2,1)S(1)}, bf16[80,384]{1,0:T(8,128)(2,1)S(1)}, u32[]{:S(2)}, u32[]{:S(2)}) collective-permute-start(bf16[80,384]{1,0:T(8,128)(2,1)S(1)} %get-tuple-element.32), channel_id=1, source_target_pairs={{0,4},{4,0},{8,12},{12,8},{16,20},{20,16},{24,28},{28,24},{1,5},{5... | collective-permute-start | bytes 184328 | tf_op jit(solution)/shard_map/ppermute | solution.py:195
  13.8 2.0 %collective-permute-done.2 = bf16[80,384]{1,0:T(8,128)(2,1)S(1)} collective-permute-done((bf16[80,384]{1,0:T(8,128)(2,1)S(1)}, bf16[80,384]{1,0:T(8,128)(2,1)S(1)}, u32[]{:S(2)}, u32[]{:S(2)}) %collective-permute-start.2) | collective-permute-done | bytes 61472 | tf_op jit(solution)/shard_map/ppermute | solution.py:195
  15.8 1.5 %collective-permute-done.3 = bf16[80,384]{1,0:T(8,128)(2,1)S(1)} collective-permute-done((bf16[80,384]{1,0:T(8,128)(2,1)S(1)}, bf16[80,384]{1,0:T(8,128)(2,1)S(1)}, u32[]{:S(2)}, u32[]{:S(2)}) %collective-permute-start.3) | collective-permute-done | bytes 61472 | tf_op jit(solution)/shard_map/ppermute | solution.py:195
  17.3 0.3 %collective-permute-done.4 = bf16[80,384]{1,0:T(8,128)(2,1)S(1)} collective-permute-done((bf16[80,384]{1,0:T(8,128)(2,1)S(1)}, bf16[80,384]{1,0:T(8,128)(2,1)S(1)}, u32[]{:S(2)}, u32[]{:S(2)}) %collective-permute-start.4) | collective-permute-done | bytes 61472 | tf_op jit(solution)/shard_map/ppermute | solution.py:195
  17.8 0.1 fusion
  17.8 2.7 %collective-permute-start.5 = (bf16[72,384]{1,0:T(8,128)(2,1)S(1)}, bf16[72,384]{1,0:T(8,128)(2,1)S(1)}, u32[]{:S(2)}, u32[]{:S(2)}) collective-permute-start(bf16[72,384]{1,0:T(8,128)(2,1)S(1)} %get-tuple-element.56), channel_id=1, source_target_pairs={{0,16},{4,20},{8,24},{12,28},{16,0},{20,4},{24,8},{28,12},{1,17},{... | collective-permute-start | bytes 165896 | tf_op jit(solution)/shard_map/ppermute | solution.py:195
  20.6 2.3 %collective-permute-done.5 = bf16[72,384]{1,0:T(8,128)(2,1)S(1)} collective-permute-done((bf16[72,384]{1,0:T(8,128)(2,1)S(1)}, bf16[72,384]{1,0:T(8,128)(2,1)S(1)}, u32[]{:S(2)}, u32[]{:S(2)}) %collective-permute-start.5) | collective-permute-done | bytes 55328 | tf_op jit(solution)/shard_map/ppermute | solution.py:195
  22.9 0.1 add_convert_fusion
  23.0 1.6 %collective-permute-start.8 = (bf16[72,384]{1,0:T(8,128)(2,1)S(1)}, bf16[72,384]{1,0:T(8,128)(2,1)S(1)}, u32[]{:S(2)}, u32[]{:S(2)}) collective-permute-start(bf16[72,384]{1,0:T(8,128)(2,1)S(1)} %get-tuple-element.65), channel_id=1, source_target_pairs={{0,12},{4,8},{8,4},{12,0},{16,28},{20,24},{24,20},{28,16},{1,13},{... | collective-permute-start | bytes 165896 | tf_op jit(solution)/shard_map/ppermute | solution.py:195
  24.6 0.4 %collective-permute-start.7 = (bf16[72,384]{1,0:T(8,128)(2,1)S(1)}, bf16[72,384]{1,0:T(8,128)(2,1)S(1)}, u32[]{:S(2)}, u32[]{:S(2)}) collective-permute-start(bf16[72,384]{1,0:T(8,128)(2,1)S(1)} %get-tuple-element.66), channel_id=1, source_target_pairs={{0,8},{4,12},{8,0},{12,4},{16,24},{20,28},{24,16},{28,20},{1,9},{5... | collective-permute-start | bytes 165896 | tf_op jit(solution)/shard_map/ppermute | solution.py:195
  25.0 1.6 %collective-permute-start.6 = (bf16[72,384]{1,0:T(8,128)(2,1)S(1)}, bf16[72,384]{1,0:T(8,128)(2,1)S(1)}, u32[]{:S(2)}, u32[]{:S(2)}) collective-permute-start(bf16[72,384]{1,0:T(8,128)(2,1)S(1)} %get-tuple-element.68), channel_id=1, source_target_pairs={{0,4},{4,0},{8,12},{12,8},{16,20},{20,16},{24,28},{28,24},{1,5},{5... | collective-permute-start | bytes 165896 | tf_op jit(solution)/shard_map/ppermute | solution.py:195
  26.6 1.6 %collective-permute-done.8.other = bf16[72,384]{1,0:T(8,128)(2,1)S(1)} collective-permute-done((bf16[72,384]{1,0:T(8,128)(2,1)S(1)}, bf16[72,384]{1,0:T(8,128)(2,1)S(1)}, u32[]{:S(2)}, u32[]{:S(2)}) %collective-permute-start.8) | collective-permute-done | bytes 55328 | tf_op jit(solution)/shard_map/ppermute | solution.py:195
  28.1 0.9 %shard_map.67.rest_0_ = f32[3,2,144,384]{3,2,1,0:T(8,128)} custom-call(f32[3,144,384]{2,1,0:T(8,128)S(1)} %get-tuple-element.26.far_ref, f32[3,144,384]{2,1,0:T(8,128)S(1)} %get-tuple-element.29.near_ref, f32[3,384]{1,0:T(4,128)S(1)} %copy-done.4, bf16[72,384]{1,0:T(8,128)(2,1)S(1)} %get-tuple-element.67.one, bf16[72,384]{1,0:T(8,128)(2,1)S(1)} %collective-permute-done.8.other), custom_call_target="tpu_custom_call" | custom-call | flops 500000 | bytes 2000000 | tf_op jit(solution)/shard_map/pallas_call | solution.py:135
  29.1 0.0 collective-permute-done.7.other
  29.1 0.0 collective-permute-done.6.one
  29.1 0.9 %shard_map.68 = f32[3,2,144,384]{3,2,1,0:T(8,128)} custom-call(f32[3,144,384]{2,1,0:T(8,128)S(1)} %get-tuple-element.26.far_ref, f32[3,144,384]{2,1,0:T(8,128)S(1)} %get-tuple-element.29.near_ref, f32[3,384]{1,0:T(4,128)S(1)} %copy-done.4, bf16[72,384]{1,0:T(8,128)(2,1)S(1)} %collective-permute-done.6.one, ...), custom_call_target="tpu_custom_call", output_to_operand_aliasing={{}: (5, {})} | custom-call | flops 500000 | bytes 2000000 | tf_op jit(solution)/shard_map/pallas_call | solution.py:135
  (15 shorter events, 0.3 us)
Async XLA Ops:
  0.0 1.1 %copy-start = (bf16[3,2,144,384]{3,2,1,0:T(8,128)(2,1)S(1)}, bf16[3,2,144,384]{3,2,1,0:T(8,128)(2,1)}, u32[]{:S(2)}) copy-start(bf16[3,2,144,384]{3,2,1,0:T(8,128)(2,1)} %param.7) | copy-start | bytes 1990660
  0.0 4.4 %copy-start.5 = (s32[4,3,2,144]{3,2,1,0:T(2,128)S(1)}, s32[4,3,2,144]{3,2,1,0:T(2,128)}, u32[]{:S(2)}) copy-start(s32[4,3,2,144]{3,2,1,0:T(2,128)} %mask_ref.1) | copy-start | bytes 41476
  1.1 8.5 %collective-permute-start.1 = (bf16[3,144,384]{2,1,0:T(8,128)(2,1)S(1)}, bf16[3,144,384]{2,1,0:T(8,128)(2,1)S(1)}, u32[]{:S(2)}, u32[]{:S(2)}) collective-permute-start(bf16[3,144,384]{2,1,0:T(8,128)(2,1)S(1)} %dynamic-slice_bitcast_fusion.1.after.near_row), channel_id=1, source_target_pairs={{0,4},{1,2},{2,1},{3,7},{4,0},{5,6},{6,5},{7,3},{8,12},{9,10},{10,... | collective-permute-start | bytes 995336 | tf_op jit(solution)/shard_map/ppermute | solution.py:166
  4.2 1.8 %copy-start.1 = (bf16[3,2,384,384]{3,2,1,0:T(8,128)(2,1)S(1)}, bf16[3,2,384,384]{3,2,1,0:T(8,128)(2,1)}, u32[]{:S(2)}) copy-start(bf16[3,2,384,384]{3,2,1,0:T(8,128)(2,1)} %inverse.1) | copy-start | bytes 5308420
  4.2 1.8 %copy-start.2 = (bf16[4,384,384]{2,1,0:T(8,128)(2,1)S(1)}, bf16[4,384,384]{2,1,0:T(8,128)(2,1)}, u32[]{:S(2)}) copy-start(bf16[4,384,384]{2,1,0:T(8,128)(2,1)} %lift.1) | copy-start | bytes 3538948
  4.2 2.0 %copy-start.3 = (bf16[3,2,144,384]{3,2,1,0:T(8,128)(2,1)S(1)}, bf16[3,2,144,384]{3,2,1,0:T(8,128)(2,1)}, u32[]{:S(2)}) copy-start(bf16[3,2,144,384]{3,2,1,0:T(8,128)(2,1)} %forcing.1) | copy-start | bytes 1990660
  4.2 1.9 %copy-start.4 = (f32[3,384]{1,0:T(4,128)S(1)}, f32[3,384]{1,0:T(4,128)}, u32[]{:S(2)}) copy-start(f32[3,384]{1,0:T(4,128)} %keep_ref.7) | copy-start | bytes 13828
  4.2 1.7 %collective-permute-start = (bf16[3,144,384]{2,1,0:T(8,128)(2,1)S(1)}, bf16[3,144,384]{2,1,0:T(8,128)(2,1)S(1)}, u32[]{:S(2)}, u32[]{:S(2)}) collective-permute-start(bf16[3,144,384]{2,1,0:T(8,128)(2,1)S(1)} %dynamic-slice_bitcast_fusion.far_row), channel_id=1, source_target_pairs={{0,1},{1,0},{2,3},{3,2},{4,5},{5,4},{6,7},{7,6},{8,9},{9,8},{10,11... | collective-permute-start | bytes 995336 | tf_op jit(solution)/shard_map/ppermute | solution.py:167
  10.3 5.5 %collective-permute-start.2 = (bf16[80,384]{1,0:T(8,128)(2,1)S(1)}, bf16[80,384]{1,0:T(8,128)(2,1)S(1)}, u32[]{:S(2)}, u32[]{:S(2)}) collective-permute-start(bf16[80,384]{1,0:T(8,128)(2,1)S(1)} %get-tuple-element.30), channel_id=1, source_target_pairs={{0,12},{4,8},{8,4},{12,0},{16,28},{20,24},{24,20},{28,16},{1,13},{... | collective-permute-start | bytes 184328 | tf_op jit(solution)/shard_map/ppermute | solution.py:195
  13.0 4.2 %collective-permute-start.3 = (bf16[80,384]{1,0:T(8,128)(2,1)S(1)}, bf16[80,384]{1,0:T(8,128)(2,1)S(1)}, u32[]{:S(2)}, u32[]{:S(2)}) collective-permute-start(bf16[80,384]{1,0:T(8,128)(2,1)S(1)} %get-tuple-element.31), channel_id=1, source_target_pairs={{0,8},{4,12},{8,0},{12,4},{16,24},{20,28},{24,16},{28,20},{1,9},{5... | collective-permute-start | bytes 184328 | tf_op jit(solution)/shard_map/ppermute | solution.py:195
  13.5 4.2 %collective-permute-start.4 = (bf16[80,384]{1,0:T(8,128)(2,1)S(1)}, bf16[80,384]{1,0:T(8,128)(2,1)S(1)}, u32[]{:S(2)}, u32[]{:S(2)}) collective-permute-start(bf16[80,384]{1,0:T(8,128)(2,1)S(1)} %get-tuple-element.32), channel_id=1, source_target_pairs={{0,4},{4,0},{8,12},{12,8},{16,20},{20,16},{24,28},{28,24},{1,5},{5... | collective-permute-start | bytes 184328 | tf_op jit(solution)/shard_map/ppermute | solution.py:195
  17.8 5.1 %collective-permute-start.5 = (bf16[72,384]{1,0:T(8,128)(2,1)S(1)}, bf16[72,384]{1,0:T(8,128)(2,1)S(1)}, u32[]{:S(2)}, u32[]{:S(2)}) collective-permute-start(bf16[72,384]{1,0:T(8,128)(2,1)S(1)} %get-tuple-element.56), channel_id=1, source_target_pairs={{0,16},{4,20},{8,24},{12,28},{16,0},{20,4},{24,8},{28,12},{1,17},{... | collective-permute-start | bytes 165896 | tf_op jit(solution)/shard_map/ppermute | solution.py:195
  23.0 5.1 %collective-permute-start.8 = (bf16[72,384]{1,0:T(8,128)(2,1)S(1)}, bf16[72,384]{1,0:T(8,128)(2,1)S(1)}, u32[]{:S(2)}, u32[]{:S(2)}) collective-permute-start(bf16[72,384]{1,0:T(8,128)(2,1)S(1)} %get-tuple-element.65), channel_id=1, source_target_pairs={{0,12},{4,8},{8,4},{12,0},{16,28},{20,24},{24,20},{28,16},{1,13},{... | collective-permute-start | bytes 165896 | tf_op jit(solution)/shard_map/ppermute | solution.py:195
  24.6 4.5 %collective-permute-start.7 = (bf16[72,384]{1,0:T(8,128)(2,1)S(1)}, bf16[72,384]{1,0:T(8,128)(2,1)S(1)}, u32[]{:S(2)}, u32[]{:S(2)}) collective-permute-start(bf16[72,384]{1,0:T(8,128)(2,1)S(1)} %get-tuple-element.66), channel_id=1, source_target_pairs={{0,8},{4,12},{8,0},{12,4},{16,24},{20,28},{24,16},{28,20},{1,9},{5... | collective-permute-start | bytes 165896 | tf_op jit(solution)/shard_map/ppermute | solution.py:195
  25.0 4.2 %collective-permute-start.6 = (bf16[72,384]{1,0:T(8,128)(2,1)S(1)}, bf16[72,384]{1,0:T(8,128)(2,1)S(1)}, u32[]{:S(2)}, u32[]{:S(2)}) collective-permute-start(bf16[72,384]{1,0:T(8,128)(2,1)S(1)} %get-tuple-element.68), channel_id=1, source_target_pairs={{0,4},{4,0},{8,12},{12,8},{16,20},{20,16},{24,28},{28,24},{1,5},{5... | collective-permute-start | bytes 165896 | tf_op jit(solution)/shard_map/ppermute | solution.py:195

commit v9 on v8

--- a/solution.py
+++ b/solution.py
@@ -84,10 +84,11 @@
     odd = cross & 1
     inside = (cross != 0) & (cross != lax.axis_size("cross") - 1)
     total = None
+    scale = jnp.where(inside, 1.0, 0.0).astype(BF16)
     for l in range(layers):
         edge = jnp.where(odd == 1, columns_ref[l, :, 3:4], columns_ref[l, :, 0:1])
-        halo = jnp.where(inside, halo_ref[l].astype(F32), 0.0)
-        solved = dot(masked_jump(edge, halo, near_row[l].astype(F32)), matrix_ref[l])
+        edge = jnp.broadcast_to(edge, (width, dofs)).astype(BF16)
+        solved = dot(edge * (halo_ref[l] * scale - near_row[l]), matrix_ref[l])
         total = solved if l == 0 else keep_ref[l : l + 1, :] * total + solved
         near_ref[l] = start_ref[l] + total
     total = total + start_ref[layers - 1]

time: 30.2 us -> 30.1 us (level)
  no operation moved by 1% of the time
where the time goes in v9:
time: 30.1 us; the launch traced here: 30 us
  starting transfers between devices  12.9 us (43%)
  waiting for transfers between devices  9.13 us (30%)
  Pallas kernels  5.97 us (20%)
  local copies, waits for them, and re-layouts  1.41 us (5%)
  other arithmetic  0.39 us (1%)
    ppermute x7, starting transfers between devices, swap(): lax.ppermute(part, 'stream', [(i, i ^ distance) for i in range(streams)])  9.76 us
    ppermute x7, waiting for transfers between devices, swap(): lax.ppermute(part, 'stream', [(i, i ^ distance) for i in range(streams)])  7.72 us
    pallas_call x5, Pallas kernels, call(): pl.pallas_call(kernel, out_shape=outs, in_specs=in_specs, out_specs=out_s...  5.97 us
    ppermute x1, starting transfers between devices, body(): chip_halo = lax.ppermute(near_row, ('stream', 'cross'), links)  3.03 us
    ppermute x1, waiting for transfers between devices, body(): lax.ppermute(far_row, 'cross', [(i, i ^ 1) for i in range(crosses)])  1.41 us
    unnamed x12, local copies, waits for them, and re-layouts  1.34 us
  transfers between devices with their start and end apart: 9, of which 6 were waited for; matrix products, arithmetic and copies ran while one was open for 1% of the time, Pallas kernels for 15%

profile of v9, /device:TPU:0, one launch (start us, length us, event | category | flops | bytes accessed | tf_op | source)
XLA Modules:
  0.0 30.0 jit_solution(16617365042012361914)
XLA Ops:
  0.0 0.0 copy-start
  0.0 0.0 copy-start.5
  0.0 1.1 %copy-done = bf16[3,2,144,384]{3,2,1,0:T(8,128)(2,1)S(1)} copy-done((bf16[3,2,144,384]{3,2,1,0:T(8,128)(2,1)S(1)}, bf16[3,2,144,384]{3,2,1,0:T(8,128)(2,1)}, u32[]{:S(2)}) %copy-start) | copy-done | bytes 663576
  1.1 3.0 %collective-permute-start.1 = (bf16[3,144,384]{2,1,0:T(8,128)(2,1)S(1)}, bf16[3,144,384]{2,1,0:T(8,128)(2,1)S(1)}, u32[]{:S(2)}, u32[]{:S(2)}) collective-permute-start(bf16[3,144,384]{2,1,0:T(8,128)(2,1)S(1)} %dynamic-slice_bitcast_fusion.1.after.near_row), channel_id=1, source_target_pairs={{0,4},{1,2},{2,1},{3,7},{4,0},{5,6},{6,5},{7,3},{8,12},{9,10},{10,... | collective-permute-start | bytes 995336 | tf_op jit(solution)/shard_map/ppermute | solution.py:167
  4.2 0.0 copy-start.1
  4.2 0.0 copy-start.2
  4.2 0.0 copy-start.3
  4.2 0.0 copy-start.4
  4.2 0.2 collective-permute-start
  4.4 0.0 copy-done.5
  4.4 0.1 shard_map.64.columns_ref
  4.5 1.4 %collective-permute-done.halo_ref = bf16[3,144,384]{2,1,0:T(8,128)(2,1)S(1)} collective-permute-done((bf16[3,144,384]{2,1,0:T(8,128)(2,1)S(1)}, bf16[3,144,384]{2,1,0:T(8,128)(2,1)S(1)}, u32[]{:S(2)}, u32[]{:S(2)}) %collective-permute-start) | collective-permute-done | bytes 331808 | tf_op jit(solution)/shard_map/ppermute | solution.py:168
  5.9 0.0 copy-done.1
  6.0 0.1 copy-done.2
  6.0 0.2 copy-done.3
  6.2 0.0 copy-done.4
  6.2 3.4 %shard_map.65 = (f32[3,144,384]{2,1,0:T(8,128)S(1)}, f32[3,144,384]{2,1,0:T(8,128)S(1)}, bf16[3,384,384]{2,1,0:T(8,128)(2,1)S(1)}) custom-call(f32[3,144,128]{2,1,0:T(8,128)S(1)} %shard_map.64.columns_ref, bf16[3,144,384]{2,1,0:T(8,128)(2,1)S(1)} %collective-permute-done.halo_ref, f32[3,384]{1,0:T(4,128)S(1)} %copy-done.4, ...), custom_call_target="tpu_custom_call" | custom-call | flops 1146617856 | bytes 5000000 | tf_op jit(solution)/shard_map/pallas_call | solution.py:136
  9.6 0.0 collective-permute-done.1.halo_ref
  9.6 0.6 %shard_map.66 = (f32[3,144,384]{2,1,0:T(8,128)S(1)}, bf16[80,384]{1,0:T(8,128)(2,1)S(1)}, bf16[80,384]{1,0:T(8,128)(2,1)S(1)}, bf16[80,384]{1,0:T(8,128)(2,1)S(1)}, bf16[80,384]{1,0:T(8,128)(2,1)S(1)}) custom-call(bf16[3,144,384]{2,1,0:T(8,128)(2,1)S(1)} %collective-permute-done.1.halo_ref, f32[3,144,128]{2,1,0:T(8,128)S(1)} %shard_map.64.columns_ref, ...), custom_call_target="tpu_custom_call" | custom-call | flops 254803968 | bytes 3000000 | tf_op jit(solution)/shard_map/pallas_call | solution.py:136
  10.2 2.8 %collective-permute-start.2 = (bf16[80,384]{1,0:T(8,128)(2,1)S(1)}, bf16[80,384]{1,0:T(8,128)(2,1)S(1)}, u32[]{:S(2)}, u32[]{:S(2)}) collective-permute-start(bf16[80,384]{1,0:T(8,128)(2,1)S(1)} %get-tuple-element.30), channel_id=1, source_target_pairs={{0,12},{4,8},{8,4},{12,0},{16,28},{20,24},{24,20},{28,16},{1,13},{... | collective-permute-start | bytes 184328 | tf_op jit(solution)/shard_map/ppermute | solution.py:196
  13.0 0.4 %collective-permute-start.3 = (bf16[80,384]{1,0:T(8,128)(2,1)S(1)}, bf16[80,384]{1,0:T(8,128)(2,1)S(1)}, u32[]{:S(2)}, u32[]{:S(2)}) collective-permute-start(bf16[80,384]{1,0:T(8,128)(2,1)S(1)} %get-tuple-element.31), channel_id=1, source_target_pairs={{0,8},{4,12},{8,0},{12,4},{16,24},{20,28},{24,16},{28,20},{1,9},{5... | collective-permute-start | bytes 184328 | tf_op jit(solution)/shard_map/ppermute | solution.py:196
  13.4 0.4 %collective-permute-start.4 = (bf16[80,384]{1,0:T(8,128)(2,1)S(1)}, bf16[80,384]{1,0:T(8,128)(2,1)S(1)}, u32[]{:S(2)}, u32[]{:S(2)}) collective-permute-start(bf16[80,384]{1,0:T(8,128)(2,1)S(1)} %get-tuple-element.32), channel_id=1, source_target_pairs={{0,4},{4,0},{8,12},{12,8},{16,20},{20,16},{24,28},{28,24},{1,5},{5... | collective-permute-start | bytes 184328 | tf_op jit(solution)/shard_map/ppermute | solution.py:196
  13.8 2.0 %collective-permute-done.2 = bf16[80,384]{1,0:T(8,128)(2,1)S(1)} collective-permute-done((bf16[80,384]{1,0:T(8,128)(2,1)S(1)}, bf16[80,384]{1,0:T(8,128)(2,1)S(1)}, u32[]{:S(2)}, u32[]{:S(2)}) %collective-permute-start.2) | collective-permute-done | bytes 61472 | tf_op jit(solution)/shard_map/ppermute | solution.py:196
  15.7 1.5 %collective-permute-done.3 = bf16[80,384]{1,0:T(8,128)(2,1)S(1)} collective-permute-done((bf16[80,384]{1,0:T(8,128)(2,1)S(1)}, bf16[80,384]{1,0:T(8,128)(2,1)S(1)}, u32[]{:S(2)}, u32[]{:S(2)}) %collective-permute-start.3) | collective-permute-done | bytes 61472 | tf_op jit(solution)/shard_map/ppermute | solution.py:196
  17.3 0.3 %collective-permute-done.4 = bf16[80,384]{1,0:T(8,128)(2,1)S(1)} collective-permute-done((bf16[80,384]{1,0:T(8,128)(2,1)S(1)}, bf16[80,384]{1,0:T(8,128)(2,1)S(1)}, u32[]{:S(2)}, u32[]{:S(2)}) %collective-permute-start.4) | collective-permute-done | bytes 61472 | tf_op jit(solution)/shard_map/ppermute | solution.py:196
  17.7 0.1 fusion
  17.8 2.7 %collective-permute-start.5 = (bf16[72,384]{1,0:T(8,128)(2,1)S(1)}, bf16[72,384]{1,0:T(8,128)(2,1)S(1)}, u32[]{:S(2)}, u32[]{:S(2)}) collective-permute-start(bf16[72,384]{1,0:T(8,128)(2,1)S(1)} %get-tuple-element.56), channel_id=1, source_target_pairs={{0,16},{4,20},{8,24},{12,28},{16,0},{20,4},{24,8},{28,12},{1,17},{... | collective-permute-start | bytes 165896 | tf_op jit(solution)/shard_map/ppermute | solution.py:196
  20.6 2.3 %collective-permute-done.5 = bf16[72,384]{1,0:T(8,128)(2,1)S(1)} collective-permute-done((bf16[72,384]{1,0:T(8,128)(2,1)S(1)}, bf16[72,384]{1,0:T(8,128)(2,1)S(1)}, u32[]{:S(2)}, u32[]{:S(2)}) %collective-permute-start.5) | collective-permute-done | bytes 55328 | tf_op jit(solution)/shard_map/ppermute | solution.py:196
  22.9 0.1 add_convert_fusion
  23.0 1.6 %collective-permute-start.8 = (bf16[72,384]{1,0:T(8,128)(2,1)S(1)}, bf16[72,384]{1,0:T(8,128)(2,1)S(1)}, u32[]{:S(2)}, u32[]{:S(2)}) collective-permute-start(bf16[72,384]{1,0:T(8,128)(2,1)S(1)} %get-tuple-element.65), channel_id=1, source_target_pairs={{0,12},{4,8},{8,4},{12,0},{16,28},{20,24},{24,20},{28,16},{1,13},{... | collective-permute-start | bytes 165896 | tf_op jit(solution)/shard_map/ppermute | solution.py:196
  24.5 0.4 %collective-permute-start.7 = (bf16[72,384]{1,0:T(8,128)(2,1)S(1)}, bf16[72,384]{1,0:T(8,128)(2,1)S(1)}, u32[]{:S(2)}, u32[]{:S(2)}) collective-permute-start(bf16[72,384]{1,0:T(8,128)(2,1)S(1)} %get-tuple-element.66), channel_id=1, source_target_pairs={{0,8},{4,12},{8,0},{12,4},{16,24},{20,28},{24,16},{28,20},{1,9},{5... | collective-permute-start | bytes 165896 | tf_op jit(solution)/shard_map/ppermute | solution.py:196
  24.9 1.6 %collective-permute-start.6 = (bf16[72,384]{1,0:T(8,128)(2,1)S(1)}, bf16[72,384]{1,0:T(8,128)(2,1)S(1)}, u32[]{:S(2)}, u32[]{:S(2)}) collective-permute-start(bf16[72,384]{1,0:T(8,128)(2,1)S(1)} %get-tuple-element.68), channel_id=1, source_target_pairs={{0,4},{4,0},{8,12},{12,8},{16,20},{20,16},{24,28},{28,24},{1,5},{5... | collective-permute-start | bytes 165896 | tf_op jit(solution)/shard_map/ppermute | solution.py:196
  26.5 1.6 %collective-permute-done.8.other = bf16[72,384]{1,0:T(8,128)(2,1)S(1)} collective-permute-done((bf16[72,384]{1,0:T(8,128)(2,1)S(1)}, bf16[72,384]{1,0:T(8,128)(2,1)S(1)}, u32[]{:S(2)}, u32[]{:S(2)}) %collective-permute-start.8) | collective-permute-done | bytes 55328 | tf_op jit(solution)/shard_map/ppermute | solution.py:196
  28.1 0.9 %shard_map.67.rest_0_ = f32[3,2,144,384]{3,2,1,0:T(8,128)} custom-call(f32[3,144,384]{2,1,0:T(8,128)S(1)} %get-tuple-element.26.far_ref, f32[3,144,384]{2,1,0:T(8,128)S(1)} %get-tuple-element.29.near_ref, f32[3,384]{1,0:T(4,128)S(1)} %copy-done.4, bf16[72,384]{1,0:T(8,128)(2,1)S(1)} %get-tuple-element.67.one, bf16[72,384]{1,0:T(8,128)(2,1)S(1)} %collective-permute-done.8.other), custom_call_target="tpu_custom_call" | custom-call | flops 500000 | bytes 2000000 | tf_op jit(solution)/shard_map/pallas_call | solution.py:136
  29.0 0.0 collective-permute-done.7.other
  29.0 0.0 collective-permute-done.6.one
  29.1 0.9 %shard_map.68 = f32[3,2,144,384]{3,2,1,0:T(8,128)} custom-call(f32[3,144,384]{2,1,0:T(8,128)S(1)} %get-tuple-element.26.far_ref, f32[3,144,384]{2,1,0:T(8,128)S(1)} %get-tuple-element.29.near_ref, f32[3,384]{1,0:T(4,128)S(1)} %copy-done.4, bf16[72,384]{1,0:T(8,128)(2,1)S(1)} %collective-permute-done.6.one, ...), custom_call_target="tpu_custom_call", output_to_operand_aliasing={{}: (5, {})} | custom-call | flops 500000 | bytes 2000000 | tf_op jit(solution)/shard_map/pallas_call | solution.py:136
  (15 shorter events, 0.3 us)
Async XLA Ops:
  0.0 1.1 %copy-start = (bf16[3,2,144,384]{3,2,1,0:T(8,128)(2,1)S(1)}, bf16[3,2,144,384]{3,2,1,0:T(8,128)(2,1)}, u32[]{:S(2)}) copy-start(bf16[3,2,144,384]{3,2,1,0:T(8,128)(2,1)} %param.7) | copy-start | bytes 1990660
  0.0 4.4 %copy-start.5 = (s32[4,3,2,144]{3,2,1,0:T(2,128)S(1)}, s32[4,3,2,144]{3,2,1,0:T(2,128)}, u32[]{:S(2)}) copy-start(s32[4,3,2,144]{3,2,1,0:T(2,128)} %mask_ref.1) | copy-start | bytes 41476
  1.1 8.5 %collective-permute-start.1 = (bf16[3,144,384]{2,1,0:T(8,128)(2,1)S(1)}, bf16[3,144,384]{2,1,0:T(8,128)(2,1)S(1)}, u32[]{:S(2)}, u32[]{:S(2)}) collective-permute-start(bf16[3,144,384]{2,1,0:T(8,128)(2,1)S(1)} %dynamic-slice_bitcast_fusion.1.after.near_row), channel_id=1, source_target_pairs={{0,4},{1,2},{2,1},{3,7},{4,0},{5,6},{6,5},{7,3},{8,12},{9,10},{10,... | collective-permute-start | bytes 995336 | tf_op jit(solution)/shard_map/ppermute | solution.py:167
  4.2 1.8 %copy-start.1 = (bf16[3,2,384,384]{3,2,1,0:T(8,128)(2,1)S(1)}, bf16[3,2,384,384]{3,2,1,0:T(8,128)(2,1)}, u32[]{:S(2)}) copy-start(bf16[3,2,384,384]{3,2,1,0:T(8,128)(2,1)} %inverse.1) | copy-start | bytes 5308420
  4.2 1.8 %copy-start.2 = (bf16[4,384,384]{2,1,0:T(8,128)(2,1)S(1)}, bf16[4,384,384]{2,1,0:T(8,128)(2,1)}, u32[]{:S(2)}) copy-start(bf16[4,384,384]{2,1,0:T(8,128)(2,1)} %lift.1) | copy-start | bytes 3538948
  4.2 2.0 %copy-start.3 = (bf16[3,2,144,384]{3,2,1,0:T(8,128)(2,1)S(1)}, bf16[3,2,144,384]{3,2,1,0:T(8,128)(2,1)}, u32[]{:S(2)}) copy-start(bf16[3,2,144,384]{3,2,1,0:T(8,128)(2,1)} %forcing.1) | copy-start | bytes 1990660
  4.2 1.9 %copy-start.4 = (f32[3,384]{1,0:T(4,128)S(1)}, f32[3,384]{1,0:T(4,128)}, u32[]{:S(2)}) copy-start(f32[3,384]{1,0:T(4,128)} %keep_ref.7) | copy-start | bytes 13828
  4.2 1.7 %collective-permute-start = (bf16[3,144,384]{2,1,0:T(8,128)(2,1)S(1)}, bf16[3,144,384]{2,1,0:T(8,128)(2,1)S(1)}, u32[]{:S(2)}, u32[]{:S(2)}) collective-permute-start(bf16[3,144,384]{2,1,0:T(8,128)(2,1)S(1)} %dynamic-slice_bitcast_fusion.far_row), channel_id=1, source_target_pairs={{0,1},{1,0},{2,3},{3,2},{4,5},{5,4},{6,7},{7,6},{8,9},{9,8},{10,11... | collective-permute-start | bytes 995336 | tf_op jit(solution)/shard_map/ppermute | solution.py:168
  10.2 5.5 %collective-permute-start.2 = (bf16[80,384]{1,0:T(8,128)(2,1)S(1)}, bf16[80,384]{1,0:T(8,128)(2,1)S(1)}, u32[]{:S(2)}, u32[]{:S(2)}) collective-permute-start(bf16[80,384]{1,0:T(8,128)(2,1)S(1)} %get-tuple-element.30), channel_id=1, source_target_pairs={{0,12},{4,8},{8,4},{12,0},{16,28},{20,24},{24,20},{28,16},{1,13},{... | collective-permute-start | bytes 184328 | tf_op jit(solution)/shard_map/ppermute | solution.py:196
  13.0 4.2 %collective-permute-start.3 = (bf16[80,384]{1,0:T(8,128)(2,1)S(1)}, bf16[80,384]{1,0:T(8,128)(2,1)S(1)}, u32[]{:S(2)}, u32[]{:S(2)}) collective-permute-start(bf16[80,384]{1,0:T(8,128)(2,1)S(1)} %get-tuple-element.31), channel_id=1, source_target_pairs={{0,8},{4,12},{8,0},{12,4},{16,24},{20,28},{24,16},{28,20},{1,9},{5... | collective-permute-start | bytes 184328 | tf_op jit(solution)/shard_map/ppermute | solution.py:196
  13.4 4.2 %collective-permute-start.4 = (bf16[80,384]{1,0:T(8,128)(2,1)S(1)}, bf16[80,384]{1,0:T(8,128)(2,1)S(1)}, u32[]{:S(2)}, u32[]{:S(2)}) collective-permute-start(bf16[80,384]{1,0:T(8,128)(2,1)S(1)} %get-tuple-element.32), channel_id=1, source_target_pairs={{0,4},{4,0},{8,12},{12,8},{16,20},{20,16},{24,28},{28,24},{1,5},{5... | collective-permute-start | bytes 184328 | tf_op jit(solution)/shard_map/ppermute | solution.py:196
  17.8 5.1 %collective-permute-start.5 = (bf16[72,384]{1,0:T(8,128)(2,1)S(1)}, bf16[72,384]{1,0:T(8,128)(2,1)S(1)}, u32[]{:S(2)}, u32[]{:S(2)}) collective-permute-start(bf16[72,384]{1,0:T(8,128)(2,1)S(1)} %get-tuple-element.56), channel_id=1, source_target_pairs={{0,16},{4,20},{8,24},{12,28},{16,0},{20,4},{24,8},{28,12},{1,17},{... | collective-permute-start | bytes 165896 | tf_op jit(solution)/shard_map/ppermute | solution.py:196
  23.0 5.1 %collective-permute-start.8 = (bf16[72,384]{1,0:T(8,128)(2,1)S(1)}, bf16[72,384]{1,0:T(8,128)(2,1)S(1)}, u32[]{:S(2)}, u32[]{:S(2)}) collective-permute-start(bf16[72,384]{1,0:T(8,128)(2,1)S(1)} %get-tuple-element.65), channel_id=1, source_target_pairs={{0,12},{4,8},{8,4},{12,0},{16,28},{20,24},{24,20},{28,16},{1,13},{... | collective-permute-start | bytes 165896 | tf_op jit(solution)/shard_map/ppermute | solution.py:196
  24.5 4.5 %collective-permute-start.7 = (bf16[72,384]{1,0:T(8,128)(2,1)S(1)}, bf16[72,384]{1,0:T(8,128)(2,1)S(1)}, u32[]{:S(2)}, u32[]{:S(2)}) collective-permute-start(bf16[72,384]{1,0:T(8,128)(2,1)S(1)} %get-tuple-element.66), channel_id=1, source_target_pairs={{0,8},{4,12},{8,0},{12,4},{16,24},{20,28},{24,16},{28,20},{1,9},{5... | collective-permute-start | bytes 165896 | tf_op jit(solution)/shard_map/ppermute | solution.py:196
  24.9 4.2 %collective-permute-start.6 = (bf16[72,384]{1,0:T(8,128)(2,1)S(1)}, bf16[72,384]{1,0:T(8,128)(2,1)S(1)}, u32[]{:S(2)}, u32[]{:S(2)}) collective-permute-start(bf16[72,384]{1,0:T(8,128)(2,1)S(1)} %get-tuple-element.68), channel_id=1, source_target_pairs={{0,4},{4,0},{8,12},{12,8},{16,20},{20,16},{24,28},{28,24},{1,5},{5... | collective-permute-start | bytes 165896 | tf_op jit(solution)/shard_map/ppermute | solution.py:196
